TPU v7x, 128 devices: a whole 4x4x4 slice. The times are simulated.
128 devices in a mesh: dp: 8 (over z, core), ctx: 16 (over y, x).
Axes of the slice: x: 4, y: 4, z: 4, core: 2. Of those that a mesh axis runs over, the one named last changes fastest.
Arguments:
- tokens: bfloat16 [8, 2048, 2240], P('dp', 'ctx'), may hold values from -6 to 6
- queries: bfloat16 [8, 2048, 2240], P('dp', 'ctx'), may hold values from -6 to 6
- cotangent: bfloat16 [8, 2048, 2240], P('dp', 'ctx'), may hold values from -6 to 6
- key_weight: bfloat16 [2240, 2240], P('ctx'), may hold values from -0.125 to 0.125
- value_weight: bfloat16 [2240, 2240], P('ctx'), may hold values from -0.125 to 0.125
- clip_len: int32 [8], P('dp'), may hold values from 512 to 2048, as said below
Outputs:
- grad_queries: bfloat16 [8, 2048, 2240], P('dp', 'ctx')
- grad_key_weight: float32 [2240, 2240], P('ctx')
Inputs may be any that keep to these rules, and one draw needn't show every extreme that they name: `clip_len`: some clip has exactly 2048 live tokens.
All inputs are finite; a program needn't handle non-finite values.
Results may differ from a plain program's by a relative error of at most 0.02.
Values may be sent and summed in bfloat16 or wider, within the bound.
No kernel may reach another device: no remote copies, remote signals or barrier semaphores. Data moves between devices by JAX's collectives and lax.ppermute only.
A program may use at most 128 MiB of HBM per device.

v0:
```python
import jax
import jax.numpy as jnp
from jax import lax
from jax.sharding import PartitionSpec as P

HEADS = 20
HEAD_DIM = 112


def per_device(tokens, queries, cotangent, key_weight, value_weight, clip_len):
    heads = HEADS
    head_dim = HEAD_DIM
    width = heads * head_dim
    rows = tokens.shape[1]
    member = lax.axis_index("ctx")
    length = clip_len[0]
    length_float = length.astype(jnp.float32)
    feats = tokens[0]
    quers = queries[0]
    backs = cotangent[0]
    key_full, value_full = (
        lax.all_gather(key_weight, "ctx", axis=0, tiled=True),
        lax.all_gather(value_weight, "ctx", axis=0, tiled=True),
    )
    valid = jnp.clip(length - member * rows, 0, rows)
    block = min(128, rows)
    nblocks = (valid + block - 1) // block

    def row_mask(start):
        return (start + jnp.arange(block, dtype=jnp.int32) < valid).astype(jnp.float32)[
            :, None, None
        ]

    def forward_step(step, carry):
        keys_all, values_all, summary, normer = carry
        start = step * block
        keys = jax.nn.relu(jnp.dot(feats, key_full, preferred_element_type=jnp.float32)).astype(
            jnp.bfloat16
        )
        values = jnp.dot(feats, value_full, preferred_element_type=jnp.float32).astype(jnp.bfloat16)
        live = row_mask(start)
        kf = keys.astype(jnp.float32).reshape(block, heads, head_dim) * live
        vf = values.astype(jnp.float32).reshape(block, heads, head_dim)
        summary = summary + jnp.einsum("the,thf->hef", kf, vf)
        normer = normer + jnp.sum(kf, axis=0)
        keys_all = keys
        values_all = values
        return (keys_all, values_all, summary, normer)

    start_carry = (
        jnp.zeros((rows, width), jnp.bfloat16),
        jnp.zeros((rows, width), jnp.bfloat16),
        jnp.zeros((heads, head_dim, head_dim), jnp.float32),
        jnp.zeros((heads, head_dim), jnp.float32),
    )
    keys_all, values_all, summary, normer = lax.fori_loop(0, nblocks, forward_step, start_carry)
    summary, normer = lax.psum((summary, normer), "ctx")

    def query_step(step, carry):
        grad_all, dsummary, dnormer = carry
        start = step * block
        phi = jax.nn.relu(quers.astype(jnp.float32)).reshape(block, heads, head_dim)
        back = backs.astype(jnp.float32).reshape(block, heads, head_dim) * row_mask(start)
        numer = jnp.einsum("the,hef->thf", phi, summary)
        denom = jnp.einsum("the,he->th", phi, normer) + length_float
        dnum = back / denom[:, :, None]
        dden = -jnp.sum(back * numer, axis=-1) / (denom * denom)
        dphi = jnp.einsum("thf,hef->the", dnum, summary) + dden[:, :, None] * normer[None]
        grad_q = (dphi * (phi > 0)).reshape(block, width).astype(jnp.bfloat16)
        dsummary = dsummary + jnp.einsum("the,thf->hef", phi, dnum)
        dnormer = dnormer + jnp.sum(phi * dden[:, :, None], axis=0)
        grad_all = grad_q
        return (grad_all, dsummary, dnormer)

    query_carry = (
        jnp.zeros((rows, width), jnp.bfloat16),
        jnp.zeros((heads, head_dim, head_dim), jnp.float32),
        jnp.zeros((heads, head_dim), jnp.float32),
    )
    grad_all, dsummary, dnormer = lax.fori_loop(0, nblocks, query_step, query_carry)
    dsummary, dnormer = lax.psum((dsummary, dnormer), "ctx")

    def key_step(step, dkeys_all):
        start = step * block
        kf = keys_all.astype(jnp.float32).reshape(block, heads, head_dim)
        vf = values_all.astype(jnp.float32).reshape(block, heads, head_dim)
        dkeys = (
            (jnp.einsum("thf,hef->the", vf, dsummary) + dnormer[None]) * row_mask(start) * (kf > 0)
        )
        return dkeys.reshape(block, width).astype(jnp.bfloat16)

    dkeys_all = lax.fori_loop(0, nblocks, key_step, jnp.zeros((rows, width), jnp.bfloat16))
    grad_rows = lax.psum_scatter(
        lax.dot_general(
            feats, dkeys_all, (((0,), (0,)), ((), ())), preferred_element_type=jnp.float32
        ).astype(jnp.bfloat16),
        "ctx",
        scatter_dimension=0,
        tiled=True,
    ).astype(jnp.float32)
    grad_rows = lax.psum(grad_rows, "dp")
    return (grad_all[None], grad_rows)


def solution(mesh):
    in_specs = (
        P("dp", "ctx", None),
        P("dp", "ctx", None),
        P("dp", "ctx", None),
        P("ctx", None),
        P("ctx", None),
        P("dp"),
    )
    out_specs = (P("dp", "ctx", None), P("ctx", None))
    return jax.shard_map(
        per_device, mesh=mesh, in_specs=in_specs, out_specs=out_specs, check_vma=False
    )
```

profile of v0, /device:TPU:7, one launch (start us, length us, event | category | flops | bytes accessed | tf_op | source)
XLA Modules:
  0.0 617.6 jit_solution(13979003126979362039)
XLA Ops:
  7.2 0.0 copy-start
  7.2 0.0 all-gather.7.cloned.1.call-start
  7.2 0.7 all-gather.7.cloned.1.call-update
  7.9 0.0 all-gather.5.cloned.1.call-start
  8.0 0.7 all-gather.5.cloned.1.call-update
  8.7 0.0 all-reduce.10.cloned.1.call-start
  9.4 83.9 %all-gather.7.cloned.1.call-done = bf16[16,140,2240]{2,1,0:T(8,128)(2,1)} async-done(((bf16[1,140,2240]{2,1,0:T(8,128)(2,1)}), bf16[16,140,2240]{2,1,0:T(8,128)(2,1)}) %all-gather.7.cloned.1.call-update) | async-done | bytes 10035216 | tf_op jit(solution)/shard_map/all_gather | solution.py:23
  93.3 11.9 %reshape.84 = bf16[2240,2240]{1,0:T(8,128)(2,1)} reshape(bf16[16,140,2240]{2,1,0:T(8,128)(2,1)} %all-gather.7.cloned.1.call-done) | data formatting | bytes 20070400
  105.2 0.0 copy-done
  105.2 8.5 %convolution_convert_fusion.1 = bf16[128,2240]{0,1:T(8,128)(2,1)S(1)} fusion(bf16[2240,2240]{1,0:T(8,128)(2,1)} %reshape.84, bf16[1,128,2240]{1,2,0:T(8,128)(2,1)S(1)} %copy-done), kind=kOutput, calls=%fused_computation.35 | convolution fusion | flops 1284792320 | bytes 11182080 | tf_op jit(solution)/shard_map/while/body/dot_general | solution.py:40
  113.7 62.3 %all-gather.5.cloned.1.call-done = bf16[16,140,2240]{2,1,0:T(8,128)(2,1)} async-done(((bf16[1,140,2240]{2,1,0:T(8,128)(2,1)}), bf16[16,140,2240]{2,1,0:T(8,128)(2,1)}) %all-gather.5.cloned.1.call-update) | async-done | bytes 10035216 | tf_op jit(solution)/shard_map/all_gather | solution.py:22
  176.1 11.9 %reshape.82 = bf16[2240,2240]{1,0:T(8,128)(2,1)} reshape(bf16[16,140,2240]{2,1,0:T(8,128)(2,1)} %all-gather.5.cloned.1.call-done) | data formatting | bytes 20070400
  187.9 8.1 %fusion.21 = bf16[128,2240]{0,1:T(8,128)(2,1)S(1)} fusion(bf16[2240,2240]{1,0:T(8,128)(2,1)} %reshape.82, bf16[1,128,2240]{1,2,0:T(8,128)(2,1)S(1)} %copy-done), kind=kOutput, calls=%fused_computation.39 | convolution fusion | flops 1284505600 | bytes 11182080 | tf_op jit(solution)/shard_map/while/body/dot_general | solution.py:37
  196.0 0.1 broadcast.81.clone
  196.1 0.9 broadcast.80.clone.1
  197.0 0.9 broadcast.80.clone.2
  197.9 2.1 while.44
  197.9 0.4 multiply_reduce_fusion.4
  198.3 0.0 copy-start.1
  198.3 0.5 convolution_add_fusion.4
  198.8 0.3 copy-done.1
  199.1 0.1 reduce_sum.37
  199.2 0.8 copy.49
  200.0 0.3 copy.19
  200.3 63.6 %all-reduce.11 = (f32[20,112]{1,0:T(8,128)S(1)}, bf16[20,112,112]{1,2,0:T(8,128)(2,1)S(1)}) all-reduce(f32[20,112]{1,0:T(8,128)S(1)} %get-tuple-element.268, f32[20,112,112]{1,2,0:T(8,128)S(1)} %copy.19), channel_id=1, replica_groups=mesh['dp'=8,'ctx'=16] {'ctx'}, use_global_device_ids=true, to_apply=%region_4.5 | all-reduce | flops 253120 | bytes 1523200 | tf_op jit(solution)/shard_map/psum | solution.py:57
  263.9 0.0 copy-start.3
  263.9 0.0 copy-start.4
  264.0 1.1 broadcast.81
  265.0 0.9 broadcast.80.clone
  265.9 0.0 copy-done.3
  265.9 0.0 copy-done.4
  265.9 5.5 while.45
  265.9 0.1 convert_maximum_fusion.2
  266.0 0.3 fusion.61
  266.4 0.3 fusion.62
  266.7 0.2 convert_compare_fusion.4
  266.9 1.4 fusion.64
  268.3 0.4 multiply_reduce_fusion.5
  268.7 2.7 convolution_add_fusion.5
  271.4 0.0 copy-start.5
  271.4 71.0 %all-reduce.12 = (f32[20,112]{1,0:T(8,128)S(1)}, bf16[20,112,112]{2,1,0:T(8,128)(2,1)S(1)}) all-reduce(f32[20,112]{1,0:T(8,128)S(1)} %get-tuple-element.272, f32[20,112,112]{2,1,0:T(8,128)} %get-tuple-element.273), channel_id=1, replica_groups=mesh['dp'=8,'ctx'=16] {'ctx'}, use_global_device_ids=true, to_apply=%region_9.10 | all-reduce | flops 253120 | bytes 1523200 | tf_op jit(solution)/shard_map/psum | solution.py:81
  342.5 0.0 copy-done.5
  342.5 0.0 copy-start.2
  342.5 0.4 fusion.24
  342.9 0.9 broadcast.80
  343.8 0.0 copy-done.2
  343.8 1.4 while.46
  343.8 0.2 convert_compare_fusion.5
  344.0 1.2 fusion.65
  345.2 7.7 %fusion.18 = bf16[2240,2240]{0,1:T(8,128)(2,1)} fusion(bf16[128,2240]{0,1:T(8,128)(2,1)} %get-tuple-element.275, bf16[1,128,2240]{1,2,0:T(8,128)(2,1)S(1)} %copy-done), kind=kOutput, calls=%fused_computation.34 | convolution fusion | flops 1289523200 | bytes 11182080 | tf_op jit(solution)/shard_map/dot_general | solution.py:94
  352.9 0.0 copy-start.6
  352.9 0.0 all-reduce.10.cloned.1.call-update
  352.9 0.0 all-reduce.8.cloned.1.call-start
  353.0 0.6 copy-done.6
  353.6 0.6 dynamic-slice
  354.8 185.6 %all-reduce.10.cloned.1.call-done = bf16[2240,2240]{0,1:T(8,128)(2,1)} async-done(((bf16[2240,2240]{0,1:T(8,128)(2,1)}), bf16[2240,2240]{0,1:T(8,128)(2,1)}) %all-reduce.10.cloned.1.call-update) | async-done | bytes 10035216
  540.4 3.3 dynamic-slice_convert_fusion
  543.7 0.0 all-reduce.8.cloned.1.call-update
  543.7 64.6 %all-reduce.8.cloned.1.call-done = f32[140,2240]{0,1:T(8,128)} async-done(((f32[140,2240]{0,1:T(8,128)}), f32[140,2240]{0,1:T(8,128)}) %all-reduce.8.cloned.1.call-update) | async-done | bytes 1254416 | tf_op jit(solution)/shard_map/psum | solution.py:101
  608.3 2.8 copy.20
  (9 shorter events, 0.0 us)
Async XLA Ops:
  7.2 98.0 %copy-start = (bf16[1,128,2240]{1,2,0:T(8,128)(2,1)S(1)}, bf16[1,128,2240]{1,2,0:T(8,128)(2,1)}, u32[]{:S(2)}) copy-start(bf16[1,128,2240]{1,2,0:T(8,128)(2,1)} %param.12) | copy-start | bytes 1720324
  7.2 86.1 %all-gather.7.cloned.1.call-start = ((), (), s32[]{:S(2)}) async-start(), calls=%async_computation.2 | async-start | bytes 11280384 | tf_op jit(solution)/shard_map/all_gather | solution.py:23
  7.9 168.1 %all-gather.5.cloned.1.call-start = ((), (), s32[]{:S(2)}) async-start(), calls=%async_computation.1 | async-start | bytes 11280384 | tf_op jit(solution)/shard_map/all_gather | solution.py:22
  8.7 531.8 %all-reduce.10.cloned.1.call-start = ((), (), s32[]{:S(2)}) async-start(), calls=%async_computation.3 | async-start | bytes 20643840
  198.3 0.8 copy-start.1
  263.9 2.0 copy-start.3
  263.9 2.0 copy-start.4
  271.4 71.0 %copy-start.5 = (bf16[128,2240]{0,1:T(8,128)(2,1)S(1)}, bf16[128,2240]{0,1:T(8,128)(2,1)}, u32[]{:S(2)}) copy-start(bf16[128,2240]{0,1:T(8,128)(2,1)} %get-tuple-element.274) | copy-start | bytes 1720324
  342.5 1.3 copy-start.2
  352.9 0.7 copy-start.6
  352.9 255.4 %all-reduce.8.cloned.1.call-start = ((), (), s32[]{:S(2)}) async-start(), calls=%async_computation | async-start | bytes 4587520 | tf_op jit(solution)/shard_map/psum | solution.py:101
Sparse Core Ops, SparseCore 0:
  10.1 83.1 all-gather.6
  95.4 80.5 all-gather.4
  353.1 187.3 all-reduce.9
  543.8 64.4 all-reduce.7
where the time goes:
time: 621 us; the launch traced here: 618 us
  waiting for transfers between devices  398 us (64%)
  blocking collectives  135 us (22%)
  local copies, waits for them, and re-layouts  33.9 us (5%)
  matrix products  30 us (5%)
  between operations  15.2 us (2%)
    unnamed x5, waiting for transfers between devices  187 us
    all_gather x1, waiting for transfers between devices, per_device(): lax.all_gather(value_weight, 'ctx', axis=0, tiled=True)  83.9 us
    psum x1, blocking collectives, per_device(): dsummary, dnormer = lax.psum((dsummary, dnormer), 'ctx')  71 us
    psum x1, waiting for transfers between devices, per_device(): grad_rows = lax.psum(grad_rows, 'dp')  64.6 us
    psum x1, blocking collectives, per_device(): summary, normer = lax.psum((summary, normer), 'ctx')  63.6 us
    all_gather x1, waiting for transfers between devices, per_device(): lax.all_gather(key_weight, 'ctx', axis=0, tiled=True)  62.3 us
    unnamed x16, local copies, waits for them, and re-layouts  27.7 us
  transfers between devices with their start and end apart: 4, of which 4 were waited for; matrix products, arithmetic and copies ran while one was open for 3% of the time, Pallas kernels for 0%

commit v1 on v0

v1 whole, which is shorter than its diff:
```python
import functools

import jax
import jax.numpy as jnp
from jax import lax
from jax.experimental import pallas as pl
from jax.experimental.pallas import tpu as pltpu
from jax.sharding import Mesh
from jax.sharding import PartitionSpec as P

HEADS = 20
HEAD_DIM = 112
D = 2240
NX = 4
NY = 4
NZ = 4
GH = HEADS // NX
GW = GH * HEAD_DIM
ROWS = 128
TOK = ROWS * NX
SH = D // 16
HALF = SH // 2
PAD = 72
SPLIT = 288
BF = jnp.bfloat16
F32 = jnp.float32
VMEM = pl.BlockSpec(memory_space=pltpu.VMEM)
SMEM = pl.BlockSpec(memory_space=pltpu.SMEM)
ANY = pl.BlockSpec(memory_space=pl.ANY)


def params():
    return pltpu.CompilerParams(vmem_limit_bytes=50 * 1024 * 1024)


def call(body, out_shape, in_specs, args, scratch=(), flops=0, nbytes=0, name=None):
    return pl.pallas_call(
        body,
        out_shape=out_shape,
        in_specs=in_specs,
        out_specs=jax.tree.map(lambda _: VMEM, out_shape),
        scratch_shapes=list(scratch),
        compiler_params=params(),
        cost_estimate=pl.CostEstimate(flops=flops, bytes_accessed=nbytes, transcendentals=0),
        name=name,
    )(*args)


def nt(a, b):
    return lax.dot_general(a, b, (((1,), (1,)), ((), ())), preferred_element_type=F32)


def tn(a, b):
    return lax.dot_general(a, b, (((0,), (0,)), ((), ())), preferred_element_type=F32)


def nn(a, b):
    return jnp.dot(a, b, preferred_element_type=F32)


def prep_weights(idx, wk, wv, out):
    for c, src in ((0, wk), (1, wv)):

        @pl.when(idx[1] == c)
        def _():
            for k in range(NX):
                out[k] = src[:, GW * k : GW * (k + 1)]


def prep_queries(idx, q, ct, *outs):
    for d in range(NX):
        for k in range(NX):

            @pl.when(lax.rem(idx[3] + d, NX) == k)
            def _():
                outs[d][0] = q[:, GW * k : GW * (k + 1)]
                outs[d][1] = ct[:, GW * k : GW * (k + 1)]


def live_mask(idx, width=TOK):
    pos = lax.broadcasted_iota(jnp.int32, (1, width), 1) + idx[2] * TOK
    return (pos < idx[4]).astype(F32)


def ones_row(v, row):
    pad = jnp.zeros((15, v.shape[1]), F32)
    return jnp.concatenate([v, row, pad], axis=0)


def project(idx, *refs):
    wblocks, tblocks = refs[:10], refs[10:15]
    kt, vt, summ, tfull, wbuf, sems = refs[15:]
    c, y, x = idx[1], idx[2], idx[3]
    copies = []

    def load(src, dst):
        cp = pltpu.make_async_copy(src, dst, sems.at[len(copies)])
        cp.start()
        copies.append(cp)

    def trow(off):
        return pl.ds(pl.multiple_of(lax.rem(x + off, NX) * ROWS, ROWS), ROWS)

    load(tblocks[0], tfull.at[trow(0)])
    load(tblocks[1], tfull.at[trow(3)])
    load(tblocks[2], tfull.at[trow(1)])
    base = pl.multiple_of(lax.rem(x + 2, NX) * ROWS, ROWS)
    load(tblocks[3], tfull.at[pl.ds(base, ROWS // 2)])
    load(tblocks[4], tfull.at[pl.ds(pl.multiple_of(base + ROWS // 2, ROWS // 2), ROWS // 2)])
    for g, blocks in ((c, wblocks[:5]), (1 - c, wblocks[5:])):
        dst = wbuf.at[g]

        def wrow(off, lo, size):
            start = lax.rem(y + off, NY) * GW + lo
            return pl.ds(pl.multiple_of(start, 16), size)

        load(blocks[0], dst.at[wrow(0, 0, GW)])
        load(blocks[1], dst.at[wrow(3, 0, GW)])
        load(blocks[2], dst.at[wrow(1, 0, GW)])
        load(blocks[3], dst.at[wrow(2, 0, SPLIT)])
        load(blocks[4], dst.at[wrow(2, SPLIT, GW - SPLIT)])
    for cp in copies:
        cp.wait()
    t = tfull[...]
    keys = jnp.maximum(nn(t, wbuf[0]), 0.0).T
    kt[...] = keys.astype(BF)
    vt[...] = nn(t, wbuf[1]).T.astype(BF)
    live = live_mask(idx)
    one = jnp.ones((1, TOK), F32)
    for h in range(GH):
        s = slice(HEAD_DIM * h, HEAD_DIM * (h + 1))
        kh = (kt[s].astype(F32) * live).astype(BF)
        vh = ones_row(vt[s].astype(F32), one).astype(BF)
        summ[s] = nt(kh, vh).astype(BF)


def query_side(idx, s0, s1, s2, s3, q0, q1, q2, q3, *refs):
    gq, dsum, qbuf, cbuf, gbuf, sems = refs[0:4], refs[4], refs[5], refs[6], refs[7], refs[8]
    x = idx[3]
    copies = []
    for d, src in enumerate((q0, q1, q2, q3)):
        rows = pl.ds(pl.multiple_of(lax.rem(x + d, NX) * ROWS, ROWS), ROWS)
        for k, dst in ((0, qbuf), (1, cbuf)):
            cp = pltpu.make_async_copy(src.at[k], dst.at[rows], sems.at[len(copies)])
            cp.start()
            copies.append(cp)
    summ = s0[...].astype(F32) + s1[...].astype(F32) + s2[...].astype(F32) + s3[...].astype(F32)
    live = live_mask(idx)
    length = idx[4].astype(F32)
    for cp in copies:
        cp.wait()
    qt = qbuf[...].astype(F32).T
    ct = cbuf[...].astype(F32).T
    grads = []
    for h in range(GH):
        s = slice(HEAD_DIM * h, HEAD_DIM * (h + 1))
        phi = jnp.maximum(qt[s], 0.0)
        phib = phi.astype(BF)
        back = ct[s] * live
        sh = summ[s].astype(BF)
        numer = tn(sh, phib)
        inv = 1.0 / (numer[HEAD_DIM : HEAD_DIM + 1] + length)
        dnum = back * inv
        dden = -jnp.sum(back * numer[:HEAD_DIM], axis=0, keepdims=True) * inv * inv
        ext = ones_row(dnum, dden).astype(BF)
        dphi = nn(sh, ext)
        grads.append(jnp.where(qt[s] > 0, dphi, 0.0))
        dsum[s] = nt(phib, ext).astype(BF)
    gbuf[...] = jnp.concatenate(grads, axis=0).T.astype(BF)
    for d in range(NX):
        rows = pl.ds(pl.multiple_of(lax.rem(x + d, NX) * ROWS, ROWS), ROWS)
        gq[d][...] = gbuf[rows]


def key_side(idx, s0, s1, s2, s3, kt, vt, dkt):
    summ = s0[...].astype(F32) + s1[...].astype(F32) + s2[...].astype(F32) + s3[...].astype(F32)
    summ = summ.astype(BF)
    live = live_mask(idx)
    one = jnp.ones((1, TOK), F32)
    for h in range(GH):
        s = slice(HEAD_DIM * h, HEAD_DIM * (h + 1))
        vh = ones_row(vt[s].astype(F32), one).astype(BF)
        dk = nn(summ[s], vh)
        keep = (kt[s].astype(F32) > 0) & (live > 0)
        dkt[s] = jnp.where(keep, dk, 0.0).astype(BF)


def transpose_tokens(idx, t, own, oth, buf):
    for k in range(0, D, 128):
        w = min(128, D - k)
        buf[k : k + w] = t[:, k : k + w].astype(F32).T
    zero = jnp.zeros((PAD - HALF, TOK), F32)
    for c in range(2):

        @pl.when(idx[1] == c)
        def _():
            for i in range(16):
                base = SH * ((i % 4) * 4 + i // 4)
                for half, dst in ((c, own), (1 - c, oth)):
                    lo = base + HALF * half
                    rows = jnp.concatenate([buf[lo : lo + HALF], zero], axis=0)
                    dst[PAD * i : PAD * (i + 1)] = rows.astype(BF)


def grad_weights(t_own, t_oth, d_own, d_oth, out):
    out[...] = (nt(t_own[...], d_own[...]) + nt(t_oth[...], d_oth[...])).astype(BF)


def sum_pieces(g, out):
    total = g[0].astype(F32)
    for i in range(1, 16):
        total = total + g[i].astype(F32)
    out[...] = total.astype(BF)


def place_rows(g, out):
    for z in range(NZ):
        for c in range(2):
            out[HALF * c : HALF * (c + 1), GW * z : GW * (z + 1)] = g[2 * z + c, :HALF].astype(F32)


def place_queries(idx, g0, g1, g2, g3, out):
    for d, src in enumerate((g0, g1, g2, g3)):
        for k in range(NX):

            @pl.when(lax.rem(idx[3] + d, NX) == k)
            def _():
                out[:, GW * k : GW * (k + 1)] = src[...]


def shift(v, axis, d, n=4):
    return lax.ppermute(v, axis, [(i, (i + d) % n) for i in range(n)])


def sds(shape, dtype=BF):
    return jax.ShapeDtypeStruct(shape, dtype)


def per_device(tokens, queries, cotangent, key_weight, value_weight, clip_len):
    z, c, y, x = (lax.axis_index(a) for a in ("z", "core", "y", "x"))
    idx = jnp.stack([z, c, y, x, clip_len[0]]).astype(jnp.int32)
    feats, quers, backs = tokens[0], queries[0], cotangent[0]

    def swap(v):
        return shift(v, "core", 1, 2)

    def sum_parts(s):
        return [s] + [shift(s, "y", d) for d in (1, 3, 2)]

    pieces = call(
        prep_weights, sds((NX, SH, GW)), [SMEM, VMEM, VMEM], (idx, key_weight, value_weight)
    )
    w_own = lax.all_to_all(pieces, "x", 0, 0, tiled=True).reshape(GW, GW)
    w_prev = shift(w_own, "y", 1)
    w_next = shift(w_own, "y", -1)
    t_prev = shift(feats, "x", 1)
    t_next = shift(feats, "x", -1)
    w_lo = shift(w_prev[:SPLIT], "y", 1)
    w_hi = shift(w_next[SPLIT:], "y", -1)
    t_lo = shift(t_prev[: ROWS // 2], "x", 1)
    t_hi = shift(t_next[ROWS // 2 :], "x", -1)
    blocks = [w_own, w_prev, w_next, w_lo, w_hi]
    blocks = blocks + [swap(b) for b in blocks]

    qc = call(
        prep_queries, [sds((2, ROWS, GW))] * NX, [SMEM, VMEM, VMEM], (idx, quers, backs)
    )
    q_in = [qc[0]]
    for d in (1, 2, 3):
        q_in.append(shift(qc[NX - d], "x", -d))

    kt, vt, summ, tfull = call(
        project,
        [sds((GW, TOK)), sds((GW, TOK)), sds((GW, 128)), sds((TOK, D))],
        [SMEM] + [ANY] * 15,
        (idx, *blocks, feats, t_prev, t_next, t_lo, t_hi),
        scratch=[pltpu.VMEM((2, D, GW), BF), pltpu.SemaphoreType.DMA((15,))],
        flops=4 * TOK * D * GW,
        nbytes=12_000_000,
    )
    t_own, t_oth = call(
        transpose_tokens,
        [sds((16 * PAD, TOK))] * 2,
        [SMEM, VMEM],
        (idx, tfull),
        scratch=[pltpu.VMEM((D, TOK), F32)],
        nbytes=10_000_000,
    )
    t_oth = swap(t_oth)

    outs = call(
        query_side,
        [sds((ROWS, GW))] * NX + [sds((GW, 128))],
        [SMEM] + [VMEM] * 4 + [ANY] * 4,
        (idx, *sum_parts(summ), *q_in),
        scratch=[pltpu.VMEM((TOK, GW), BF)] * 3 + [pltpu.SemaphoreType.DMA((8,))],
        flops=6 * TOK * GW * 128,
        nbytes=4_000_000,
    )
    gq, dsum = outs[:NX], outs[NX]
    g_in = [gq[0]]
    for d in (1, 2, 3):
        g_in.append(shift(gq[NX - d], "x", -d))
    dkt = call(
        key_side,
        sds((GW, TOK)),
        [SMEM] + [VMEM] * 6,
        (idx, *sum_parts(dsum), kt, vt),
        flops=2 * TOK * GW * 128,
        nbytes=2_000_000,
    )
    part = call(
        grad_weights,
        sds((16 * PAD, GW)),
        [VMEM] * 4,
        (t_own, t_oth, dkt, swap(dkt)),
        flops=4 * 16 * PAD * TOK * GW,
        nbytes=6_000_000,
    )
    part = lax.all_to_all(part.reshape(16, PAD, GW), ("z", "y"), 0, 0, tiled=True)
    rows = call(sum_pieces, sds((PAD, GW)), [VMEM], (part,))
    rows = lax.ppermute(rows, ("z", "x"), [(a * 4 + b, b * 4 + a) for a in range(4) for b in range(4)])
    rows = lax.all_gather(rows, ("z", "core"))
    grad_rows = call(place_rows, sds((SH, D), F32), [VMEM], (rows,))
    grad_q = call(place_queries, sds((ROWS, D)), [SMEM] + [VMEM] * 4, (idx, *g_in))
    return grad_q[None], grad_rows


def solution(mesh):
    grid = Mesh(mesh.devices.reshape(NZ, 2, NY, NX), ("z", "core", "y", "x"))
    dp, ctx = ("z", "core"), ("y", "x")
    in_specs = (
        P(dp, ctx, None),
        P(dp, ctx, None),
        P(dp, ctx, None),
        P(ctx, None),
        P(ctx, None),
        P(dp),
    )
    out_specs = (P(dp, ctx, None), P(ctx, None))
    return jax.shard_map(
        per_device, mesh=grid, in_specs=in_specs, out_specs=out_specs, check_vma=False
    )
```

time: 621 us -> 175 us (0.28)
  waiting for transfers between devices: 398 us -> 63.5 us
  blocking collectives: 135 us -> 16.1 us
  starting transfers between devices: 0.16 us -> 56.4 us
  matrix products: 30 us -> 0 us
  Pallas kernels: 0 us -> 25.5 us
  local copies, waits for them, and re-layouts: 33.9 us -> 11.2 us
  between operations: 15.2 us -> 1.59 us
    unnamed x5 -> x0, waiting for transfers between devices: 187 us -> none
    all_gather x2 -> x0, waiting for transfers between devices: 146 us -> none  [the longest x1 83.9 us: per_device(): lax.all_gather(value_weight, 'ctx', axis=0, tiled=True)]
    psum x2 -> x0, blocking collectives: 135 us -> none  [the longest x1 71 us: per_device(): dsummary, dnormer = lax.psum((dsummary, dnormer), 'ctx')]
    psum x1 -> x0, waiting for transfers between devices: 64.6 us -> none  [per_device(): grad_rows = lax.psum(grad_rows, 'dp')]
    ppermute x0 -> x28, starting transfers between devices: none -> 45.7 us  [the longest x27 43.7 us: shift(): return lax.ppermute(v, axis, [(i, (i + d) % n) for i in range(n)])]
    ppermute x0 -> x28, waiting for transfers between devices: none -> 37.7 us  [the longest x27 32.3 us: shift(): return lax.ppermute(v, axis, [(i, (i + d) % n) for i in range(n)])]
    dot_general x9 -> x0, matrix products: 30 us -> none  [the longest x1 8.51 us: forward_step(): jnp.dot(feats, value_full, preferred_element_type=jnp.float32)]
    all_to_all x0 -> x2, waiting for transfers between devices: none -> 25.8 us  [the longest x1 18.1 us: per_device(): lax.all_to_all(part.reshape(16, PAD, GW), ('z', 'y'), 0, 0, tiled=True)]
  transfers between devices with their start and end apart: 4 -> 30, of which waited for: 4 -> 13; matrix products, arithmetic and copies ran while one was open for 3% -> 4% of each run, Pallas kernels for 0% -> 4%
where the time goes in v1:
time: 175 us; the launch traced here: 174 us
  waiting for transfers between devices  63.5 us (36%)
  starting transfers between devices  56.4 us (32%)
  Pallas kernels  25.5 us (15%)
  blocking collectives  16.1 us (9%)
  local copies, waits for them, and re-layouts  11.2 us (6%)
    ppermute x27, starting transfers between devices, shift(): return lax.ppermute(v, axis, [(i, (i + d) % n) for i in range(n)])  43.7 us
    ppermute x27, waiting for transfers between devices, shift(): return lax.ppermute(v, axis, [(i, (i + d) % n) for i in range(n)])  32.3 us
    pallas_call x10, Pallas kernels, call(): pl.pallas_call(body, out_shape=out_shape, in_specs=in_specs, out_specs=ja...  25.5 us
    all_to_all x1, waiting for transfers between devices, per_device(): lax.all_to_all(part.reshape(16, PAD, GW), ('z', 'y'), 0, 0, tiled=True)  18.1 us
    all_gather x1, blocking collectives, per_device(): rows = lax.all_gather(rows, ('z', 'core'))  16.1 us
    all_to_all x1, waiting for transfers between devices, per_device(): w_own = lax.all_to_all(pieces, 'x', 0, 0, tiled=True).reshape(GW, GW)  7.64 us
    unnamed x32, local copies, waits for them, and re-layouts  7.42 us
    all_to_all x1, starting transfers between devices, per_device(): lax.all_to_all(part.reshape(16, PAD, GW), ('z', 'y'), 0, 0, tiled=True)  6.56 us
  transfers between devices with their start and end apart: 30, of which 13 were waited for; matrix products, arithmetic and copies ran while one was open for 4% of the time, Pallas kernels for 4%

profile of v1, /device:TPU:7, one launch (start us, length us, event | category | flops | bytes accessed | tf_op | source)
XLA Modules:
  0.0 174.3 jit_solution(13535519882013527616)
XLA Ops:
  1.3 0.1 stack.19.idx
  1.4 1.1 copy-done
  2.5 1.1 copy-done.1
  3.5 1.7 shard_map.77
  5.2 4.2 %all-to-all-start = ((bf16[4,140,560]{2,1,0:T(8,128)(2,1)}), bf16[4,140,560]{2,1,0:T(8,128)(2,1)S(1)}, u32[]{:S(2)}, u32[]{:S(2)}) async-start(bf16[4,140,560]{2,1,0:T(8,128)(2,1)} %shard_map.77), calls=%async_computation | async-start | bytes 1474560 | tf_op jit(solution)/shard_map/all_to_all | solution.py:253
  9.4 1.4 collective-permute-start.10
  10.9 7.6 %all-to-all-done = bf16[4,140,560]{2,1,0:T(8,128)(2,1)S(1)} async-done(((bf16[4,140,560]{2,1,0:T(8,128)(2,1)}), bf16[4,140,560]{2,1,0:T(8,128)(2,1)S(1)}, u32[]{:S(2)}, u32[]{:S(2)}) %all-to-all-start) | async-done | bytes 627232 | tf_op jit(solution)/shard_map/all_to_all | solution.py:253
  18.5 1.1 reshape.10.refs_0_
  19.7 1.3 collective-permute-start
  21.0 1.4 collective-permute-start.1
  22.4 7.9 %collective-permute-done.9 = bf16[128,2240]{0,1:T(8,128)(2,1)S(1)} collective-permute-done((bf16[128,2240]{0,1:T(8,128)(2,1)S(1)}, bf16[128,2240]{0,1:T(8,128)(2,1)S(1)}, u32[]{:S(2)}, u32[]{:S(2)}) %collective-permute-start.9) | collective-permute-done | bytes 573472 | tf_op jit(solution)/shard_map/ppermute | solution.py:232
  30.3 0.3 copy.21.refs_11_
  30.6 2.1 %collective-permute-start.11 = (bf16[64,2240]{1,0:T(8,128)(2,1)S(1)}, bf16[64,2240]{1,0:T(8,128)(2,1)S(1)}, u32[]{:S(2)}, u32[]{:S(2)}) collective-permute-start(bf16[64,2240]{1,0:T(8,128)(2,1)S(1)} %slice.18), channel_id=1, source_target_pairs={{0,1},{1,2},{2,3},{3,0},{4,5},{5,6},{6,7},{7,4},{8,9},{9,10},{10,1... | collective-permute-start | bytes 860168 | tf_op jit(solution)/shard_map/ppermute | solution.py:232
  32.7 0.3 copy.22.refs_12_
  33.0 0.8 copy-done.11
  33.8 0.1 collective-permute-start.12
  33.9 1.6 collective-permute-done.refs_1_
  35.5 1.0 slice.16
  36.7 4.5 %collective-permute-start.4 = (bf16[560,560]{1,0:T(8,128)(2,1)}, bf16[560,560]{1,0:T(8,128)(2,1)}, u32[]{:S(2)}, u32[]{:S(2)}) collective-permute-start(bf16[560,560]{1,0:T(8,128)(2,1)} %reshape.10.refs_0_), channel_id=1, source_target_pairs={{0,16},{16,0},{1,17},{17,1},{2,18},{18,2},{3,19},{19,3},{4,20},{20... | collective-permute-start | bytes 1881608 | tf_op jit(solution)/shard_map/ppermute | solution.py:232
  41.1 0.5 collective-permute-start.6
  41.6 1.0 slice.17
  42.7 2.7 %collective-permute-start.3 = (bf16[272,560]{1,0:T(8,128)(2,1)S(1)}, bf16[272,560]{1,0:T(8,128)(2,1)S(1)}, u32[]{:S(2)}, u32[]{:S(2)}) collective-permute-start(bf16[272,560]{1,0:T(8,128)(2,1)S(1)} %slice.17), channel_id=1, source_target_pairs={{0,12},{4,0},{8,4},{12,8},{1,13},{5,1},{9,5},{13,9},{2,14},{6,2},{... | collective-permute-start | bytes 913928 | tf_op jit(solution)/shard_map/ppermute | solution.py:232
  45.4 4.2 %collective-permute-start.7 = (bf16[288,560]{1,0:T(8,128)(2,1)S(1)}, bf16[288,560]{1,0:T(8,128)(2,1)S(1)}, u32[]{:S(2)}, u32[]{:S(2)}) collective-permute-start(bf16[288,560]{1,0:T(8,128)(2,1)S(1)} %collective-permute-done.2.refs_3_), channel_id=1, source_target_pairs={{0,16},{16,0},{1,17},{17,1},{2,18},{18,2},{3,19},{19,3},{4,20},{20... | collective-permute-start | bytes 967688 | tf_op jit(solution)/shard_map/ppermute | solution.py:232
  49.5 1.4 collective-permute-done.3.refs_4_
  51.0 2.8 %collective-permute-start.8 = (bf16[272,560]{1,0:T(8,128)(2,1)S(1)}, bf16[272,560]{1,0:T(8,128)(2,1)S(1)}, u32[]{:S(2)}, u32[]{:S(2)}) collective-permute-start(bf16[272,560]{1,0:T(8,128)(2,1)S(1)} %collective-permute-done.3.refs_4_), channel_id=1, source_target_pairs={{0,16},{16,0},{1,17},{17,1},{2,18},{18,2},{3,19},{19,3},{4,20},{20... | collective-permute-start | bytes 913928 | tf_op jit(solution)/shard_map/ppermute | solution.py:232
  53.8 0.3 copy.16
  54.0 1.0 collective-permute-done.8.refs_9_
  55.1 7.5 %shard_map.78 = (bf16[560,512]{1,0:T(8,128)(2,1)S(1)}, bf16[560,512]{1,0:T(8,128)(2,1)S(1)}, bf16[560,128]{1,0:T(8,128)(2,1)S(1)}, bf16[512,2240]{1,0:T(8,128)(2,1)}) custom-call(s32[5]{0:T(128)S(1)} %stack.19.idx, bf16[560,560]{1,0:T(8,128)(2,1)} %reshape.10.refs_0_, bf16[560,560]{1,0:T(8,128)(2,1)} %collective-permute-done.refs_1_, ...), custom_call_target="tpu_custom_call" | custom-call | flops 2569011200 | bytes 12000000 | tf_op jit(solution)/shard_map/pallas_call | solution.py:37
  62.6 4.2 %shard_map.82 = (bf16[1152,512]{1,0:T(8,128)(2,1)S(1)}, bf16[1152,512]{1,0:T(8,128)(2,1)}) custom-call(s32[5]{0:T(128)S(1)} %stack.19.idx, bf16[512,2240]{1,0:T(8,128)(2,1)} %get-tuple-element.26.t), custom_call_target="tpu_custom_call" | custom-call | bytes 10000000 | tf_op jit(solution)/shard_map/pallas_call | solution.py:37
  66.8 0.4 collective-permute-start.22
  67.3 0.3 copy.23
  67.5 1.3 copy.24
  68.8 1.4 shard_map.79
  70.3 3.0 %collective-permute-start.17 = (bf16[2,128,560]{2,1,0:T(8,128)(2,1)S(1)}, bf16[2,128,560]{2,1,0:T(8,128)(2,1)S(1)}, u32[]{:S(2)}, u32[]{:S(2)}) collective-permute-start(bf16[2,128,560]{2,1,0:T(8,128)(2,1)S(1)} %get-tuple-element.20), channel_id=1, source_target_pairs={{0,2},{1,3},{2,0},{3,1},{4,6},{5,7},{6,4},{7,5},{8,10},{9,11},{10,... | collective-permute-start | bytes 860168 | tf_op jit(solution)/shard_map/ppermute | solution.py:232
  73.3 0.9 collective-permute-start.18
  74.2 0.8 collective-permute-start.13
  75.0 5.7 %collective-permute-done.16.q1 = bf16[2,128,560]{2,1,0:T(8,128)(2,1)S(1)} collective-permute-done((bf16[2,128,560]{2,1,0:T(8,128)(2,1)S(1)}, bf16[2,128,560]{2,1,0:T(8,128)(2,1)S(1)}, u32[]{:S(2)}, u32[]{:S(2)}) %collective-permute-start.16) | collective-permute-done | bytes 286752 | tf_op jit(solution)/shard_map/ppermute | solution.py:232
  80.7 3.4 %collective-permute-start.14 = (bf16[560,128]{1,0:T(8,128)(2,1)}, bf16[560,128]{1,0:T(8,128)(2,1)S(1)}, u32[]{:S(2)}, u32[]{:S(2)}) collective-permute-start(bf16[560,128]{1,0:T(8,128)(2,1)} %copy-done.8), channel_id=1, source_target_pairs={{0,12},{4,0},{8,4},{12,8},{1,13},{5,1},{9,5},{13,9},{2,14},{6,2},{... | collective-permute-start | bytes 430088 | tf_op jit(solution)/shard_map/ppermute | solution.py:232
  84.1 3.9 %collective-permute-done.17.q2 = bf16[2,128,560]{2,1,0:T(8,128)(2,1)S(1)} collective-permute-done((bf16[2,128,560]{2,1,0:T(8,128)(2,1)S(1)}, bf16[2,128,560]{2,1,0:T(8,128)(2,1)S(1)}, u32[]{:S(2)}, u32[]{:S(2)}) %collective-permute-start.17) | collective-permute-done | bytes 286752 | tf_op jit(solution)/shard_map/ppermute | solution.py:232
  88.0 2.3 %collective-permute-start.15 = (bf16[560,128]{1,0:T(8,128)(2,1)}, bf16[560,128]{1,0:T(8,128)(2,1)S(1)}, u32[]{:S(2)}, u32[]{:S(2)}) collective-permute-start(bf16[560,128]{1,0:T(8,128)(2,1)} %copy-done.8), channel_id=1, source_target_pairs={{0,8},{4,12},{8,0},{12,4},{1,9},{5,13},{9,1},{13,5},{2,10},{6,14},... | collective-permute-start | bytes 430088 | tf_op jit(solution)/shard_map/ppermute | solution.py:232
  90.3 3.7 %collective-permute-done.15.s3 = bf16[560,128]{1,0:T(8,128)(2,1)S(1)} collective-permute-done((bf16[560,128]{1,0:T(8,128)(2,1)}, bf16[560,128]{1,0:T(8,128)(2,1)S(1)}, u32[]{:S(2)}, u32[]{:S(2)}) %collective-permute-start.15) | collective-permute-done | bytes 143392 | tf_op jit(solution)/shard_map/ppermute | solution.py:232
  94.1 0.9 copy-done.9
  95.0 4.2 %shard_map.80 = (bf16[128,560]{1,0:T(8,128)(2,1)S(1)}, bf16[128,560]{1,0:T(8,128)(2,1)S(1)}, bf16[128,560]{1,0:T(8,128)(2,1)S(1)}, bf16[128,560]{1,0:T(8,128)(2,1)S(1)}, bf16[560,128]{1,0:T(8,128)(2,1)S(1)}) custom-call(s32[5]{0:T(128)S(1)} %stack.19.idx, bf16[560,128]{1,0:T(8,128)(2,1)S(1)} %copy-done.9, bf16[560,128]{1,0:T(8,128)(2,1)S(1)} %collective-permute-done.13.s1, ...), custom_call_target="tpu_custom_call" | custom-call | flops 220200960 | bytes 4000000 | tf_op jit(solution)/shard_map/pallas_call | solution.py:37
  99.1 0.6 copy-done.6
  99.8 1.3 collective-permute-start.23
  101.1 2.2 %collective-permute-start.24 = (bf16[560,128]{1,0:T(8,128)(2,1)S(1)}, bf16[560,128]{1,0:T(8,128)(2,1)S(1)}, u32[]{:S(2)}, u32[]{:S(2)}) collective-permute-start(bf16[560,128]{1,0:T(8,128)(2,1)S(1)} %get-tuple-element.29.s0), channel_id=1, source_target_pairs={{0,12},{4,0},{8,4},{12,8},{1,13},{5,1},{9,5},{13,9},{2,14},{6,2},{... | collective-permute-start | bytes 430088 | tf_op jit(solution)/shard_map/ppermute | solution.py:232
  103.2 1.2 collective-permute-start.25
  104.4 1.3 collective-permute-done.23.s1
  105.7 4.0 %collective-permute-done.25.s3 = bf16[560,128]{1,0:T(8,128)(2,1)S(1)} collective-permute-done((bf16[560,128]{1,0:T(8,128)(2,1)S(1)}, bf16[560,128]{1,0:T(8,128)(2,1)S(1)}, u32[]{:S(2)}, u32[]{:S(2)}) %collective-permute-start.25) | collective-permute-done | bytes 143392 | tf_op jit(solution)/shard_map/ppermute | solution.py:232
  109.7 0.9 shard_map.83.d_own
  110.6 2.8 %collective-permute-start.26 = (bf16[560,512]{1,0:T(8,128)(2,1)S(1)}, bf16[560,512]{1,0:T(8,128)(2,1)S(1)}, u32[]{:S(2)}, u32[]{:S(2)}) collective-permute-start(bf16[560,512]{1,0:T(8,128)(2,1)S(1)} %shard_map.83.d_own), channel_id=1, source_target_pairs={{0,16},{16,0},{1,17},{17,1},{2,18},{18,2},{3,19},{19,3},{4,20},{20... | collective-permute-start | bytes 1720328 | tf_op jit(solution)/shard_map/ppermute | solution.py:232
  113.4 1.6 collective-permute-done.26.d_oth
  115.0 3.2 %shard_map.84 = bf16[1152,560]{1,0:T(8,128)(2,1)} custom-call(bf16[1152,512]{1,0:T(8,128)(2,1)S(1)} %get-tuple-element.27.t_own, bf16[1152,512]{1,0:T(8,128)(2,1)S(1)} %collective-permute-done.22.t_oth, bf16[560,512]{1,0:T(8,128)(2,1)S(1)} %shard_map.83.d_own, bf16[560,512]{1,0:T(8,128)(2,1)S(1)} %collective-permute-done.26.d_oth), custom_call_target="tpu_custom_call" | custom-call | flops 1321205760 | bytes 6000000 | tf_op jit(solution)/shard_map/pallas_call | solution.py:37
  118.2 6.6 %all-to-all-start.1 = ((bf16[16,72,560]{2,1,0:T(8,128)(2,1)}), bf16[16,72,560]{2,1,0:T(8,128)(2,1)S(1)}, u32[]{:S(2)}, u32[]{:S(2)}) async-start(bf16[16,72,560]{2,1,0:T(8,128)(2,1)} %bitcast.16), calls=%async_computation.1 | async-start | bytes 2949120 | tf_op jit(solution)/shard_map/all_to_all | solution.py:320
  124.8 2.3 %collective-permute-start.20 = (bf16[128,560]{1,0:T(8,128)(2,1)S(1)}, bf16[128,560]{1,0:T(8,128)(2,1)S(1)}, u32[]{:S(2)}, u32[]{:S(2)}) collective-permute-start(bf16[128,560]{1,0:T(8,128)(2,1)S(1)} %get-tuple-element.24), channel_id=1, source_target_pairs={{0,2},{1,3},{2,0},{3,1},{4,6},{5,7},{6,4},{7,5},{8,10},{9,11},{10,... | collective-permute-start | bytes 430088 | tf_op jit(solution)/shard_map/ppermute | solution.py:232
  127.1 2.0 %collective-permute-start.21 = (bf16[128,560]{1,0:T(8,128)(2,1)S(1)}, bf16[128,560]{1,0:T(8,128)(2,1)S(1)}, u32[]{:S(2)}, u32[]{:S(2)}) collective-permute-start(bf16[128,560]{1,0:T(8,128)(2,1)S(1)} %get-tuple-element.25), channel_id=1, source_target_pairs={{0,1},{1,2},{2,3},{3,0},{4,5},{5,6},{6,7},{7,4},{8,9},{9,10},{10,1... | collective-permute-start | bytes 430088 | tf_op jit(solution)/shard_map/ppermute | solution.py:232
  129.1 18.1 %all-to-all-done.1.g = bf16[16,72,560]{2,1,0:T(8,128)(2,1)S(1)} async-done(((bf16[16,72,560]{2,1,0:T(8,128)(2,1)}), bf16[16,72,560]{2,1,0:T(8,128)(2,1)S(1)}, u32[]{:S(2)}, u32[]{:S(2)}) %all-to-all-start.1) | async-done | bytes 1290272 | tf_op jit(solution)/shard_map/all_to_all | solution.py:320
  147.2 0.2 shard_map.85
  147.4 1.9 %collective-permute-start.27 = (bf16[72,560]{1,0:T(8,128)(2,1)S(1)}, bf16[72,560]{1,0:T(8,128)(2,1)S(1)}, u32[]{:S(2)}, u32[]{:S(2)}) collective-permute-start(bf16[72,560]{1,0:T(8,128)(2,1)S(1)} %shard_map.85), channel_id=1, source_target_pairs={{0,0},{1,32},{2,64},{3,96},{32,1},{33,33},{34,65},{35,97},{64,2},{... | collective-permute-start | bytes 241928 | tf_op jit(solution)/shard_map/ppermute | solution.py:322
  149.4 1.1 shard_map.81
  150.5 1.0 copy.25
  151.5 5.4 %collective-permute-done.27 = bf16[72,560]{1,0:T(8,128)(2,1)S(1)} collective-permute-done((bf16[72,560]{1,0:T(8,128)(2,1)S(1)}, bf16[72,560]{1,0:T(8,128)(2,1)S(1)}, u32[]{:S(2)}, u32[]{:S(2)}) %collective-permute-start.27) | collective-permute-done | bytes 80672 | tf_op jit(solution)/shard_map/ppermute | solution.py:322
  156.9 16.1 %all-gather = bf16[576,560]{1,0:T(8,128)(2,1)S(1)} all-gather(bf16[72,560]{1,0:T(8,128)(2,1)S(1)} %collective-permute-done.27), channel_id=2, replica_groups=mesh['z'=4,'core'=2,'y'=4,'x'=4] {'z','core'}, dimensions={0}, use_global_device_ids=true | all-gather | bytes 725760 | tf_op jit(solution)/shard_map/all_gather | solution.py:323
  173.0 1.3 shard_map.86
  (47 shorter events, 0.4 us)
Async XLA Ops:
  1.4 1.1 copy-start
  2.5 1.1 copy-start.1
  3.5 5.9 %copy-start.12 = (bf16[1,128,2240]{1,2,0:T(8,128)(2,1)S(1)}, bf16[1,128,2240]{1,2,0:T(8,128)(2,1)}, u32[]{:S(2)}) copy-start(bf16[1,128,2240]{1,2,0:T(8,128)(2,1)} %param.6) | copy-start | bytes 1720324
  5.2 13.3 %all-to-all-start = ((bf16[4,140,560]{2,1,0:T(8,128)(2,1)}), bf16[4,140,560]{2,1,0:T(8,128)(2,1)S(1)}, u32[]{:S(2)}, u32[]{:S(2)}) async-start(bf16[4,140,560]{2,1,0:T(8,128)(2,1)} %shard_map.77), calls=%async_computation | async-start | bytes 1474560 | tf_op jit(solution)/shard_map/all_to_all | solution.py:253
  9.4 20.9 %collective-permute-start.9 = (bf16[128,2240]{0,1:T(8,128)(2,1)S(1)}, bf16[128,2240]{0,1:T(8,128)(2,1)S(1)}, u32[]{:S(2)}, u32[]{:S(2)}) collective-permute-start(bf16[128,2240]{0,1:T(8,128)(2,1)S(1)} %bitcast.17), channel_id=1, source_target_pairs={{0,1},{1,2},{2,3},{3,0},{4,5},{5,6},{6,7},{7,4},{8,9},{9,10},{10,1... | collective-permute-start | bytes 1720328 | tf_op jit(solution)/shard_map/ppermute | solution.py:232
  9.4 23.3 %collective-permute-start.10 = (bf16[128,2240]{0,1:T(8,128)(2,1)S(1)}, bf16[128,2240]{0,1:T(8,128)(2,1)S(1)}, u32[]{:S(2)}, u32[]{:S(2)}) collective-permute-start(bf16[128,2240]{0,1:T(8,128)(2,1)S(1)} %bitcast.18), channel_id=1, source_target_pairs={{0,3},{1,0},{2,1},{3,2},{4,7},{5,4},{6,5},{7,6},{8,11},{9,8},{10,9... | collective-permute-start | bytes 1720328 | tf_op jit(solution)/shard_map/ppermute | solution.py:232
  19.7 15.9 %collective-permute-start = (bf16[560,560]{1,0:T(8,128)(2,1)}, bf16[560,560]{1,0:T(8,128)(2,1)}, u32[]{:S(2)}, u32[]{:S(2)}) collective-permute-start(bf16[560,560]{1,0:T(8,128)(2,1)} %reshape.10.refs_0_), channel_id=1, source_target_pairs={{0,4},{4,8},{8,12},{12,0},{1,5},{5,9},{9,13},{13,1},{2,6},{6,10},{... | collective-permute-start | bytes 1881608 | tf_op jit(solution)/shard_map/ppermute | solution.py:232
  21.0 20.2 %collective-permute-start.1 = (bf16[560,560]{1,0:T(8,128)(2,1)}, bf16[560,560]{1,0:T(8,128)(2,1)}, u32[]{:S(2)}, u32[]{:S(2)}) collective-permute-start(bf16[560,560]{1,0:T(8,128)(2,1)} %reshape.10.refs_0_), channel_id=1, source_target_pairs={{0,12},{4,0},{8,4},{12,8},{1,13},{5,1},{9,5},{13,9},{2,14},{6,2},{... | collective-permute-start | bytes 1881608 | tf_op jit(solution)/shard_map/ppermute | solution.py:232
  30.6 6.0 %copy-start.10 = (bf16[128,2240]{1,0:T(8,128)(2,1)}, bf16[128,2240]{1,0:T(8,128)(2,1)S(1)}, u32[]{:S(2)}) copy-start(bf16[128,2240]{1,0:T(8,128)(2,1)S(1)} %copy.21.refs_11_) | copy-start | bytes 1720324
  30.6 10.5 %collective-permute-start.11 = (bf16[64,2240]{1,0:T(8,128)(2,1)S(1)}, bf16[64,2240]{1,0:T(8,128)(2,1)S(1)}, u32[]{:S(2)}, u32[]{:S(2)}) collective-permute-start(bf16[64,2240]{1,0:T(8,128)(2,1)S(1)} %slice.18), channel_id=1, source_target_pairs={{0,1},{1,2},{2,3},{3,0},{4,5},{5,6},{6,7},{7,4},{8,9},{9,10},{10,1... | collective-permute-start | bytes 860168 | tf_op jit(solution)/shard_map/ppermute | solution.py:232
  33.0 0.8 copy-start.11
  33.8 8.8 %collective-permute-start.12 = (bf16[64,2240]{1,0:T(8,128)(2,1)S(1)}, bf16[64,2240]{1,0:T(8,128)(2,1)S(1)}, u32[]{:S(2)}, u32[]{:S(2)}) collective-permute-start(bf16[64,2240]{1,0:T(8,128)(2,1)S(1)} %slice.19), channel_id=1, source_target_pairs={{0,3},{1,0},{2,1},{3,2},{4,7},{5,4},{6,5},{7,6},{8,11},{9,8},{10,9... | collective-permute-start | bytes 860168 | tf_op jit(solution)/shard_map/ppermute | solution.py:232
  36.6 8.8 %collective-permute-start.2 = (bf16[288,560]{1,0:T(8,128)(2,1)S(1)}, bf16[288,560]{1,0:T(8,128)(2,1)S(1)}, u32[]{:S(2)}, u32[]{:S(2)}) collective-permute-start(bf16[288,560]{1,0:T(8,128)(2,1)S(1)} %slice.16), channel_id=1, source_target_pairs={{0,4},{4,8},{8,12},{12,0},{1,5},{5,9},{9,13},{13,1},{2,6},{6,10},{... | collective-permute-start | bytes 967688 | tf_op jit(solution)/shard_map/ppermute | solution.py:232
  36.7 17.4 %collective-permute-start.4 = (bf16[560,560]{1,0:T(8,128)(2,1)}, bf16[560,560]{1,0:T(8,128)(2,1)}, u32[]{:S(2)}, u32[]{:S(2)}) collective-permute-start(bf16[560,560]{1,0:T(8,128)(2,1)} %reshape.10.refs_0_), channel_id=1, source_target_pairs={{0,16},{16,0},{1,17},{17,1},{2,18},{18,2},{3,19},{19,3},{4,20},{20... | collective-permute-start | bytes 1881608 | tf_op jit(solution)/shard_map/ppermute | solution.py:232
  41.1 13.9 %collective-permute-start.5 = (bf16[560,560]{1,0:T(8,128)(2,1)}, bf16[560,560]{1,0:T(8,128)(2,1)}, u32[]{:S(2)}, u32[]{:S(2)}) collective-permute-start(bf16[560,560]{1,0:T(8,128)(2,1)} %collective-permute-done.refs_1_), channel_id=1, source_target_pairs={{0,16},{16,0},{1,17},{17,1},{2,18},{18,2},{3,19},{19,3},{4,20},{20... | collective-permute-start | bytes 1881608 | tf_op jit(solution)/shard_map/ppermute | solution.py:232
  41.1 13.9 %collective-permute-start.6 = (bf16[560,560]{1,0:T(8,128)(2,1)}, bf16[560,560]{1,0:T(8,128)(2,1)}, u32[]{:S(2)}, u32[]{:S(2)}) collective-permute-start(bf16[560,560]{1,0:T(8,128)(2,1)} %collective-permute-done.1.refs_2_), channel_id=1, source_target_pairs={{0,16},{16,0},{1,17},{17,1},{2,18},{18,2},{3,19},{19,3},{4,20},{20... | collective-permute-start | bytes 1881608 | tf_op jit(solution)/shard_map/ppermute | solution.py:232
  42.7 8.3 %collective-permute-start.3 = (bf16[272,560]{1,0:T(8,128)(2,1)S(1)}, bf16[272,560]{1,0:T(8,128)(2,1)S(1)}, u32[]{:S(2)}, u32[]{:S(2)}) collective-permute-start(bf16[272,560]{1,0:T(8,128)(2,1)S(1)} %slice.17), channel_id=1, source_target_pairs={{0,12},{4,0},{8,4},{12,8},{1,13},{5,1},{9,5},{13,9},{2,14},{6,2},{... | collective-permute-start | bytes 913928 | tf_op jit(solution)/shard_map/ppermute | solution.py:232
  45.4 9.7 %collective-permute-start.7 = (bf16[288,560]{1,0:T(8,128)(2,1)S(1)}, bf16[288,560]{1,0:T(8,128)(2,1)S(1)}, u32[]{:S(2)}, u32[]{:S(2)}) collective-permute-start(bf16[288,560]{1,0:T(8,128)(2,1)S(1)} %collective-permute-done.2.refs_3_), channel_id=1, source_target_pairs={{0,16},{16,0},{1,17},{17,1},{2,18},{18,2},{3,19},{19,3},{4,20},{20... | collective-permute-start | bytes 967688 | tf_op jit(solution)/shard_map/ppermute | solution.py:232
  51.0 4.1 %collective-permute-start.8 = (bf16[272,560]{1,0:T(8,128)(2,1)S(1)}, bf16[272,560]{1,0:T(8,128)(2,1)S(1)}, u32[]{:S(2)}, u32[]{:S(2)}) collective-permute-start(bf16[272,560]{1,0:T(8,128)(2,1)S(1)} %collective-permute-done.3.refs_4_), channel_id=1, source_target_pairs={{0,16},{16,0},{1,17},{17,1},{2,18},{18,2},{3,19},{19,3},{4,20},{20... | collective-permute-start | bytes 913928 | tf_op jit(solution)/shard_map/ppermute | solution.py:232
  62.6 4.2 %copy-start.2 = (bf16[560,512]{1,0:T(8,128)(2,1)}, bf16[560,512]{1,0:T(8,128)(2,1)S(1)}, u32[]{:S(2)}) copy-start(bf16[560,512]{1,0:T(8,128)(2,1)S(1)} %get-tuple-element.30.kt) | copy-start | bytes 1720324
  62.6 4.2 %copy-start.4 = (bf16[560,512]{1,0:T(8,128)(2,1)}, bf16[560,512]{1,0:T(8,128)(2,1)S(1)}, u32[]{:S(2)}) copy-start(bf16[560,512]{1,0:T(8,128)(2,1)S(1)} %get-tuple-element.31.vt) | copy-start | bytes 1720324
  62.6 4.2 %copy-start.8 = (bf16[560,128]{1,0:T(8,128)(2,1)}, bf16[560,128]{1,0:T(8,128)(2,1)S(1)}, u32[]{:S(2)}) copy-start(bf16[560,128]{1,0:T(8,128)(2,1)S(1)} %get-tuple-element.17.s0) | copy-start | bytes 430084
  62.6 4.6 %copy-start.13 = (bf16[1,128,2240]{1,2,0:T(8,128)(2,1)S(1)}, bf16[1,128,2240]{1,2,0:T(8,128)(2,1)}, u32[]{:S(2)}) copy-start(bf16[1,128,2240]{1,2,0:T(8,128)(2,1)} %param.7) | copy-start | bytes 1720324
  66.8 48.2 %collective-permute-start.22 = (bf16[1152,512]{1,0:T(8,128)(2,1)}, bf16[1152,512]{1,0:T(8,128)(2,1)S(1)}, u32[]{:S(2)}, u32[]{:S(2)}) collective-permute-start(bf16[1152,512]{1,0:T(8,128)(2,1)} %get-tuple-element.28), channel_id=1, source_target_pairs={{0,16},{16,0},{1,17},{17,1},{2,18},{18,2},{3,19},{19,3},{4,20},{20... | collective-permute-start | bytes 3538952 | tf_op jit(solution)/shard_map/ppermute | solution.py:232
  68.8 40.9 %copy-start.3 = (bf16[560,512]{1,0:T(8,128)(2,1)S(1)}, bf16[560,512]{1,0:T(8,128)(2,1)}, u32[]{:S(2)}) copy-start(bf16[560,512]{1,0:T(8,128)(2,1)} %copy-done.2) | copy-start | bytes 1720324
  68.8 40.9 %copy-start.5 = (bf16[560,512]{1,0:T(8,128)(2,1)S(1)}, bf16[560,512]{1,0:T(8,128)(2,1)}, u32[]{:S(2)}) copy-start(bf16[560,512]{1,0:T(8,128)(2,1)} %copy-done.4) | copy-start | bytes 1720324
  70.2 10.4 %collective-permute-start.16 = (bf16[2,128,560]{2,1,0:T(8,128)(2,1)S(1)}, bf16[2,128,560]{2,1,0:T(8,128)(2,1)S(1)}, u32[]{:S(2)}, u32[]{:S(2)}) collective-permute-start(bf16[2,128,560]{2,1,0:T(8,128)(2,1)S(1)} %get-tuple-element.19), channel_id=1, source_target_pairs={{0,3},{1,0},{2,1},{3,2},{4,7},{5,4},{6,5},{7,6},{8,11},{9,8},{10,9... | collective-permute-start | bytes 860168 | tf_op jit(solution)/shard_map/ppermute | solution.py:232
  70.3 17.7 %collective-permute-start.17 = (bf16[2,128,560]{2,1,0:T(8,128)(2,1)S(1)}, bf16[2,128,560]{2,1,0:T(8,128)(2,1)S(1)}, u32[]{:S(2)}, u32[]{:S(2)}) collective-permute-start(bf16[2,128,560]{2,1,0:T(8,128)(2,1)S(1)} %get-tuple-element.20), channel_id=1, source_target_pairs={{0,2},{1,3},{2,0},{3,1},{4,6},{5,7},{6,4},{7,5},{8,10},{9,11},{10,... | collective-permute-start | bytes 860168 | tf_op jit(solution)/shard_map/ppermute | solution.py:232
  73.3 17.0 %collective-permute-start.18 = (bf16[2,128,560]{2,1,0:T(8,128)(2,1)S(1)}, bf16[2,128,560]{2,1,0:T(8,128)(2,1)S(1)}, u32[]{:S(2)}, u32[]{:S(2)}) collective-permute-start(bf16[2,128,560]{2,1,0:T(8,128)(2,1)S(1)} %get-tuple-element.21), channel_id=1, source_target_pairs={{0,1},{1,2},{2,3},{3,0},{4,5},{5,6},{6,7},{7,4},{8,9},{9,10},{10,1... | collective-permute-start | bytes 860168 | tf_op jit(solution)/shard_map/ppermute | solution.py:232
  74.2 16.1 %collective-permute-start.13 = (bf16[560,128]{1,0:T(8,128)(2,1)}, bf16[560,128]{1,0:T(8,128)(2,1)S(1)}, u32[]{:S(2)}, u32[]{:S(2)}) collective-permute-start(bf16[560,128]{1,0:T(8,128)(2,1)} %copy-done.8), channel_id=1, source_target_pairs={{0,4},{4,8},{8,12},{12,0},{1,5},{5,9},{9,13},{13,1},{2,6},{6,10},{... | collective-permute-start | bytes 430088 | tf_op jit(solution)/shard_map/ppermute | solution.py:232
  80.7 9.6 %collective-permute-start.14 = (bf16[560,128]{1,0:T(8,128)(2,1)}, bf16[560,128]{1,0:T(8,128)(2,1)S(1)}, u32[]{:S(2)}, u32[]{:S(2)}) collective-permute-start(bf16[560,128]{1,0:T(8,128)(2,1)} %copy-done.8), channel_id=1, source_target_pairs={{0,12},{4,0},{8,4},{12,8},{1,13},{5,1},{9,5},{13,9},{2,14},{6,2},{... | collective-permute-start | bytes 430088 | tf_op jit(solution)/shard_map/ppermute | solution.py:232
  88.0 6.0 %collective-permute-start.15 = (bf16[560,128]{1,0:T(8,128)(2,1)}, bf16[560,128]{1,0:T(8,128)(2,1)S(1)}, u32[]{:S(2)}, u32[]{:S(2)}) collective-permute-start(bf16[560,128]{1,0:T(8,128)(2,1)} %copy-done.8), channel_id=1, source_target_pairs={{0,8},{4,12},{8,0},{12,4},{1,9},{5,13},{9,1},{13,5},{2,10},{6,14},... | collective-permute-start | bytes 430088 | tf_op jit(solution)/shard_map/ppermute | solution.py:232
  94.1 0.9 copy-start.9
  99.1 0.7 copy-start.6
  99.8 5.9 %collective-permute-start.23 = (bf16[560,128]{1,0:T(8,128)(2,1)S(1)}, bf16[560,128]{1,0:T(8,128)(2,1)S(1)}, u32[]{:S(2)}, u32[]{:S(2)}) collective-permute-start(bf16[560,128]{1,0:T(8,128)(2,1)S(1)} %get-tuple-element.29.s0), channel_id=1, source_target_pairs={{0,4},{4,8},{8,12},{12,0},{1,5},{5,9},{9,13},{13,1},{2,6},{6,10},{... | collective-permute-start | bytes 430088 | tf_op jit(solution)/shard_map/ppermute | solution.py:232
  101.1 4.6 %collective-permute-start.24 = (bf16[560,128]{1,0:T(8,128)(2,1)S(1)}, bf16[560,128]{1,0:T(8,128)(2,1)S(1)}, u32[]{:S(2)}, u32[]{:S(2)}) collective-permute-start(bf16[560,128]{1,0:T(8,128)(2,1)S(1)} %get-tuple-element.29.s0), channel_id=1, source_target_pairs={{0,12},{4,0},{8,4},{12,8},{1,13},{5,1},{9,5},{13,9},{2,14},{6,2},{... | collective-permute-start | bytes 430088 | tf_op jit(solution)/shard_map/ppermute | solution.py:232
  103.2 6.5 %collective-permute-start.25 = (bf16[560,128]{1,0:T(8,128)(2,1)S(1)}, bf16[560,128]{1,0:T(8,128)(2,1)S(1)}, u32[]{:S(2)}, u32[]{:S(2)}) collective-permute-start(bf16[560,128]{1,0:T(8,128)(2,1)S(1)} %get-tuple-element.29.s0), channel_id=1, source_target_pairs={{0,8},{4,12},{8,0},{12,4},{1,9},{5,13},{9,1},{13,5},{2,10},{6,14},... | collective-permute-start | bytes 430088 | tf_op jit(solution)/shard_map/ppermute | solution.py:232
  110.6 4.4 %collective-permute-start.26 = (bf16[560,512]{1,0:T(8,128)(2,1)S(1)}, bf16[560,512]{1,0:T(8,128)(2,1)S(1)}, u32[]{:S(2)}, u32[]{:S(2)}) collective-permute-start(bf16[560,512]{1,0:T(8,128)(2,1)S(1)} %shard_map.83.d_own), channel_id=1, source_target_pairs={{0,16},{16,0},{1,17},{17,1},{2,18},{18,2},{3,19},{19,3},{4,20},{20... | collective-permute-start | bytes 1720328 | tf_op jit(solution)/shard_map/ppermute | solution.py:232
  118.2 29.1 %all-to-all-start.1 = ((bf16[16,72,560]{2,1,0:T(8,128)(2,1)}), bf16[16,72,560]{2,1,0:T(8,128)(2,1)S(1)}, u32[]{:S(2)}, u32[]{:S(2)}) async-start(bf16[16,72,560]{2,1,0:T(8,128)(2,1)} %bitcast.16), calls=%async_computation.1 | async-start | bytes 2949120 | tf_op jit(solution)/shard_map/all_to_all | solution.py:320
  124.8 24.6 %copy-start.7 = (bf16[128,560]{1,0:T(8,128)(2,1)S(1)}, bf16[128,560]{1,0:T(8,128)(2,1)}, u32[]{:S(2)}) copy-start(bf16[128,560]{1,0:T(8,128)(2,1)} %copy-done.6) | copy-start | bytes 430084
  124.8 24.6 %collective-permute-start.19 = (bf16[128,560]{1,0:T(8,128)(2,1)S(1)}, bf16[128,560]{1,0:T(8,128)(2,1)S(1)}, u32[]{:S(2)}, u32[]{:S(2)}) collective-permute-start(bf16[128,560]{1,0:T(8,128)(2,1)S(1)} %get-tuple-element.23), channel_id=1, source_target_pairs={{0,3},{1,0},{2,1},{3,2},{4,7},{5,4},{6,5},{7,6},{8,11},{9,8},{10,9... | collective-permute-start | bytes 430088 | tf_op jit(solution)/shard_map/ppermute | solution.py:232
  124.8 24.5 %collective-permute-start.20 = (bf16[128,560]{1,0:T(8,128)(2,1)S(1)}, bf16[128,560]{1,0:T(8,128)(2,1)S(1)}, u32[]{:S(2)}, u32[]{:S(2)}) collective-permute-start(bf16[128,560]{1,0:T(8,128)(2,1)S(1)} %get-tuple-element.24), channel_id=1, source_target_pairs={{0,2},{1,3},{2,0},{3,1},{4,6},{5,7},{6,4},{7,5},{8,10},{9,11},{10,... | collective-permute-start | bytes 430088 | tf_op jit(solution)/shard_map/ppermute | solution.py:232
  127.1 22.3 %collective-permute-start.21 = (bf16[128,560]{1,0:T(8,128)(2,1)S(1)}, bf16[128,560]{1,0:T(8,128)(2,1)S(1)}, u32[]{:S(2)}, u32[]{:S(2)}) collective-permute-start(bf16[128,560]{1,0:T(8,128)(2,1)S(1)} %get-tuple-element.25), channel_id=1, source_target_pairs={{0,1},{1,2},{2,3},{3,0},{4,5},{5,6},{6,7},{7,4},{8,9},{9,10},{10,1... | collective-permute-start | bytes 430088 | tf_op jit(solution)/shard_map/ppermute | solution.py:232
  147.4 9.5 %collective-permute-start.27 = (bf16[72,560]{1,0:T(8,128)(2,1)S(1)}, bf16[72,560]{1,0:T(8,128)(2,1)S(1)}, u32[]{:S(2)}, u32[]{:S(2)}) collective-permute-start(bf16[72,560]{1,0:T(8,128)(2,1)S(1)} %shard_map.85), channel_id=1, source_target_pairs={{0,0},{1,32},{2,64},{3,96},{32,1},{33,33},{34,65},{35,97},{64,2},{... | collective-permute-start | bytes 241928 | tf_op jit(solution)/shard_map/ppermute | solution.py:322

commit v2 on v1

v2 whole, which is shorter than its diff:
```python
import jax
import jax.numpy as jnp
from jax import lax
from jax.experimental import pallas as pl
from jax.experimental.pallas import tpu as pltpu
from jax.sharding import Mesh
from jax.sharding import PartitionSpec as P

HEADS = 20
HEAD_DIM = 112
D = 2240
NX = 4
NY = 4
NZ = 4
GH = HEADS // NX
GW = GH * HEAD_DIM
ROWS = 128
TOK = ROWS * NX
SH = D // 16
HALF = SH // 2
PAD = 72
SPLIT = 288
BF = jnp.bfloat16
F32 = jnp.float32
VMEM = pl.BlockSpec(memory_space=pltpu.VMEM)
SMEM = pl.BlockSpec(memory_space=pltpu.SMEM)
ANY = pl.BlockSpec(memory_space=pl.ANY)
HBM = pl.BlockSpec(memory_space=pltpu.HBM)


def params(vmem):
    return pltpu.CompilerParams(vmem_limit_bytes=vmem * 1024 * 1024)


def call(body, out_shape, in_specs, args, scratch=(), flops=0, nbytes=0, name=None, vmem=6):
    return pl.pallas_call(
        body,
        out_shape=out_shape,
        in_specs=in_specs,
        out_specs=jax.tree.map(lambda _: VMEM, out_shape),
        scratch_shapes=list(scratch),
        compiler_params=params(vmem),
        cost_estimate=pl.CostEstimate(flops=flops, bytes_accessed=nbytes, transcendentals=0),
        name=name,
    )(*args)


def nt(a, b):
    return lax.dot_general(a, b, (((1,), (1,)), ((), ())), preferred_element_type=F32)


def tn(a, b):
    return lax.dot_general(a, b, (((0,), (0,)), ((), ())), preferred_element_type=F32)


def nn(a, b):
    return jnp.dot(a, b, preferred_element_type=F32)


def prep_weights(idx, wk, wv, out, buf, sem):
    for c, src in ((0, wk), (1, wv)):

        @pl.when(idx[1] == c)
        def _():
            cp = pltpu.make_async_copy(src, buf, sem)
            cp.start()
            cp.wait()

    for k in range(NX):
        out[k] = buf[:, GW * k : GW * (k + 1)]


def merge_weights(g, full):
    full[...] = jnp.concatenate([g[k].astype(F32) for k in range(NX)], axis=0).T.astype(BF)


def run_copies(pairs, sems):
    copies = [pltpu.make_async_copy(a, b, sems.at[i]) for i, (a, b) in enumerate(pairs)]
    for cp in copies:
        cp.start()
    return copies


def wait_all(copies):
    for cp in copies:
        cp.wait()


def prep_queries(idx, q, ct, o0, o1, o2, o3, sems):
    pairs = []
    for d, out in enumerate((o0, o1, o2, o3)):
        rows = pl.ds(pl.multiple_of(lax.rem(idx[3] + d, NX) * GW, 16), GW)
        pairs += [(q.at[rows], out.at[0]), (ct.at[rows], out.at[1])]
    wait_all(run_copies(pairs, sems))


def live_mask(idx, shift):
    lane = lax.broadcasted_iota(jnp.int32, (1, TOK), 1)
    block = lax.rem(shift + lane // ROWS, NX)
    pos = idx[2] * TOK + block * ROWS + lane % ROWS
    return (pos < idx[4]).astype(F32)


def ones_row(v, row):
    pad = jnp.zeros((15, v.shape[1]), F32)
    return jnp.concatenate([v, row, pad], axis=0)


def project(
    idx, w0, w_prev, w_next, w_lo, w_hi, v0, v_prev, v_next, v_lo, v_hi,
    t0, t1, t3, t2_lo, t2_hi, kt, vt, summ, tbuf, acc,
):
    for i, off in enumerate((0, 3, 1, 2)):
        block = lax.rem(idx[2] + off, NY)
        start = pl.multiple_of(block * GW, 16)
        for d, t in ((0, t0), (1, t1), (3, t3)):
            tbuf[i, :, ROWS * d : ROWS * (d + 1)] = t[pl.ds(start, GW)]
        near = pl.multiple_of(lax.rem(block, 2) * GW, 16)
        for lo, t in ((True, t2_lo), (False, t2_hi)):

            @pl.when((block < 2) == lo)
            def _():
                tbuf[i, :, 2 * ROWS : 3 * ROWS] = t[pl.ds(near, GW)]

    c = idx[1]
    for g, ws in ((c, (w0, w_prev, w_next)), (1 - c, (v0, v_prev, v_next))):
        lo, hi = (w_lo, w_hi) if ws[0] is w0 else (v_lo, v_hi)
        far = jnp.concatenate([lo[...], hi[...]], axis=0)
        total = nn(far, tbuf[3])
        for i, w in enumerate(ws):
            total = total + nn(w[...], tbuf[i])
        acc[g] = total.astype(BF)
    live = live_mask(idx, idx[3])
    one = jnp.ones((1, TOK), F32)
    for h in range(GH):
        s = slice(HEAD_DIM * h, HEAD_DIM * (h + 1))
        keys = jnp.maximum(acc[0, s].astype(F32), 0.0)
        values = acc[1, s]
        kt[s] = keys.astype(BF)
        vt[s] = values
        vh = ones_row(values.astype(F32), one).astype(BF)
        summ[s] = nt((keys * live).astype(BF), vh).astype(BF)


def total_of(parts):
    total = parts[0][...].astype(F32)
    for p in parts[1:]:
        total = total + p[...].astype(F32)
    return total.astype(BF)


def query_side(idx, s0, s1, s2, s3, q0, q1, q2, q3, g0, g1, g2, g3, dsum):
    summ = total_of((s0, s1, s2, s3))
    live = live_mask(idx, idx[3])
    qc = (q0, q1, q2, q3)
    length = idx[4].astype(F32)
    for h in range(GH):
        s = slice(HEAD_DIM * h, HEAD_DIM * (h + 1))
        q = jnp.concatenate([r[0, s].astype(F32) for r in qc], axis=1)
        back = jnp.concatenate([r[1, s].astype(F32) for r in qc], axis=1) * live
        phi = jnp.maximum(q, 0.0)
        phib = phi.astype(BF)
        sh = summ[s]
        numer = tn(sh, phib)
        inv = 1.0 / (numer[HEAD_DIM : HEAD_DIM + 1] + length)
        dnum = back * inv
        dden = -jnp.sum(back * numer[:HEAD_DIM], axis=0, keepdims=True) * inv * inv
        ext = ones_row(dnum, dden).astype(BF)
        grad = jnp.where(q > 0, nn(sh, ext), 0.0).astype(BF)
        for d, g in enumerate((g0, g1, g2, g3)):
            g[s] = grad[:, ROWS * d : ROWS * (d + 1)]
        dsum[s] = nt(phib, ext).astype(BF)


def key_side(idx, s0, s1, s2, s3, kt, vt, dkt):
    summ = total_of((s0, s1, s2, s3))
    live = live_mask(idx, idx[3])
    one = jnp.ones((1, TOK), F32)
    for h in range(GH):
        s = slice(HEAD_DIM * h, HEAD_DIM * (h + 1))
        vh = ones_row(vt[s].astype(F32), one).astype(BF)
        dk = nn(summ[s], vh)
        keep = (kt[s].astype(F32) > 0) & (live > 0)
        dkt[s] = jnp.where(keep, dk, 0.0).astype(BF)


def group_tokens(idx, t0, t1, t3, t2_lo, t2_hi, own, oth, buf):
    for d, t in ((0, t0), (1, t1), (3, t3)):
        buf[:, ROWS * d : ROWS * (d + 1)] = t[...].astype(F32)
    buf[: D // 2, 2 * ROWS : 3 * ROWS] = t2_lo[...].astype(F32)
    buf[D // 2 :, 2 * ROWS : 3 * ROWS] = t2_hi[...].astype(F32)
    zero = jnp.zeros((PAD - HALF, TOK), F32)
    for c in range(2):

        @pl.when(idx[1] == c)
        def _():
            for i in range(16):
                base = SH * i
                for half, dst in ((c, own), (1 - c, oth)):
                    lo = base + HALF * half
                    rows = jnp.concatenate([buf[lo : lo + HALF], zero], axis=0)
                    dst[PAD * i : PAD * (i + 1)] = rows.astype(BF)


def grad_weights(idx, t_own, t_oth, d_own, d_oth, out):
    part = (nt(t_own[...], d_own[...]) + nt(t_oth[...], d_oth[...])).astype(BF)
    for y in range(NY):
        for x in range(NX):
            i = NX * y + x
            z = lax.rem(x - idx[3] + NX, NX)
            out[z * NY + y] = part[PAD * i : PAD * (i + 1)]


def sum_pieces(g, out):
    total = g[0].astype(F32)
    for i in range(1, 16):
        total = total + g[i].astype(F32)
    out[...] = total.astype(BF)


def place_rows(idx, r0, r1, r2, r3, o0, o1, o2, o3, out):
    for c in range(2):
        for k in range(NX):
            for step, (r, o) in enumerate(((r0, o0), (r1, o1), (r2, o2), (r3, o3))):

                @pl.when((idx[1] == c) & (lax.rem(idx[3] - idx[0] + step + NX, NX) == k))
                def _():
                    cols = slice(GW * k, GW * (k + 1))
                    out[HALF * c : HALF * (c + 1), cols] = r[:HALF].astype(F32)
                    out[HALF * (1 - c) : HALF * (2 - c), cols] = o[:HALF].astype(F32)


def place_queries(idx, g0, g1, g2, g3, out):
    for d, src in enumerate((g0, g1, g2, g3)):
        out[pl.ds(pl.multiple_of(lax.rem(idx[3] + d, NX) * GW, 16), GW)] = src[...]


def shift(v, axis, d, n=4):
    return lax.ppermute(v, axis, [(i, (i + d) % n) for i in range(n)])


def sds(shape, dtype=BF):
    return jax.ShapeDtypeStruct(shape, dtype)


def per_device(tokens, queries, cotangent, key_weight, value_weight, clip_len):
    z, c, y, x = (lax.axis_index(a) for a in ("z", "core", "y", "x"))
    idx = jnp.stack([z, c, y, x, clip_len[0]]).astype(jnp.int32)
    t_own, quers, backs = tokens[0].T, queries[0].T, cotangent[0].T

    def swap(v):
        return shift(v, "core", 1, 2)

    def sum_parts(s):
        return [s] + [shift(s, "y", d) for d in (1, 3, 2)]

    pieces = call(
        prep_weights,
        sds((NX, SH, GW)),
        [SMEM, HBM, HBM],
        (idx, key_weight, value_weight),
        scratch=[pltpu.VMEM((SH, D), BF), pltpu.SemaphoreType.DMA],
        vmem=60,
    )
    merged = lax.all_to_all(pieces, "x", 0, 0, tiled=True)
    t_own, _ = lax.optimization_barrier((t_own, pieces))
    qc = call(
        prep_queries,
        [sds((2, GW, ROWS))] * NX,
        [SMEM, ANY, ANY],
        (idx, quers, backs),
        scratch=[pltpu.SemaphoreType.DMA((8,))],
    )
    merged, *qc = lax.optimization_barrier((merged, *qc))
    w_own = call(merge_weights, sds((GW, GW)), [VMEM], (merged,))
    w_prev = shift(w_own, "y", 1)
    w_next = shift(w_own, "y", -1)
    t_prev = shift(t_own, "x", 1)
    t_next = shift(t_own, "x", -1)
    f_lo = shift(w_prev[:SPLIT], "y", 1)
    f_hi = shift(w_next[SPLIT:], "y", -1)
    t_lo = shift(t_prev[: D // 2], "x", 1)
    t_hi = shift(t_next[D // 2 :], "x", -1)
    ts = (t_own, t_next, t_prev, t_lo, t_hi)
    g_own, g_oth = call(
        group_tokens,
        [sds((16 * PAD, TOK))] * 2,
        [SMEM] + [VMEM] * 5,
        (idx, *ts),
        scratch=[pltpu.VMEM((D, TOK), F32)],
        vmem=10,
        nbytes=10_000_000,
    )
    f_lo, f_hi, g_own, g_oth = lax.optimization_barrier((f_lo, f_hi, g_own, g_oth))
    ws = (w_own, w_prev, w_next, f_lo, f_hi)
    kt, vt, summ = call(
        project,
        [sds((GW, TOK)), sds((GW, TOK)), sds((GW, 128))],
        [SMEM] + [VMEM] * 15,
        (idx, *ws, *[swap(w) for w in ws], *ts),
        scratch=[pltpu.VMEM((NY, GW, TOK), BF), pltpu.VMEM((2, GW, TOK), BF)],
        vmem=16,
        flops=4 * TOK * D * GW,
        nbytes=5_000_000,
    )
    summ, *qc = lax.optimization_barrier((summ, *qc))
    parts = sum_parts(summ)
    q_in = [qc[0]] + [shift(qc[NX - d], "x", -d) for d in (1, 2, 3)]
    g_oth = swap(g_oth)

    outs = call(
        query_side,
        [sds((GW, ROWS))] * NX + [sds((GW, 128))],
        [SMEM] + [VMEM] * 8,
        (idx, *parts, *q_in),
        flops=6 * TOK * GW * 128,
        nbytes=4_000_000,
    )
    gq, dsum = outs[:NX], outs[NX]
    parts = sum_parts(dsum)
    g_in = [gq[0]]
    for d in (1, 2, 3):
        g_in.append(shift(gq[NX - d], "x", -d))
    dkt = call(
        key_side,
        sds((GW, TOK)),
        [SMEM] + [VMEM] * 6,
        (idx, *parts, kt, vt),
        flops=2 * TOK * GW * 128,
        nbytes=2_000_000,
    )
    part = call(
        grad_weights,
        sds((16, PAD, GW)),
        [SMEM] + [VMEM] * 4,
        (idx, g_own, g_oth, dkt, swap(dkt)),
        flops=4 * 16 * PAD * TOK * GW,
        nbytes=6_000_000,
    )
    part = lax.all_to_all(part, ("z", "y"), 0, 0, tiled=True)
    grad_q = call(place_queries, sds((D, ROWS)), [SMEM] + [VMEM] * 4, (idx, *g_in))
    part, grad_q = lax.optimization_barrier((part, grad_q))
    rows = call(sum_pieces, sds((PAD, GW)), [VMEM], (part,))
    got = [
        lax.ppermute(
            rows,
            ("z", "x"),
            [
                (z_at * NX + x_at, (z_at + s) % NZ * NX + (x_at + z_at) % NX)
                for z_at in range(NZ)
                for x_at in range(NX)
            ],
        )
        for s in range(NZ)
    ]
    grad_rows = call(
        place_rows, sds((SH, D), F32), [SMEM] + [VMEM] * 8, (idx, *got, *[swap(g) for g in got])
    )
    return grad_q.T[None], grad_rows


def solution(mesh):
    grid = Mesh(mesh.devices.reshape(NZ, 2, NY, NX), ("z", "core", "y", "x"))
    dp, ctx = ("z", "core"), ("y", "x")
    in_specs = (
        P(dp, ctx, None),
        P(dp, ctx, None),
        P(dp, ctx, None),
        P(ctx, None),
        P(ctx, None),
        P(dp),
    )
    out_specs = (P(dp, ctx, None), P(ctx, None))
    return jax.shard_map(
        per_device, mesh=grid, in_specs=in_specs, out_specs=out_specs, check_vma=False
    )
```

time: 175 us -> 143 us (0.82)
  blocking collectives: 16.1 us -> 0 us
  waiting for transfers between devices: 63.5 us -> 50.9 us
  local copies, waits for them, and re-layouts: 11.2 us -> 3.97 us
  starting transfers between devices: 56.4 us -> 63 us
  Pallas kernels: 25.5 us -> 22.6 us
    all_gather x1 -> x0, blocking collectives: 16.1 us -> none  [per_device(): rows = lax.all_gather(rows, ('z', 'core'))]
    all_to_all x2, waiting for transfers between devices: 25.8 us -> 12.5 us  [the longest x1 10.2 us: per_device(): part = lax.all_to_all(part, ('z', 'y'), 0, 0, tiled=True)]
    ppermute x27 -> x31, waiting for transfers between devices: 32.3 us -> 37.2 us  [shift(): return lax.ppermute(v, axis, [(i, (i + d) % n) for i in range(n)])]
    ppermute x1 -> x4, waiting for transfers between devices: 5.39 us -> 1.17 us  [per_device(): lax.ppermute(rows, ('z', 'x'), [(z_at * NX + x_at, (z_at + s) % NZ * NX +...]
    unnamed x32 -> x20, local copies, waits for them, and re-layouts: 7.42 us -> 3.2 us
    ppermute x27 -> x31, starting transfers between devices: 43.7 us -> 47.6 us  [shift(): return lax.ppermute(v, axis, [(i, (i + d) % n) for i in range(n)])]
    ppermute x1 -> x4, starting transfers between devices: 1.92 us -> 5.48 us  [per_device(): lax.ppermute(rows, ('z', 'x'), [(z_at * NX + x_at, (z_at + s) % NZ * NX +...]
    pallas_call x10 -> x11, Pallas kernels: 25.5 us -> 22.6 us  [call(): pl.pallas_call(body, out_shape=out_shape, in_specs=in_specs, out_specs=ja...]
  transfers between devices with their start and end apart: 30 -> 37, of which waited for: 13 -> 19; matrix products, arithmetic and copies ran while one was open for 4% -> 0% of each run, Pallas kernels for 4% -> 9%
where the time goes in v2:
time: 143 us; the launch traced here: 142 us
  starting transfers between devices  63 us (44%)
  waiting for transfers between devices  50.9 us (36%)
  Pallas kernels  22.6 us (16%)
  local copies, waits for them, and re-layouts  3.97 us (3%)
  between operations  1.5 us (1%)
    ppermute x31, starting transfers between devices, shift(): return lax.ppermute(v, axis, [(i, (i + d) % n) for i in range(n)])  47.6 us
    ppermute x31, waiting for transfers between devices, shift(): return lax.ppermute(v, axis, [(i, (i + d) % n) for i in range(n)])  37.2 us
    pallas_call x11, Pallas kernels, call(): pl.pallas_call(body, out_shape=out_shape, in_specs=in_specs, out_specs=ja...  22.6 us
    all_to_all x1, waiting for transfers between devices, per_device(): part = lax.all_to_all(part, ('z', 'y'), 0, 0, tiled=True)  10.2 us
    all_to_all x1, starting transfers between devices, per_device(): part = lax.all_to_all(part, ('z', 'y'), 0, 0, tiled=True)  5.7 us
    ppermute x4, starting transfers between devices, per_device(): lax.ppermute(rows, ('z', 'x'), [(z_at * NX + x_at, (z_at + s) % NZ * NX +...  5.48 us
    all_to_all x1, starting transfers between devices, per_device(): merged = lax.all_to_all(pieces, 'x', 0, 0, tiled=True)  4.22 us
    unnamed x20, local copies, waits for them, and re-layouts  3.2 us
  transfers between devices with their start and end apart: 37, of which 19 were waited for; matrix products, arithmetic and copies ran while one was open for 0% of the time, Pallas kernels for 9%

profile of v2, /device:TPU:7, one launch (start us, length us, event | category | flops | bytes accessed | tf_op | source)
XLA Modules:
  0.0 141.9 jit_solution(12485866645241153046)
XLA Ops:
  1.3 0.7 stack.19.idx
  2.0 3.0 %shard_map.77 = bf16[4,140,560]{2,1,0:T(8,128)(2,1)} custom-call(s32[5]{0:T(128)} %stack.19.idx, bf16[140,2240]{1,0:T(8,128)(2,1)} %wk.1, bf16[140,2240]{1,0:T(8,128)(2,1)} %wv.1), custom_call_target="tpu_custom_call" | custom-call | tf_op jit(solution)/shard_map/pallas_call | solution.py:36
  5.0 4.2 %all-to-all-start = ((bf16[4,140,560]{2,1,0:T(8,128)(2,1)}), bf16[4,140,560]{2,1,0:T(8,128)(2,1)S(1)}, u32[]{:S(2)}, u32[]{:S(2)}) async-start(bf16[4,140,560]{2,1,0:T(8,128)(2,1)} %shard_map.77), calls=%async_computation | async-start | bytes 1474560 | tf_op jit(solution)/shard_map/all_to_all | solution.py:265
  9.2 1.4 %collective-permute-start.4 = (bf16[2240,128]{1,0:T(8,128)(2,1)S(1)}, bf16[2240,128]{1,0:T(8,128)(2,1)S(1)}, u32[]{:S(2)}, u32[]{:S(2)}) collective-permute-start(bf16[2240,128]{1,0:T(8,128)(2,1)S(1)} %bitcast.17), channel_id=1, source_target_pairs={{0,3},{1,0},{2,1},{3,2},{4,7},{5,4},{6,5},{7,6},{8,11},{9,8},{10,9... | collective-permute-start | bytes 1720328 | tf_op jit(solution)/shard_map/ppermute | solution.py:239
  10.7 1.1 copy-done.2
  11.7 2.1 %shard_map.78 = (bf16[2,560,128]{2,1,0:T(8,128)(2,1)S(1)}, bf16[2,560,128]{2,1,0:T(8,128)(2,1)S(1)}, bf16[2,560,128]{2,1,0:T(8,128)(2,1)S(1)}, bf16[2,560,128]{2,1,0:T(8,128)(2,1)S(1)}) custom-call(s32[5]{0:T(128)S(1)} %copy-done.3, bf16[2240,128]{1,0:T(8,128)(2,1)S(1)} %bitcast.20, bf16[2240,128]{1,0:T(8,128)(2,1)S(1)} %bitcast.21), custom_call_target="tpu_custom_call" | custom-call | tf_op jit(solution)/shard_map/pallas_call | solution.py:36
  13.8 0.7 copy-done.4
  14.5 0.7 copy-done.6
  15.3 0.7 copy-done.8
  16.0 2.3 %all-to-all-done.g = bf16[4,140,560]{2,1,0:T(8,128)(2,1)S(1)} async-done(((bf16[4,140,560]{2,1,0:T(8,128)(2,1)}), bf16[4,140,560]{2,1,0:T(8,128)(2,1)S(1)}, u32[]{:S(2)}, u32[]{:S(2)}) %all-to-all-start) | async-done | bytes 627232 | tf_op jit(solution)/shard_map/all_to_all | solution.py:265
  18.3 0.3 shard_map.79.w0
  18.6 1.4 collective-permute-start
  19.9 1.5 %collective-permute-start.2 = (bf16[560,560]{1,0:T(8,128)(2,1)S(1)}, bf16[560,560]{1,0:T(8,128)(2,1)S(1)}, u32[]{:S(2)}, u32[]{:S(2)}) collective-permute-start(bf16[560,560]{1,0:T(8,128)(2,1)S(1)} %shard_map.79.w0), channel_id=1, source_target_pairs={{0,12},{4,0},{8,4},{12,8},{1,13},{5,1},{9,5},{13,9},{2,14},{6,2},{... | collective-permute-start | bytes 1881608 | tf_op jit(solution)/shard_map/ppermute | solution.py:239
  21.5 8.5 %collective-permute-done.5.t3 = bf16[2240,128]{1,0:T(8,128)(2,1)S(1)} collective-permute-done((bf16[2240,128]{1,0:T(8,128)(2,1)S(1)}, bf16[2240,128]{1,0:T(8,128)(2,1)S(1)}, u32[]{:S(2)}, u32[]{:S(2)}) %collective-permute-start.5) | collective-permute-done | bytes 573472 | tf_op jit(solution)/shard_map/ppermute | solution.py:239
  30.0 2.1 %collective-permute-start.6 = (bf16[1120,128]{1,0:T(8,128)(2,1)S(1)}, bf16[1120,128]{1,0:T(8,128)(2,1)S(1)}, u32[]{:S(2)}, u32[]{:S(2)}) collective-permute-start(bf16[1120,128]{1,0:T(8,128)(2,1)S(1)} %slice.18), channel_id=1, source_target_pairs={{0,1},{1,2},{2,3},{3,0},{4,5},{5,6},{6,7},{7,4},{8,9},{9,10},{10,1... | collective-permute-start | bytes 860168 | tf_op jit(solution)/shard_map/ppermute | solution.py:239
  32.2 2.0 %collective-permute-done.w_prev = bf16[560,560]{1,0:T(8,128)(2,1)S(1)} collective-permute-done((bf16[560,560]{1,0:T(8,128)(2,1)S(1)}, bf16[560,560]{1,0:T(8,128)(2,1)S(1)}, u32[]{:S(2)}, u32[]{:S(2)}) %collective-permute-start) | collective-permute-done | bytes 627232 | tf_op jit(solution)/shard_map/ppermute | solution.py:239
  34.4 2.7 %collective-permute-start.3 = (bf16[272,560]{1,0:T(8,128)(2,1)S(1)}, bf16[272,560]{1,0:T(8,128)(2,1)S(1)}, u32[]{:S(2)}, u32[]{:S(2)}) collective-permute-start(bf16[272,560]{1,0:T(8,128)(2,1)S(1)} %slice.17), channel_id=1, source_target_pairs={{0,12},{4,0},{8,4},{12,8},{1,13},{5,1},{9,5},{13,9},{2,14},{6,2},{... | collective-permute-start | bytes 913928 | tf_op jit(solution)/shard_map/ppermute | solution.py:239
  37.1 4.8 %collective-permute-start.9 = (bf16[560,560]{1,0:T(8,128)(2,1)S(1)}, bf16[560,560]{1,0:T(8,128)(2,1)S(1)}, u32[]{:S(2)}, u32[]{:S(2)}) collective-permute-start(bf16[560,560]{1,0:T(8,128)(2,1)S(1)} %shard_map.79.w0), channel_id=1, source_target_pairs={{0,16},{16,0},{1,17},{17,1},{2,18},{18,2},{3,19},{19,3},{4,20},{20... | collective-permute-start | bytes 1881608 | tf_op jit(solution)/shard_map/ppermute | solution.py:239
  41.8 0.8 collective-permute-start.10
  42.7 1.5 %shard_map.80 = (bf16[1152,512]{1,0:T(8,128)(2,1)S(1)}, bf16[1152,512]{1,0:T(8,128)(2,1)S(1)}) custom-call(s32[5]{0:T(128)S(1)} %copy-done.3, bf16[2240,128]{1,0:T(8,128)(2,1)S(1)} %bitcast.18, bf16[2240,128]{1,0:T(8,128)(2,1)S(1)} %collective-permute-done.4.t1, bf16[2240,128]{1,0:T(8,128)(2,1)S(1)} %collective-permute-done.5.t3, ...), custom_call_target="tpu_custom_call" | custom-call | bytes 10000000 | tf_op jit(solution)/shard_map/pallas_call | solution.py:36
  44.2 3.0 %collective-permute-start.12 = (bf16[288,560]{1,0:T(8,128)(2,1)S(1)}, bf16[288,560]{1,0:T(8,128)(2,1)S(1)}, u32[]{:S(2)}, u32[]{:S(2)}) collective-permute-start(bf16[288,560]{1,0:T(8,128)(2,1)S(1)} %collective-permute-done.1.w_lo), channel_id=1, source_target_pairs={{0,16},{16,0},{1,17},{17,1},{2,18},{18,2},{3,19},{19,3},{4,20},{20... | collective-permute-start | bytes 967688 | tf_op jit(solution)/shard_map/ppermute | solution.py:239
  47.3 0.1 collective-permute-start.13
  47.4 0.4 collective-permute-start.8
  47.8 1.3 collective-permute-done.13.v_hi
  49.1 5.1 %shard_map.81 = (bf16[560,512]{1,0:T(8,128)(2,1)S(1)}, bf16[560,512]{1,0:T(8,128)(2,1)S(1)}, bf16[560,128]{1,0:T(8,128)(2,1)S(1)}) custom-call(s32[5]{0:T(128)S(1)} %copy-done.3, bf16[560,560]{1,0:T(8,128)(2,1)S(1)} %shard_map.79.w0, bf16[560,560]{1,0:T(8,128)(2,1)S(1)} %collective-permute-done.w_prev, bf16[560,560]{1,0:T(8,128)(2,1)S(1)} %collective-permute-done.2.w_next, ...), custom_call_target="tpu_custom_call" | custom-call | flops 2569011200 | bytes 5000000 | tf_op jit(solution)/shard_map/pallas_call | solution.py:36
  54.2 2.7 %collective-permute-start.16 = (bf16[560,128]{1,0:T(8,128)(2,1)S(1)}, bf16[560,128]{1,0:T(8,128)(2,1)S(1)}, u32[]{:S(2)}, u32[]{:S(2)}) collective-permute-start(bf16[560,128]{1,0:T(8,128)(2,1)S(1)} %get-tuple-element.50.s0), channel_id=1, source_target_pairs={{0,8},{4,12},{8,0},{12,4},{1,9},{5,13},{9,1},{13,5},{2,10},{6,14},... | collective-permute-start | bytes 430088 | tf_op jit(solution)/shard_map/ppermute | solution.py:239
  56.9 1.1 collective-permute-start.15
  58.0 2.7 %collective-permute-start.18 = (bf16[2,560,128]{2,1,0:T(8,128)(2,1)S(1)}, bf16[2,560,128]{2,1,0:T(8,128)(2,1)S(1)}, u32[]{:S(2)}, u32[]{:S(2)}) collective-permute-start(bf16[2,560,128]{2,1,0:T(8,128)(2,1)S(1)} %copy-done.7), channel_id=1, source_target_pairs={{0,2},{1,3},{2,0},{3,1},{4,6},{5,7},{6,4},{7,5},{8,10},{9,11},{10,... | collective-permute-start | bytes 860168 | tf_op jit(solution)/shard_map/ppermute | solution.py:239
  60.8 1.8 %collective-permute-start.19 = (bf16[2,560,128]{2,1,0:T(8,128)(2,1)S(1)}, bf16[2,560,128]{2,1,0:T(8,128)(2,1)S(1)}, u32[]{:S(2)}, u32[]{:S(2)}) collective-permute-start(bf16[2,560,128]{2,1,0:T(8,128)(2,1)S(1)} %copy-done.5), channel_id=1, source_target_pairs={{0,1},{1,2},{2,3},{3,0},{4,5},{5,6},{6,7},{7,4},{8,9},{9,10},{10,1... | collective-permute-start | bytes 860168 | tf_op jit(solution)/shard_map/ppermute | solution.py:239
  62.5 1.9 %collective-permute-done.15.s2 = bf16[560,128]{1,0:T(8,128)(2,1)S(1)} collective-permute-done((bf16[560,128]{1,0:T(8,128)(2,1)S(1)}, bf16[560,128]{1,0:T(8,128)(2,1)S(1)}, u32[]{:S(2)}, u32[]{:S(2)}) %collective-permute-start.15) | collective-permute-done | bytes 143392 | tf_op jit(solution)/shard_map/ppermute | solution.py:239
  64.4 1.5 %collective-permute-start.14 = (bf16[560,128]{1,0:T(8,128)(2,1)S(1)}, bf16[560,128]{1,0:T(8,128)(2,1)S(1)}, u32[]{:S(2)}, u32[]{:S(2)}) collective-permute-start(bf16[560,128]{1,0:T(8,128)(2,1)S(1)} %get-tuple-element.50.s0), channel_id=1, source_target_pairs={{0,4},{4,8},{8,12},{12,0},{1,5},{5,9},{9,13},{13,1},{2,6},{6,10},{... | collective-permute-start | bytes 430088 | tf_op jit(solution)/shard_map/ppermute | solution.py:239
  65.9 4.6 %collective-permute-done.14.s1 = bf16[560,128]{1,0:T(8,128)(2,1)S(1)} collective-permute-done((bf16[560,128]{1,0:T(8,128)(2,1)S(1)}, bf16[560,128]{1,0:T(8,128)(2,1)S(1)}, u32[]{:S(2)}, u32[]{:S(2)}) %collective-permute-start.14) | collective-permute-done | bytes 143392 | tf_op jit(solution)/shard_map/ppermute | solution.py:239
  70.5 2.3 %collective-permute-done.18.q2 = bf16[2,560,128]{2,1,0:T(8,128)(2,1)S(1)} collective-permute-done((bf16[2,560,128]{2,1,0:T(8,128)(2,1)S(1)}, bf16[2,560,128]{2,1,0:T(8,128)(2,1)S(1)}, u32[]{:S(2)}, u32[]{:S(2)}) %collective-permute-start.18) | collective-permute-done | bytes 286752 | tf_op jit(solution)/shard_map/ppermute | solution.py:239
  72.8 0.9 collective-permute-done.19.q3
  73.7 2.0 %shard_map.82 = (bf16[560,128]{1,0:T(8,128)(2,1)S(1)}, bf16[560,128]{1,0:T(8,128)(2,1)S(1)}, bf16[560,128]{1,0:T(8,128)(2,1)S(1)}, bf16[560,128]{1,0:T(8,128)(2,1)S(1)}, bf16[560,128]{1,0:T(8,128)(2,1)S(1)}) custom-call(s32[5]{0:T(128)S(1)} %copy-done.3, bf16[560,128]{1,0:T(8,128)(2,1)S(1)} %get-tuple-element.50.s0, ...), custom_call_target="tpu_custom_call" | custom-call | flops 220200960 | bytes 4000000 | tf_op jit(solution)/shard_map/pallas_call | solution.py:36
  75.7 1.6 %collective-permute-start.22 = (bf16[560,128]{1,0:T(8,128)(2,1)S(1)}, bf16[560,128]{1,0:T(8,128)(2,1)S(1)}, u32[]{:S(2)}, u32[]{:S(2)}) collective-permute-start(bf16[560,128]{1,0:T(8,128)(2,1)S(1)} %get-tuple-element.55.s0), channel_id=1, source_target_pairs={{0,8},{4,12},{8,0},{12,4},{1,9},{5,13},{9,1},{13,5},{2,10},{6,14},... | collective-permute-start | bytes 430088 | tf_op jit(solution)/shard_map/ppermute | solution.py:239
  77.3 1.1 collective-permute-start.21
  78.4 0.3 collective-permute-start.20
  78.8 2.4 %collective-permute-done.22.s3 = bf16[560,128]{1,0:T(8,128)(2,1)S(1)} collective-permute-done((bf16[560,128]{1,0:T(8,128)(2,1)S(1)}, bf16[560,128]{1,0:T(8,128)(2,1)S(1)}, u32[]{:S(2)}, u32[]{:S(2)}) %collective-permute-start.22) | collective-permute-done | bytes 143392 | tf_op jit(solution)/shard_map/ppermute | solution.py:239
  81.2 1.6 %collective-permute-done.21.s2 = bf16[560,128]{1,0:T(8,128)(2,1)S(1)} collective-permute-done((bf16[560,128]{1,0:T(8,128)(2,1)S(1)}, bf16[560,128]{1,0:T(8,128)(2,1)S(1)}, u32[]{:S(2)}, u32[]{:S(2)}) %collective-permute-start.21) | collective-permute-done | bytes 143392 | tf_op jit(solution)/shard_map/ppermute | solution.py:239
  82.8 2.6 %collective-permute-done.20.s1 = bf16[560,128]{1,0:T(8,128)(2,1)S(1)} collective-permute-done((bf16[560,128]{1,0:T(8,128)(2,1)S(1)}, bf16[560,128]{1,0:T(8,128)(2,1)S(1)}, u32[]{:S(2)}, u32[]{:S(2)}) %collective-permute-start.20) | collective-permute-done | bytes 143392 | tf_op jit(solution)/shard_map/ppermute | solution.py:239
  85.4 0.9 shard_map.83.d_own
  86.3 1.8 %collective-permute-start.23 = (bf16[560,512]{1,0:T(8,128)(2,1)S(1)}, bf16[560,512]{1,0:T(8,128)(2,1)S(1)}, u32[]{:S(2)}, u32[]{:S(2)}) collective-permute-start(bf16[560,512]{1,0:T(8,128)(2,1)S(1)} %shard_map.83.d_own), channel_id=1, source_target_pairs={{0,16},{16,0},{1,17},{17,1},{2,18},{18,2},{3,19},{19,3},{4,20},{20... | collective-permute-start | bytes 1720328 | tf_op jit(solution)/shard_map/ppermute | solution.py:239
  88.2 1.6 %collective-permute-done.23.d_oth = bf16[560,512]{1,0:T(8,128)(2,1)S(1)} collective-permute-done((bf16[560,512]{1,0:T(8,128)(2,1)S(1)}, bf16[560,512]{1,0:T(8,128)(2,1)S(1)}, u32[]{:S(2)}, u32[]{:S(2)}) %collective-permute-start.23) | collective-permute-done | bytes 573472 | tf_op jit(solution)/shard_map/ppermute | solution.py:239
  89.8 3.7 %shard_map.84 = bf16[16,72,560]{2,1,0:T(8,128)(2,1)} custom-call(s32[5]{0:T(128)S(1)} %copy-done.3, bf16[1152,512]{1,0:T(8,128)(2,1)S(1)} %get-tuple-element.41.t_own, bf16[1152,512]{1,0:T(8,128)(2,1)S(1)} %collective-permute-done.8.t_oth, bf16[560,512]{1,0:T(8,128)(2,1)S(1)} %shard_map.83.d_own, bf16[560,512]{1,0:T(8,128)(2,1)S(1)} %collective-permute-done.23.d_oth), custom_call_target="tpu_custom_call" | custom-call | flops 1321205760 | bytes 6000000 | tf_op jit(solution)/shard_map/pallas_call | solution.py:36
  93.5 5.7 %all-to-all-start.1 = ((bf16[16,72,560]{2,1,0:T(8,128)(2,1)}), bf16[16,72,560]{2,1,0:T(8,128)(2,1)S(1)}, u32[]{:S(2)}, u32[]{:S(2)}) async-start(bf16[16,72,560]{2,1,0:T(8,128)(2,1)} %shard_map.84), calls=%async_computation.1 | async-start | bytes 2949120 | tf_op jit(solution)/shard_map/all_to_all | solution.py:340
  99.2 2.3 %collective-permute-start.24 = (bf16[560,128]{1,0:T(8,128)(2,1)S(1)}, bf16[560,128]{1,0:T(8,128)(2,1)S(1)}, u32[]{:S(2)}, u32[]{:S(2)}) collective-permute-start(bf16[560,128]{1,0:T(8,128)(2,1)S(1)} %get-tuple-element.59), channel_id=1, source_target_pairs={{0,3},{1,0},{2,1},{3,2},{4,7},{5,4},{6,5},{7,6},{8,11},{9,8},{10,9... | collective-permute-start | bytes 430088 | tf_op jit(solution)/shard_map/ppermute | solution.py:239
  101.5 2.4 %collective-permute-start.25 = (bf16[560,128]{1,0:T(8,128)(2,1)S(1)}, bf16[560,128]{1,0:T(8,128)(2,1)S(1)}, u32[]{:S(2)}, u32[]{:S(2)}) collective-permute-start(bf16[560,128]{1,0:T(8,128)(2,1)S(1)} %get-tuple-element.60), channel_id=1, source_target_pairs={{0,2},{1,3},{2,0},{3,1},{4,6},{5,7},{6,4},{7,5},{8,10},{9,11},{10,... | collective-permute-start | bytes 430088 | tf_op jit(solution)/shard_map/ppermute | solution.py:239
  104.0 2.2 %collective-permute-done.24.g1 = bf16[560,128]{1,0:T(8,128)(2,1)S(1)} collective-permute-done((bf16[560,128]{1,0:T(8,128)(2,1)S(1)}, bf16[560,128]{1,0:T(8,128)(2,1)S(1)}, u32[]{:S(2)}, u32[]{:S(2)}) %collective-permute-start.24) | collective-permute-done | bytes 143392 | tf_op jit(solution)/shard_map/ppermute | solution.py:239
  106.2 3.9 %collective-permute-done.25.g2 = bf16[560,128]{1,0:T(8,128)(2,1)S(1)} collective-permute-done((bf16[560,128]{1,0:T(8,128)(2,1)S(1)}, bf16[560,128]{1,0:T(8,128)(2,1)S(1)}, u32[]{:S(2)}, u32[]{:S(2)}) %collective-permute-start.25) | collective-permute-done | bytes 143392 | tf_op jit(solution)/shard_map/ppermute | solution.py:239
  110.1 1.4 shard_map.85
  111.5 10.2 %all-to-all-done.1.g = bf16[16,72,560]{2,1,0:T(8,128)(2,1)S(1)} async-done(((bf16[16,72,560]{2,1,0:T(8,128)(2,1)}), bf16[16,72,560]{2,1,0:T(8,128)(2,1)S(1)}, u32[]{:S(2)}, u32[]{:S(2)}) %all-to-all-start.1) | async-done | bytes 1290272 | tf_op jit(solution)/shard_map/all_to_all | solution.py:340
  121.7 0.2 shard_map.86
  121.9 1.0 collective-permute-start.30
  122.9 2.2 %collective-permute-start.29 = (bf16[72,560]{1,0:T(8,128)(2,1)S(1)}, bf16[72,560]{1,0:T(8,128)(2,1)S(1)}, u32[]{:S(2)}, u32[]{:S(2)}) collective-permute-start(bf16[72,560]{1,0:T(8,128)(2,1)S(1)} %shard_map.86), channel_id=1, source_target_pairs={{0,64},{1,65},{2,66},{3,67},{32,97},{33,98},{34,99},{35,96},{64,2}... | collective-permute-start | bytes 241928 | tf_op jit(solution)/shard_map/ppermute | solution.py:345
  125.1 1.6 %collective-permute-start.28 = (bf16[72,560]{1,0:T(8,128)(2,1)S(1)}, bf16[72,560]{1,0:T(8,128)(2,1)S(1)}, u32[]{:S(2)}, u32[]{:S(2)}) collective-permute-start(bf16[72,560]{1,0:T(8,128)(2,1)S(1)} %shard_map.86), channel_id=1, source_target_pairs={{0,32},{1,33},{2,34},{3,35},{32,65},{33,66},{34,67},{35,64},{64,98... | collective-permute-start | bytes 241928 | tf_op jit(solution)/shard_map/ppermute | solution.py:345
  126.7 0.7 collective-permute-start.27
  127.4 2.7 %collective-permute-start.34 = (bf16[72,560]{1,0:T(8,128)(2,1)S(1)}, bf16[72,560]{1,0:T(8,128)(2,1)S(1)}, u32[]{:S(2)}, u32[]{:S(2)}) collective-permute-start(bf16[72,560]{1,0:T(8,128)(2,1)S(1)} %collective-permute-done.30.r3), channel_id=1, source_target_pairs={{0,16},{16,0},{1,17},{17,1},{2,18},{18,2},{3,19},{19,3},{4,20},{20... | collective-permute-start | bytes 241928 | tf_op jit(solution)/shard_map/ppermute | solution.py:239
  130.1 1.1 collective-permute-done.29.r2
  131.2 3.0 %collective-permute-start.33 = (bf16[72,560]{1,0:T(8,128)(2,1)S(1)}, bf16[72,560]{1,0:T(8,128)(2,1)S(1)}, u32[]{:S(2)}, u32[]{:S(2)}) collective-permute-start(bf16[72,560]{1,0:T(8,128)(2,1)S(1)} %collective-permute-done.29.r2), channel_id=1, source_target_pairs={{0,16},{16,0},{1,17},{17,1},{2,18},{18,2},{3,19},{19,3},{4,20},{20... | collective-permute-start | bytes 241928 | tf_op jit(solution)/shard_map/ppermute | solution.py:239
  134.2 4.1 %collective-permute-start.32 = (bf16[72,560]{1,0:T(8,128)(2,1)S(1)}, bf16[72,560]{1,0:T(8,128)(2,1)S(1)}, u32[]{:S(2)}, u32[]{:S(2)}) collective-permute-start(bf16[72,560]{1,0:T(8,128)(2,1)S(1)} %collective-permute-done.28.r1), channel_id=1, source_target_pairs={{0,16},{16,0},{1,17},{17,1},{2,18},{18,2},{3,19},{19,3},{4,20},{20... | collective-permute-start | bytes 241928 | tf_op jit(solution)/shard_map/ppermute | solution.py:239
  138.3 0.9 collective-permute-done.32.o1
  139.2 0.4 collective-permute-done.31.o0
  139.6 2.4 %shard_map.87 = f32[140,2240]{1,0:T(8,128)} custom-call(s32[5]{0:T(128)S(1)} %copy-done.3, bf16[72,560]{1,0:T(8,128)(2,1)S(1)} %collective-permute-done.27.r0, bf16[72,560]{1,0:T(8,128)(2,1)S(1)} %collective-permute-done.28.r1, bf16[72,560]{1,0:T(8,128)(2,1)S(1)} %collective-permute-done.29.r2, bf16[72,560]{1,0:T(8,128)(2,1)S(1)} %collective-permute-done.30.r3, ...), custom_call_target="tpu_custom_call" | custom-call | tf_op jit(solution)/shard_map/pallas_call | solution.py:36
  (46 shorter events, 0.6 us)
Async XLA Ops:
  1.9 7.2 %copy-start = (bf16[1,128,2240]{1,2,0:T(8,128)(2,1)S(1)}, bf16[1,128,2240]{1,2,0:T(8,128)(2,1)}, u32[]{:S(2)}) copy-start(bf16[1,128,2240]{1,2,0:T(8,128)(2,1)} %param.6) | copy-start | bytes 1720324
  1.9 8.7 %copy-start.1 = (bf16[1,128,2240]{1,2,0:T(8,128)(2,1)S(1)}, bf16[1,128,2240]{1,2,0:T(8,128)(2,1)}, u32[]{:S(2)}) copy-start(bf16[1,128,2240]{1,2,0:T(8,128)(2,1)} %param.7) | copy-start | bytes 1720324
  1.9 8.7 %copy-start.3 = (s32[5]{0:T(128)S(1)}, s32[5]{0:T(128)}, u32[]{:S(2)}) copy-start(s32[5]{0:T(128)} %stack.19.idx) | copy-start | bytes 64
  5.0 13.3 %all-to-all-start = ((bf16[4,140,560]{2,1,0:T(8,128)(2,1)}), bf16[4,140,560]{2,1,0:T(8,128)(2,1)S(1)}, u32[]{:S(2)}, u32[]{:S(2)}) async-start(bf16[4,140,560]{2,1,0:T(8,128)(2,1)} %shard_map.77), calls=%async_computation | async-start | bytes 1474560 | tf_op jit(solution)/shard_map/all_to_all | solution.py:265
  9.2 20.8 %collective-permute-start.5 = (bf16[2240,128]{1,0:T(8,128)(2,1)S(1)}, bf16[2240,128]{1,0:T(8,128)(2,1)S(1)}, u32[]{:S(2)}, u32[]{:S(2)}) collective-permute-start(bf16[2240,128]{1,0:T(8,128)(2,1)S(1)} %bitcast.16), channel_id=1, source_target_pairs={{0,1},{1,2},{2,3},{3,0},{4,5},{5,6},{6,7},{7,4},{8,9},{9,10},{10,1... | collective-permute-start | bytes 1720328 | tf_op jit(solution)/shard_map/ppermute | solution.py:239
  9.2 22.9 %collective-permute-start.4 = (bf16[2240,128]{1,0:T(8,128)(2,1)S(1)}, bf16[2240,128]{1,0:T(8,128)(2,1)S(1)}, u32[]{:S(2)}, u32[]{:S(2)}) collective-permute-start(bf16[2240,128]{1,0:T(8,128)(2,1)S(1)} %bitcast.17), channel_id=1, source_target_pairs={{0,3},{1,0},{2,1},{3,2},{4,7},{5,4},{6,5},{7,6},{8,11},{9,8},{10,9... | collective-permute-start | bytes 1720328 | tf_op jit(solution)/shard_map/ppermute | solution.py:239
  10.7 1.1 copy-start.2
  13.8 0.7 copy-start.4
  14.5 0.7 copy-start.6
  15.3 0.7 copy-start.8
  18.6 15.6 %collective-permute-start = (bf16[560,560]{1,0:T(8,128)(2,1)S(1)}, bf16[560,560]{1,0:T(8,128)(2,1)S(1)}, u32[]{:S(2)}, u32[]{:S(2)}) collective-permute-start(bf16[560,560]{1,0:T(8,128)(2,1)S(1)} %shard_map.79.w0), channel_id=1, source_target_pairs={{0,4},{4,8},{8,12},{12,0},{1,5},{5,9},{9,13},{13,1},{2,6},{6,10},{... | collective-permute-start | bytes 1881608 | tf_op jit(solution)/shard_map/ppermute | solution.py:239
  19.9 14.4 %collective-permute-start.2 = (bf16[560,560]{1,0:T(8,128)(2,1)S(1)}, bf16[560,560]{1,0:T(8,128)(2,1)S(1)}, u32[]{:S(2)}, u32[]{:S(2)}) collective-permute-start(bf16[560,560]{1,0:T(8,128)(2,1)S(1)} %shard_map.79.w0), channel_id=1, source_target_pairs={{0,12},{4,0},{8,4},{12,8},{1,13},{5,1},{9,5},{13,9},{2,14},{6,2},{... | collective-permute-start | bytes 1881608 | tf_op jit(solution)/shard_map/ppermute | solution.py:239
  30.0 11.8 %collective-permute-start.6 = (bf16[1120,128]{1,0:T(8,128)(2,1)S(1)}, bf16[1120,128]{1,0:T(8,128)(2,1)S(1)}, u32[]{:S(2)}, u32[]{:S(2)}) collective-permute-start(bf16[1120,128]{1,0:T(8,128)(2,1)S(1)} %slice.18), channel_id=1, source_target_pairs={{0,1},{1,2},{2,3},{3,0},{4,5},{5,6},{6,7},{7,4},{8,9},{9,10},{10,1... | collective-permute-start | bytes 860168 | tf_op jit(solution)/shard_map/ppermute | solution.py:239
  32.1 9.7 %collective-permute-start.7 = (bf16[1120,128]{1,0:T(8,128)(2,1)S(1)}, bf16[1120,128]{1,0:T(8,128)(2,1)S(1)}, u32[]{:S(2)}, u32[]{:S(2)}) collective-permute-start(bf16[1120,128]{1,0:T(8,128)(2,1)S(1)} %slice.19), channel_id=1, source_target_pairs={{0,3},{1,0},{2,1},{3,2},{4,7},{5,4},{6,5},{7,6},{8,11},{9,8},{10,9... | collective-permute-start | bytes 860168 | tf_op jit(solution)/shard_map/ppermute | solution.py:239
  34.2 9.9 %collective-permute-start.1 = (bf16[288,560]{1,0:T(8,128)(2,1)S(1)}, bf16[288,560]{1,0:T(8,128)(2,1)S(1)}, u32[]{:S(2)}, u32[]{:S(2)}) collective-permute-start(bf16[288,560]{1,0:T(8,128)(2,1)S(1)} %slice.16), channel_id=1, source_target_pairs={{0,4},{4,8},{8,12},{12,0},{1,5},{5,9},{9,13},{13,1},{2,6},{6,10},{... | collective-permute-start | bytes 967688 | tf_op jit(solution)/shard_map/ppermute | solution.py:239
  34.4 9.8 %collective-permute-start.3 = (bf16[272,560]{1,0:T(8,128)(2,1)S(1)}, bf16[272,560]{1,0:T(8,128)(2,1)S(1)}, u32[]{:S(2)}, u32[]{:S(2)}) collective-permute-start(bf16[272,560]{1,0:T(8,128)(2,1)S(1)} %slice.17), channel_id=1, source_target_pairs={{0,12},{4,0},{8,4},{12,8},{1,13},{5,1},{9,5},{13,9},{2,14},{6,2},{... | collective-permute-start | bytes 913928 | tf_op jit(solution)/shard_map/ppermute | solution.py:239
  37.1 10.3 %collective-permute-start.9 = (bf16[560,560]{1,0:T(8,128)(2,1)S(1)}, bf16[560,560]{1,0:T(8,128)(2,1)S(1)}, u32[]{:S(2)}, u32[]{:S(2)}) collective-permute-start(bf16[560,560]{1,0:T(8,128)(2,1)S(1)} %shard_map.79.w0), channel_id=1, source_target_pairs={{0,16},{16,0},{1,17},{17,1},{2,18},{18,2},{3,19},{19,3},{4,20},{20... | collective-permute-start | bytes 1881608 | tf_op jit(solution)/shard_map/ppermute | solution.py:239
  41.8 5.9 %collective-permute-start.11 = (bf16[560,560]{1,0:T(8,128)(2,1)S(1)}, bf16[560,560]{1,0:T(8,128)(2,1)S(1)}, u32[]{:S(2)}, u32[]{:S(2)}) collective-permute-start(bf16[560,560]{1,0:T(8,128)(2,1)S(1)} %collective-permute-done.2.w_next), channel_id=1, source_target_pairs={{0,16},{16,0},{1,17},{17,1},{2,18},{18,2},{3,19},{19,3},{4,20},{20... | collective-permute-start | bytes 1881608 | tf_op jit(solution)/shard_map/ppermute | solution.py:239
  41.8 5.9 %collective-permute-start.10 = (bf16[560,560]{1,0:T(8,128)(2,1)S(1)}, bf16[560,560]{1,0:T(8,128)(2,1)S(1)}, u32[]{:S(2)}, u32[]{:S(2)}) collective-permute-start(bf16[560,560]{1,0:T(8,128)(2,1)S(1)} %collective-permute-done.w_prev), channel_id=1, source_target_pairs={{0,16},{16,0},{1,17},{17,1},{2,18},{18,2},{3,19},{19,3},{4,20},{20... | collective-permute-start | bytes 1881608 | tf_op jit(solution)/shard_map/ppermute | solution.py:239
  44.2 13.8 %copy-start.9 = (bf16[2,560,128]{2,1,0:T(8,128)(2,1)S(1)}, bf16[2,560,128]{2,1,0:T(8,128)(2,1)}, u32[]{:S(2)}) copy-start(bf16[2,560,128]{2,1,0:T(8,128)(2,1)} %copy-done.8) | copy-start | bytes 860164
  44.2 13.8 %copy-start.7 = (bf16[2,560,128]{2,1,0:T(8,128)(2,1)S(1)}, bf16[2,560,128]{2,1,0:T(8,128)(2,1)}, u32[]{:S(2)}) copy-start(bf16[2,560,128]{2,1,0:T(8,128)(2,1)} %copy-done.6) | copy-start | bytes 860164
  44.2 16.6 %copy-start.5 = (bf16[2,560,128]{2,1,0:T(8,128)(2,1)S(1)}, bf16[2,560,128]{2,1,0:T(8,128)(2,1)}, u32[]{:S(2)}) copy-start(bf16[2,560,128]{2,1,0:T(8,128)(2,1)} %copy-done.4) | copy-start | bytes 860164
  44.2 4.8 %collective-permute-start.12 = (bf16[288,560]{1,0:T(8,128)(2,1)S(1)}, bf16[288,560]{1,0:T(8,128)(2,1)S(1)}, u32[]{:S(2)}, u32[]{:S(2)}) collective-permute-start(bf16[288,560]{1,0:T(8,128)(2,1)S(1)} %collective-permute-done.1.w_lo), channel_id=1, source_target_pairs={{0,16},{16,0},{1,17},{17,1},{2,18},{18,2},{3,19},{19,3},{4,20},{20... | collective-permute-start | bytes 967688 | tf_op jit(solution)/shard_map/ppermute | solution.py:239
  47.3 1.8 %collective-permute-start.13 = (bf16[272,560]{1,0:T(8,128)(2,1)S(1)}, bf16[272,560]{1,0:T(8,128)(2,1)S(1)}, u32[]{:S(2)}, u32[]{:S(2)}) collective-permute-start(bf16[272,560]{1,0:T(8,128)(2,1)S(1)} %collective-permute-done.3.w_hi), channel_id=1, source_target_pairs={{0,16},{16,0},{1,17},{17,1},{2,18},{18,2},{3,19},{19,3},{4,20},{20... | collective-permute-start | bytes 913928 | tf_op jit(solution)/shard_map/ppermute | solution.py:239
  47.4 40.8 %collective-permute-start.8 = (bf16[1152,512]{1,0:T(8,128)(2,1)S(1)}, bf16[1152,512]{1,0:T(8,128)(2,1)S(1)}, u32[]{:S(2)}, u32[]{:S(2)}) collective-permute-start(bf16[1152,512]{1,0:T(8,128)(2,1)S(1)} %get-tuple-element.42), channel_id=1, source_target_pairs={{0,16},{16,0},{1,17},{17,1},{2,18},{18,2},{3,19},{19,3},{4,20},{20... | collective-permute-start | bytes 3538952 | tf_op jit(solution)/shard_map/ppermute | solution.py:239
  54.2 6.6 %collective-permute-start.16 = (bf16[560,128]{1,0:T(8,128)(2,1)S(1)}, bf16[560,128]{1,0:T(8,128)(2,1)S(1)}, u32[]{:S(2)}, u32[]{:S(2)}) collective-permute-start(bf16[560,128]{1,0:T(8,128)(2,1)S(1)} %get-tuple-element.50.s0), channel_id=1, source_target_pairs={{0,8},{4,12},{8,0},{12,4},{1,9},{5,13},{9,1},{13,5},{2,10},{6,14},... | collective-permute-start | bytes 430088 | tf_op jit(solution)/shard_map/ppermute | solution.py:239
  56.9 7.5 %collective-permute-start.15 = (bf16[560,128]{1,0:T(8,128)(2,1)S(1)}, bf16[560,128]{1,0:T(8,128)(2,1)S(1)}, u32[]{:S(2)}, u32[]{:S(2)}) collective-permute-start(bf16[560,128]{1,0:T(8,128)(2,1)S(1)} %get-tuple-element.50.s0), channel_id=1, source_target_pairs={{0,12},{4,0},{8,4},{12,8},{1,13},{5,1},{9,5},{13,9},{2,14},{6,2},{... | collective-permute-start | bytes 430088 | tf_op jit(solution)/shard_map/ppermute | solution.py:239
  58.0 12.5 %collective-permute-start.17 = (bf16[2,560,128]{2,1,0:T(8,128)(2,1)S(1)}, bf16[2,560,128]{2,1,0:T(8,128)(2,1)S(1)}, u32[]{:S(2)}, u32[]{:S(2)}) collective-permute-start(bf16[2,560,128]{2,1,0:T(8,128)(2,1)S(1)} %copy-done.9), channel_id=1, source_target_pairs={{0,3},{1,0},{2,1},{3,2},{4,7},{5,4},{6,5},{7,6},{8,11},{9,8},{10,9... | collective-permute-start | bytes 860168 | tf_op jit(solution)/shard_map/ppermute | solution.py:239
  58.0 14.8 %collective-permute-start.18 = (bf16[2,560,128]{2,1,0:T(8,128)(2,1)S(1)}, bf16[2,560,128]{2,1,0:T(8,128)(2,1)S(1)}, u32[]{:S(2)}, u32[]{:S(2)}) collective-permute-start(bf16[2,560,128]{2,1,0:T(8,128)(2,1)S(1)} %copy-done.7), channel_id=1, source_target_pairs={{0,2},{1,3},{2,0},{3,1},{4,6},{5,7},{6,4},{7,5},{8,10},{9,11},{10,... | collective-permute-start | bytes 860168 | tf_op jit(solution)/shard_map/ppermute | solution.py:239
  60.8 12.9 %collective-permute-start.19 = (bf16[2,560,128]{2,1,0:T(8,128)(2,1)S(1)}, bf16[2,560,128]{2,1,0:T(8,128)(2,1)S(1)}, u32[]{:S(2)}, u32[]{:S(2)}) collective-permute-start(bf16[2,560,128]{2,1,0:T(8,128)(2,1)S(1)} %copy-done.5), channel_id=1, source_target_pairs={{0,1},{1,2},{2,3},{3,0},{4,5},{5,6},{6,7},{7,4},{8,9},{9,10},{10,1... | collective-permute-start | bytes 860168 | tf_op jit(solution)/shard_map/ppermute | solution.py:239
  64.4 6.1 %collective-permute-start.14 = (bf16[560,128]{1,0:T(8,128)(2,1)S(1)}, bf16[560,128]{1,0:T(8,128)(2,1)S(1)}, u32[]{:S(2)}, u32[]{:S(2)}) collective-permute-start(bf16[560,128]{1,0:T(8,128)(2,1)S(1)} %get-tuple-element.50.s0), channel_id=1, source_target_pairs={{0,4},{4,8},{8,12},{12,0},{1,5},{5,9},{9,13},{13,1},{2,6},{6,10},{... | collective-permute-start | bytes 430088 | tf_op jit(solution)/shard_map/ppermute | solution.py:239
  75.7 5.5 %collective-permute-start.22 = (bf16[560,128]{1,0:T(8,128)(2,1)S(1)}, bf16[560,128]{1,0:T(8,128)(2,1)S(1)}, u32[]{:S(2)}, u32[]{:S(2)}) collective-permute-start(bf16[560,128]{1,0:T(8,128)(2,1)S(1)} %get-tuple-element.55.s0), channel_id=1, source_target_pairs={{0,8},{4,12},{8,0},{12,4},{1,9},{5,13},{9,1},{13,5},{2,10},{6,14},... | collective-permute-start | bytes 430088 | tf_op jit(solution)/shard_map/ppermute | solution.py:239
  77.3 5.5 %collective-permute-start.21 = (bf16[560,128]{1,0:T(8,128)(2,1)S(1)}, bf16[560,128]{1,0:T(8,128)(2,1)S(1)}, u32[]{:S(2)}, u32[]{:S(2)}) collective-permute-start(bf16[560,128]{1,0:T(8,128)(2,1)S(1)} %get-tuple-element.55.s0), channel_id=1, source_target_pairs={{0,12},{4,0},{8,4},{12,8},{1,13},{5,1},{9,5},{13,9},{2,14},{6,2},{... | collective-permute-start | bytes 430088 | tf_op jit(solution)/shard_map/ppermute | solution.py:239
  78.4 7.0 %collective-permute-start.20 = (bf16[560,128]{1,0:T(8,128)(2,1)S(1)}, bf16[560,128]{1,0:T(8,128)(2,1)S(1)}, u32[]{:S(2)}, u32[]{:S(2)}) collective-permute-start(bf16[560,128]{1,0:T(8,128)(2,1)S(1)} %get-tuple-element.55.s0), channel_id=1, source_target_pairs={{0,4},{4,8},{8,12},{12,0},{1,5},{5,9},{9,13},{13,1},{2,6},{6,10},{... | collective-permute-start | bytes 430088 | tf_op jit(solution)/shard_map/ppermute | solution.py:239
  86.3 3.4 %collective-permute-start.23 = (bf16[560,512]{1,0:T(8,128)(2,1)S(1)}, bf16[560,512]{1,0:T(8,128)(2,1)S(1)}, u32[]{:S(2)}, u32[]{:S(2)}) collective-permute-start(bf16[560,512]{1,0:T(8,128)(2,1)S(1)} %shard_map.83.d_own), channel_id=1, source_target_pairs={{0,16},{16,0},{1,17},{17,1},{2,18},{18,2},{3,19},{19,3},{4,20},{20... | collective-permute-start | bytes 1720328 | tf_op jit(solution)/shard_map/ppermute | solution.py:239
  93.5 28.2 %all-to-all-start.1 = ((bf16[16,72,560]{2,1,0:T(8,128)(2,1)}), bf16[16,72,560]{2,1,0:T(8,128)(2,1)S(1)}, u32[]{:S(2)}, u32[]{:S(2)}) async-start(bf16[16,72,560]{2,1,0:T(8,128)(2,1)} %shard_map.84), calls=%async_computation.1 | async-start | bytes 2949120 | tf_op jit(solution)/shard_map/all_to_all | solution.py:340
  99.2 7.0 %collective-permute-start.24 = (bf16[560,128]{1,0:T(8,128)(2,1)S(1)}, bf16[560,128]{1,0:T(8,128)(2,1)S(1)}, u32[]{:S(2)}, u32[]{:S(2)}) collective-permute-start(bf16[560,128]{1,0:T(8,128)(2,1)S(1)} %get-tuple-element.59), channel_id=1, source_target_pairs={{0,3},{1,0},{2,1},{3,2},{4,7},{5,4},{6,5},{7,6},{8,11},{9,8},{10,9... | collective-permute-start | bytes 430088 | tf_op jit(solution)/shard_map/ppermute | solution.py:239
  101.5 8.6 %collective-permute-start.25 = (bf16[560,128]{1,0:T(8,128)(2,1)S(1)}, bf16[560,128]{1,0:T(8,128)(2,1)S(1)}, u32[]{:S(2)}, u32[]{:S(2)}) collective-permute-start(bf16[560,128]{1,0:T(8,128)(2,1)S(1)} %get-tuple-element.60), channel_id=1, source_target_pairs={{0,2},{1,3},{2,0},{3,1},{4,6},{5,7},{6,4},{7,5},{8,10},{9,11},{10,... | collective-permute-start | bytes 430088 | tf_op jit(solution)/shard_map/ppermute | solution.py:239
  103.9 6.3 %collective-permute-start.26 = (bf16[560,128]{1,0:T(8,128)(2,1)S(1)}, bf16[560,128]{1,0:T(8,128)(2,1)S(1)}, u32[]{:S(2)}, u32[]{:S(2)}) collective-permute-start(bf16[560,128]{1,0:T(8,128)(2,1)S(1)} %get-tuple-element.61), channel_id=1, source_target_pairs={{0,1},{1,2},{2,3},{3,0},{4,5},{5,6},{6,7},{7,4},{8,9},{9,10},{10,1... | collective-permute-start | bytes 430088 | tf_op jit(solution)/shard_map/ppermute | solution.py:239
  121.9 5.5 %collective-permute-start.30 = (bf16[72,560]{1,0:T(8,128)(2,1)S(1)}, bf16[72,560]{1,0:T(8,128)(2,1)S(1)}, u32[]{:S(2)}, u32[]{:S(2)}) collective-permute-start(bf16[72,560]{1,0:T(8,128)(2,1)S(1)} %shard_map.86), channel_id=1, source_target_pairs={{0,96},{1,97},{2,98},{3,99},{32,1},{33,2},{34,3},{35,0},{64,34},{6... | collective-permute-start | bytes 241928 | tf_op jit(solution)/shard_map/ppermute | solution.py:345
  122.9 8.2 %collective-permute-start.29 = (bf16[72,560]{1,0:T(8,128)(2,1)S(1)}, bf16[72,560]{1,0:T(8,128)(2,1)S(1)}, u32[]{:S(2)}, u32[]{:S(2)}) collective-permute-start(bf16[72,560]{1,0:T(8,128)(2,1)S(1)} %shard_map.86), channel_id=1, source_target_pairs={{0,64},{1,65},{2,66},{3,67},{32,97},{33,98},{34,99},{35,96},{64,2}... | collective-permute-start | bytes 241928 | tf_op jit(solution)/shard_map/ppermute | solution.py:345
  125.1 9.1 %collective-permute-start.28 = (bf16[72,560]{1,0:T(8,128)(2,1)S(1)}, bf16[72,560]{1,0:T(8,128)(2,1)S(1)}, u32[]{:S(2)}, u32[]{:S(2)}) collective-permute-start(bf16[72,560]{1,0:T(8,128)(2,1)S(1)} %shard_map.86), channel_id=1, source_target_pairs={{0,32},{1,33},{2,34},{3,35},{32,65},{33,66},{34,67},{35,64},{64,98... | collective-permute-start | bytes 241928 | tf_op jit(solution)/shard_map/ppermute | solution.py:345
  126.7 11.6 %collective-permute-start.27 = (bf16[72,560]{1,0:T(8,128)(2,1)S(1)}, bf16[72,560]{1,0:T(8,128)(2,1)S(1)}, u32[]{:S(2)}, u32[]{:S(2)}) collective-permute-start(bf16[72,560]{1,0:T(8,128)(2,1)S(1)} %shard_map.86), channel_id=1, source_target_pairs={{0,0},{1,1},{2,2},{3,3},{32,33},{33,34},{34,35},{35,32},{64,66},{6... | collective-permute-start | bytes 241928 | tf_op jit(solution)/shard_map/ppermute | solution.py:345
  127.4 10.9 %collective-permute-start.34 = (bf16[72,560]{1,0:T(8,128)(2,1)S(1)}, bf16[72,560]{1,0:T(8,128)(2,1)S(1)}, u32[]{:S(2)}, u32[]{:S(2)}) collective-permute-start(bf16[72,560]{1,0:T(8,128)(2,1)S(1)} %collective-permute-done.30.r3), channel_id=1, source_target_pairs={{0,16},{16,0},{1,17},{17,1},{2,18},{18,2},{3,19},{19,3},{4,20},{20... | collective-permute-start | bytes 241928 | tf_op jit(solution)/shard_map/ppermute | solution.py:239
  131.2 7.1 %collective-permute-start.33 = (bf16[72,560]{1,0:T(8,128)(2,1)S(1)}, bf16[72,560]{1,0:T(8,128)(2,1)S(1)}, u32[]{:S(2)}, u32[]{:S(2)}) collective-permute-start(bf16[72,560]{1,0:T(8,128)(2,1)S(1)} %collective-permute-done.29.r2), channel_id=1, source_target_pairs={{0,16},{16,0},{1,17},{17,1},{2,18},{18,2},{3,19},{19,3},{4,20},{20... | collective-permute-start | bytes 241928 | tf_op jit(solution)/shard_map/ppermute | solution.py:239
  134.2 5.0 %collective-permute-start.32 = (bf16[72,560]{1,0:T(8,128)(2,1)S(1)}, bf16[72,560]{1,0:T(8,128)(2,1)S(1)}, u32[]{:S(2)}, u32[]{:S(2)}) collective-permute-start(bf16[72,560]{1,0:T(8,128)(2,1)S(1)} %collective-permute-done.28.r1), channel_id=1, source_target_pairs={{0,16},{16,0},{1,17},{17,1},{2,18},{18,2},{3,19},{19,3},{4,20},{20... | collective-permute-start | bytes 241928 | tf_op jit(solution)/shard_map/ppermute | solution.py:239
  138.3 1.3 collective-permute-start.31

commit v3 on v2

--- a/solution.py
+++ b/solution.py
@@ -57,10 +57,11 @@
     return jnp.dot(a, b, preferred_element_type=F32)
 
 
-def prep_weights(idx, wk, wv, out, buf, sem):
+def prep_weights(wk, wv, out, buf, sem):
+    core = lax.axis_index("core")
     for c, src in ((0, wk), (1, wv)):
 
-        @pl.when(idx[1] == c)
+        @pl.when(core == c)
         def _():
             cp = pltpu.make_async_copy(src, buf, sem)
             cp.start()
@@ -152,12 +153,17 @@
 def query_side(idx, s0, s1, s2, s3, q0, q1, q2, q3, g0, g1, g2, g3, dsum):
     summ = total_of((s0, s1, s2, s3))
     live = live_mask(idx, idx[3])
-    qc = (q0, q1, q2, q3)
     length = idx[4].astype(F32)
     for h in range(GH):
         s = slice(HEAD_DIM * h, HEAD_DIM * (h + 1))
-        q = jnp.concatenate([r[0, s].astype(F32) for r in qc], axis=1)
-        back = jnp.concatenate([r[1, s].astype(F32) for r in qc], axis=1) * live
+
+        def pieces(k):
+            at = slice(D // 2 + GW * k + s.start, D // 2 + GW * k + s.stop)
+            parts = (q0[k, s], q1[at], q2[k, s], q3[at])
+            return jnp.concatenate([p.astype(F32) for p in parts], axis=1)
+
+        q = pieces(0)
+        back = pieces(1) * live
         phi = jnp.maximum(q, 0.0)
         phib = phi.astype(BF)
         sh = summ[s]
@@ -187,8 +193,8 @@
 def group_tokens(idx, t0, t1, t3, t2_lo, t2_hi, own, oth, buf):
     for d, t in ((0, t0), (1, t1), (3, t3)):
         buf[:, ROWS * d : ROWS * (d + 1)] = t[...].astype(F32)
-    buf[: D // 2, 2 * ROWS : 3 * ROWS] = t2_lo[...].astype(F32)
-    buf[D // 2 :, 2 * ROWS : 3 * ROWS] = t2_hi[...].astype(F32)
+    buf[: D // 2, 2 * ROWS : 3 * ROWS] = t2_lo[: D // 2].astype(F32)
+    buf[D // 2 :, 2 * ROWS : 3 * ROWS] = t2_hi[: D // 2].astype(F32)
     zero = jnp.zeros((PAD - HALF, TOK), F32)
     for c in range(2):
 
@@ -202,8 +208,12 @@
                     dst[PAD * i : PAD * (i + 1)] = rows.astype(BF)
 
 
-def grad_weights(idx, t_own, t_oth, d_own, d_oth, out):
-    part = (nt(t_own[...], d_own[...]) + nt(t_oth[...], d_oth[...])).astype(BF)
+def grad_first(t, d, out):
+    out[...] = nt(t[...], d[...])
+
+
+def grad_second(idx, first, t, d, out):
+    part = (first[...] + nt(t[...], d[...])).astype(BF)
     for y in range(NY):
         for x in range(NX):
             i = NX * y + x
@@ -218,16 +228,14 @@
     out[...] = total.astype(BF)
 
 
-def place_rows(idx, r0, r1, r2, r3, o0, o1, o2, o3, out):
+def place_rows(idx, r0, r1, r2, r3, o0, o1, o2, o3, out, buf):
+    for step, (r, o) in enumerate(((r0, o0), (r1, o1), (r2, o2), (r3, o3))):
+        k = lax.rem(idx[3] - idx[0] + step + NX, NX)
+        buf[idx[1], k] = r[...].astype(F32)
+        buf[1 - idx[1], k] = o[...].astype(F32)
     for c in range(2):
         for k in range(NX):
-            for step, (r, o) in enumerate(((r0, o0), (r1, o1), (r2, o2), (r3, o3))):
-
-                @pl.when((idx[1] == c) & (lax.rem(idx[3] - idx[0] + step + NX, NX) == k))
-                def _():
-                    cols = slice(GW * k, GW * (k + 1))
-                    out[HALF * c : HALF * (c + 1), cols] = r[:HALF].astype(F32)
-                    out[HALF * (1 - c) : HALF * (2 - c), cols] = o[:HALF].astype(F32)
+            out[HALF * c : HALF * (c + 1), GW * k : GW * (k + 1)] = buf[c, k, :HALF]
 
 
 def place_queries(idx, g0, g1, g2, g3, out):
@@ -257,8 +265,8 @@
     pieces = call(
         prep_weights,
         sds((NX, SH, GW)),
-        [SMEM, HBM, HBM],
-        (idx, key_weight, value_weight),
+        [HBM, HBM],
+        (key_weight, value_weight),
         scratch=[pltpu.VMEM((SH, D), BF), pltpu.SemaphoreType.DMA],
         vmem=60,
     )
@@ -272,15 +280,16 @@
         scratch=[pltpu.SemaphoreType.DMA((8,))],
     )
     merged, *qc = lax.optimization_barrier((merged, *qc))
+    t_late, _ = lax.optimization_barrier((t_own, merged))
     w_own = call(merge_weights, sds((GW, GW)), [VMEM], (merged,))
     w_prev = shift(w_own, "y", 1)
     w_next = shift(w_own, "y", -1)
-    t_prev = shift(t_own, "x", 1)
+    t_prev = shift(t_late, "x", 1)
     t_next = shift(t_own, "x", -1)
     f_lo = shift(w_prev[:SPLIT], "y", 1)
     f_hi = shift(w_next[SPLIT:], "y", -1)
-    t_lo = shift(t_prev[: D // 2], "x", 1)
-    t_hi = shift(t_next[D // 2 :], "x", -1)
+    t_lo = shift(jnp.concatenate([t_prev[: D // 2], qc[1].reshape(2 * GW, ROWS)]), "x", 1)
+    t_hi = shift(jnp.concatenate([t_next[D // 2 :], qc[3].reshape(2 * GW, ROWS)]), "x", -1)
     ts = (t_own, t_next, t_prev, t_lo, t_hi)
     g_own, g_oth = call(
         group_tokens,
@@ -303,9 +312,9 @@
         flops=4 * TOK * D * GW,
         nbytes=5_000_000,
     )
-    summ, *qc = lax.optimization_barrier((summ, *qc))
+    summ, far = lax.optimization_barrier((summ, qc[2]))
     parts = sum_parts(summ)
-    q_in = [qc[0]] + [shift(qc[NX - d], "x", -d) for d in (1, 2, 3)]
+    q_in = (qc[0], t_hi, shift(far, "x", 2), t_lo)
     g_oth = swap(g_oth)
 
     outs = call(
@@ -329,13 +338,21 @@
         flops=2 * TOK * GW * 128,
         nbytes=2_000_000,
     )
+    first = call(
+        grad_first,
+        sds((16 * PAD, GW), F32),
+        [VMEM] * 2,
+        (g_own, dkt),
+        flops=2 * 16 * PAD * TOK * GW,
+        nbytes=5_000_000,
+    )
     part = call(
-        grad_weights,
+        grad_second,
         sds((16, PAD, GW)),
-        [SMEM] + [VMEM] * 4,
-        (idx, g_own, g_oth, dkt, swap(dkt)),
-        flops=4 * 16 * PAD * TOK * GW,
-        nbytes=6_000_000,
+        [SMEM] + [VMEM] * 3,
+        (idx, first, g_oth, swap(dkt)),
+        flops=2 * 16 * PAD * TOK * GW,
+        nbytes=5_000_000,
     )
     part = lax.all_to_all(part, ("z", "y"), 0, 0, tiled=True)
     grad_q = call(place_queries, sds((D, ROWS)), [SMEM] + [VMEM] * 4, (idx, *g_in))
@@ -354,7 +371,11 @@
         for s in range(NZ)
     ]
     grad_rows = call(
-        place_rows, sds((SH, D), F32), [SMEM] + [VMEM] * 8, (idx, *got, *[swap(g) for g in got])
+        place_rows,
+        sds((SH, D), F32),
+        [SMEM] + [VMEM] * 8,
+        (idx, *got, *[swap(g) for g in got]),
+        scratch=[pltpu.VMEM((2, NX, PAD, GW), F32)],
     )
     return grad_q.T[None], grad_rows
 

time: 143 us -> 136 us (0.951)
  starting transfers between devices: 63 us -> 58.8 us
  local copies, waits for them, and re-layouts: 3.97 us -> 2.33 us
  waiting for transfers between devices: 50.9 us -> 49.3 us
    ppermute x31 -> x29, starting transfers between devices: 47.6 us -> 42.7 us  [shift(): return lax.ppermute(v, axis, [(i, (i + d) % n) for i in range(n)])]
    ppermute x31 -> x29, waiting for transfers between devices: 37.2 us -> 32.4 us  [shift(): return lax.ppermute(v, axis, [(i, (i + d) % n) for i in range(n)])]
    all_to_all x1, starting transfers between devices: 5.7 us -> 7.16 us  [per_device(): part = lax.all_to_all(part, ('z', 'y'), 0, 0, tiled=True)]
    unnamed x20 -> x18, local copies, waits for them, and re-layouts: 3.2 us -> 2.14 us
    pallas_call x11 -> x12, Pallas kernels: 22.6 us -> 21.8 us  [call(): pl.pallas_call(body, out_shape=out_shape, in_specs=in_specs, out_specs=ja...]
  transfers between devices with their start and end apart: 37 -> 35, of which waited for: 19 -> 16; matrix products, arithmetic and copies ran while one was open for 0% -> 0% of each run, Pallas kernels for 9% -> 11%
where the time goes in v3:
time: 136 us; the launch traced here: 134 us
  starting transfers between devices  58.8 us (43%)
  waiting for transfers between devices  49.3 us (36%)
  Pallas kernels  21.8 us (16%)
  local copies, waits for them, and re-layouts  2.33 us (2%)
  between operations  1.56 us (1%)
    ppermute x29, starting transfers between devices, shift(): return lax.ppermute(v, axis, [(i, (i + d) % n) for i in range(n)])  42.7 us
    ppermute x29, waiting for transfers between devices, shift(): return lax.ppermute(v, axis, [(i, (i + d) % n) for i in range(n)])  32.4 us
    pallas_call x12, Pallas kernels, call(): pl.pallas_call(body, out_shape=out_shape, in_specs=in_specs, out_specs=ja...  21.8 us
    all_to_all x1, waiting for transfers between devices, per_device(): part = lax.all_to_all(part, ('z', 'y'), 0, 0, tiled=True)  11.6 us
    all_to_all x1, starting transfers between devices, per_device(): part = lax.all_to_all(part, ('z', 'y'), 0, 0, tiled=True)  7.16 us
    ppermute x4, starting transfers between devices, per_device(): lax.ppermute(rows, ('z', 'x'), [(z_at * NX + x_at, (z_at + s) % NZ * NX +...  4.65 us
    all_to_all x1, starting transfers between devices, per_device(): merged = lax.all_to_all(pieces, 'x', 0, 0, tiled=True)  4.35 us
    all_to_all x1, waiting for transfers between devices, per_device(): merged = lax.all_to_all(pieces, 'x', 0, 0, tiled=True)  3.54 us
  transfers between devices with their start and end apart: 35, of which 16 were waited for; matrix products, arithmetic and copies ran while one was open for 0% of the time, Pallas kernels for 11%

profile of v3, /device:TPU:7, one launch (start us, length us, event | category | flops | bytes accessed | tf_op | source)
XLA Modules:
  0.0 133.9 jit_solution(3533755294845173844)
XLA Ops:
  0.6 2.3 %shard_map.77 = bf16[4,140,560]{2,1,0:T(8,128)(2,1)} custom-call(bf16[140,2240]{1,0:T(8,128)(2,1)} %wk.1, bf16[140,2240]{1,0:T(8,128)(2,1)} %wv.1), custom_call_target="tpu_custom_call" | custom-call | tf_op jit(solution)/shard_map/pallas_call | solution.py:36
  2.9 4.4 %all-to-all-start = ((bf16[4,140,560]{2,1,0:T(8,128)(2,1)}), bf16[4,140,560]{2,1,0:T(8,128)(2,1)S(1)}, u32[]{:S(2)}, u32[]{:S(2)}) async-start(bf16[4,140,560]{2,1,0:T(8,128)(2,1)} %shard_map.77), calls=%async_computation | async-start | bytes 1474560 | tf_op jit(solution)/shard_map/all_to_all | solution.py:273
  7.3 0.6 collective-permute-start.4
  8.5 0.1 stack.19.idx
  8.6 2.1 %shard_map.78 = (bf16[2,560,128]{2,1,0:T(8,128)(2,1)S(1)}, bf16[2,560,128]{2,1,0:T(8,128)(2,1)S(1)}, bf16[2,560,128]{2,1,0:T(8,128)(2,1)S(1)}, bf16[2,560,128]{2,1,0:T(8,128)(2,1)S(1)}) custom-call(s32[5]{0:T(128)S(1)} %stack.19.idx, bf16[2240,128]{1,0:T(8,128)(2,1)S(1)} %bitcast.18, bf16[2240,128]{1,0:T(8,128)(2,1)S(1)} %bitcast.19), custom_call_target="tpu_custom_call" | custom-call | tf_op jit(solution)/shard_map/pallas_call | solution.py:36
  10.7 0.7 copy-done.3
  11.5 0.7 copy-done.5
  12.2 0.7 copy-done.7
  12.9 3.5 %all-to-all-done.g = bf16[4,140,560]{2,1,0:T(8,128)(2,1)S(1)} async-done(((bf16[4,140,560]{2,1,0:T(8,128)(2,1)}), bf16[4,140,560]{2,1,0:T(8,128)(2,1)S(1)}, u32[]{:S(2)}, u32[]{:S(2)}) %all-to-all-start) | async-done | bytes 627232 | tf_op jit(solution)/shard_map/all_to_all | solution.py:273
  16.4 1.7 %collective-permute-start.5 = (bf16[2240,128]{1,0:T(8,128)(2,1)S(1)}, bf16[2240,128]{1,0:T(8,128)(2,1)S(1)}, u32[]{:S(2)}, u32[]{:S(2)}) collective-permute-start(bf16[2240,128]{1,0:T(8,128)(2,1)S(1)} %bitcast.21), channel_id=1, source_target_pairs={{0,1},{1,2},{2,3},{3,0},{4,5},{5,6},{6,7},{7,4},{8,9},{9,10},{10,1... | collective-permute-start | bytes 1720328 | tf_op jit(solution)/shard_map/ppermute | solution.py:247
  18.1 0.3 shard_map.79.w0
  18.4 0.0 copy-start.4
  18.4 2.8 %collective-permute-start.2 = (bf16[560,560]{1,0:T(8,128)(2,1)S(1)}, bf16[560,560]{1,0:T(8,128)(2,1)S(1)}, u32[]{:S(2)}, u32[]{:S(2)}) collective-permute-start(bf16[560,560]{1,0:T(8,128)(2,1)S(1)} %shard_map.79.w0), channel_id=1, source_target_pairs={{0,12},{4,0},{8,4},{12,8},{1,13},{5,1},{9,5},{13,9},{2,14},{6,2},{... | collective-permute-start | bytes 1881608 | tf_op jit(solution)/shard_map/ppermute | solution.py:247
  21.3 6.5 %collective-permute-done.4.t1 = bf16[2240,128]{1,0:T(8,128)(2,1)S(1)} collective-permute-done((bf16[2240,128]{1,0:T(8,128)(2,1)S(1)}, bf16[2240,128]{1,0:T(8,128)(2,1)S(1)}, u32[]{:S(2)}, u32[]{:S(2)}) %collective-permute-start.4) | collective-permute-done | bytes 573472 | tf_op jit(solution)/shard_map/ppermute | solution.py:247
  27.9 1.3 collective-permute-start.7
  29.2 2.9 %collective-permute-start.6 = (bf16[2240,128]{1,0:T(8,128)(2,1)S(1)}, bf16[2240,128]{1,0:T(8,128)(2,1)S(1)}, u32[]{:S(2)}, u32[]{:S(2)}) collective-permute-start(bf16[2240,128]{1,0:T(8,128)(2,1)S(1)} %pad_maximum_fusion), channel_id=1, source_target_pairs={{0,1},{1,2},{2,3},{3,0},{4,5},{5,6},{6,7},{7,4},{8,9},{9,10},{10,1... | collective-permute-start | bytes 1720328 | tf_op jit(solution)/shard_map/ppermute | solution.py:247
  32.1 5.5 %collective-permute-done.w_prev = bf16[560,560]{1,0:T(8,128)(2,1)S(1)} collective-permute-done((bf16[560,560]{1,0:T(8,128)(2,1)S(1)}, bf16[560,560]{1,0:T(8,128)(2,1)S(1)}, u32[]{:S(2)}, u32[]{:S(2)}) %collective-permute-start) | collective-permute-done | bytes 627232 | tf_op jit(solution)/shard_map/ppermute | solution.py:247
  37.6 0.1 collective-permute-start.1
  37.7 2.7 %collective-permute-start.3 = (bf16[272,560]{1,0:T(8,128)(2,1)S(1)}, bf16[272,560]{1,0:T(8,128)(2,1)S(1)}, u32[]{:S(2)}, u32[]{:S(2)}) collective-permute-start(bf16[272,560]{1,0:T(8,128)(2,1)S(1)} %slice.17), channel_id=1, source_target_pairs={{0,12},{4,0},{8,4},{12,8},{1,13},{5,1},{9,5},{13,9},{2,14},{6,2},{... | collective-permute-start | bytes 913928 | tf_op jit(solution)/shard_map/ppermute | solution.py:247
  40.5 3.9 %collective-permute-start.8 = (bf16[560,560]{1,0:T(8,128)(2,1)S(1)}, bf16[560,560]{1,0:T(8,128)(2,1)S(1)}, u32[]{:S(2)}, u32[]{:S(2)}) collective-permute-start(bf16[560,560]{1,0:T(8,128)(2,1)S(1)} %shard_map.79.w0), channel_id=1, source_target_pairs={{0,16},{16,0},{1,17},{17,1},{2,18},{18,2},{3,19},{19,3},{4,20},{20... | collective-permute-start | bytes 1881608 | tf_op jit(solution)/shard_map/ppermute | solution.py:247
  44.4 0.2 collective-permute-start.10
  44.5 0.8 collective-permute-start.9
  45.3 1.5 %shard_map.80 = (bf16[1152,512]{1,0:T(8,128)(2,1)S(1)}, bf16[1152,512]{1,0:T(8,128)(2,1)S(1)}) custom-call(s32[5]{0:T(128)S(1)} %stack.19.idx, bf16[2240,128]{1,0:T(8,128)(2,1)S(1)} %bitcast.22, bf16[2240,128]{1,0:T(8,128)(2,1)S(1)} %collective-permute-done.4.t1, bf16[2240,128]{1,0:T(8,128)(2,1)S(1)} %collective-permute-done.5.t3, ...), custom_call_target="tpu_custom_call" | custom-call | bytes 10000000 | tf_op jit(solution)/shard_map/pallas_call | solution.py:36
  46.8 3.1 %collective-permute-start.11 = (bf16[288,560]{1,0:T(8,128)(2,1)S(1)}, bf16[288,560]{1,0:T(8,128)(2,1)S(1)}, u32[]{:S(2)}, u32[]{:S(2)}) collective-permute-start(bf16[288,560]{1,0:T(8,128)(2,1)S(1)} %collective-permute-done.1.w_lo), channel_id=1, source_target_pairs={{0,16},{16,0},{1,17},{17,1},{2,18},{18,2},{3,19},{19,3},{4,20},{20... | collective-permute-start | bytes 967688 | tf_op jit(solution)/shard_map/ppermute | solution.py:247
  49.9 0.5 collective-permute-start.20
  50.4 1.3 collective-permute-done.12.v_hi
  51.7 5.1 %shard_map.81 = (bf16[560,512]{1,0:T(8,128)(2,1)S(1)}, bf16[560,512]{1,0:T(8,128)(2,1)S(1)}, bf16[560,128]{1,0:T(8,128)(2,1)S(1)}) custom-call(s32[5]{0:T(128)S(1)} %stack.19.idx, bf16[560,560]{1,0:T(8,128)(2,1)S(1)} %shard_map.79.w0, bf16[560,560]{1,0:T(8,128)(2,1)S(1)} %collective-permute-done.w_prev, bf16[560,560]{1,0:T(8,128)(2,1)S(1)} %collective-permute-done.2.w_next, ...), custom_call_target="tpu_custom_call" | custom-call | flops 2569011200 | bytes 5000000 | tf_op jit(solution)/shard_map/pallas_call | solution.py:36
  56.9 0.1 collective-permute-start.16
  57.0 2.2 %collective-permute-start.15 = (bf16[560,128]{1,0:T(8,128)(2,1)S(1)}, bf16[560,128]{1,0:T(8,128)(2,1)S(1)}, u32[]{:S(2)}, u32[]{:S(2)}) collective-permute-start(bf16[560,128]{1,0:T(8,128)(2,1)S(1)} %get-tuple-element.47.s0), channel_id=1, source_target_pairs={{0,8},{4,12},{8,0},{12,4},{1,9},{5,13},{9,1},{13,5},{2,10},{6,14},... | collective-permute-start | bytes 430088 | tf_op jit(solution)/shard_map/ppermute | solution.py:247
  59.2 0.8 collective-permute-start.14
  59.9 0.7 collective-permute-start.13
  60.6 2.7 %collective-permute-done.15.s3 = bf16[560,128]{1,0:T(8,128)(2,1)S(1)} collective-permute-done((bf16[560,128]{1,0:T(8,128)(2,1)S(1)}, bf16[560,128]{1,0:T(8,128)(2,1)S(1)}, u32[]{:S(2)}, u32[]{:S(2)}) %collective-permute-start.15) | collective-permute-done | bytes 143392 | tf_op jit(solution)/shard_map/ppermute | solution.py:247
  63.3 3.3 %collective-permute-done.14.s2 = bf16[560,128]{1,0:T(8,128)(2,1)S(1)} collective-permute-done((bf16[560,128]{1,0:T(8,128)(2,1)S(1)}, bf16[560,128]{1,0:T(8,128)(2,1)S(1)}, u32[]{:S(2)}, u32[]{:S(2)}) %collective-permute-start.14) | collective-permute-done | bytes 143392 | tf_op jit(solution)/shard_map/ppermute | solution.py:247
  66.7 0.1 collective-permute-done.13.s1
  66.8 2.0 %shard_map.82 = (bf16[560,128]{1,0:T(8,128)(2,1)S(1)}, bf16[560,128]{1,0:T(8,128)(2,1)S(1)}, bf16[560,128]{1,0:T(8,128)(2,1)S(1)}, bf16[560,128]{1,0:T(8,128)(2,1)S(1)}, bf16[560,128]{1,0:T(8,128)(2,1)S(1)}) custom-call(s32[5]{0:T(128)S(1)} %stack.19.idx, bf16[560,128]{1,0:T(8,128)(2,1)S(1)} %get-tuple-element.47.s0, ...), custom_call_target="tpu_custom_call" | custom-call | flops 220200960 | bytes 4000000 | tf_op jit(solution)/shard_map/pallas_call | solution.py:36
  68.8 2.3 %collective-permute-start.19 = (bf16[560,128]{1,0:T(8,128)(2,1)S(1)}, bf16[560,128]{1,0:T(8,128)(2,1)S(1)}, u32[]{:S(2)}, u32[]{:S(2)}) collective-permute-start(bf16[560,128]{1,0:T(8,128)(2,1)S(1)} %get-tuple-element.50.s0), channel_id=1, source_target_pairs={{0,8},{4,12},{8,0},{12,4},{1,9},{5,13},{9,1},{13,5},{2,10},{6,14},... | collective-permute-start | bytes 430088 | tf_op jit(solution)/shard_map/ppermute | solution.py:247
  71.1 1.1 collective-permute-start.18
  72.1 0.4 collective-permute-start.17
  72.5 1.8 %collective-permute-done.19.s3 = bf16[560,128]{1,0:T(8,128)(2,1)S(1)} collective-permute-done((bf16[560,128]{1,0:T(8,128)(2,1)S(1)}, bf16[560,128]{1,0:T(8,128)(2,1)S(1)}, u32[]{:S(2)}, u32[]{:S(2)}) %collective-permute-start.19) | collective-permute-done | bytes 143392 | tf_op jit(solution)/shard_map/ppermute | solution.py:247
  74.3 4.5 %collective-permute-done.18.s2 = bf16[560,128]{1,0:T(8,128)(2,1)S(1)} collective-permute-done((bf16[560,128]{1,0:T(8,128)(2,1)S(1)}, bf16[560,128]{1,0:T(8,128)(2,1)S(1)}, u32[]{:S(2)}, u32[]{:S(2)}) %collective-permute-start.18) | collective-permute-done | bytes 143392 | tf_op jit(solution)/shard_map/ppermute | solution.py:247
  78.8 0.9 shard_map.83.d
  79.8 1.5 %collective-permute-start.21 = (bf16[560,512]{1,0:T(8,128)(2,1)S(1)}, bf16[560,512]{1,0:T(8,128)(2,1)S(1)}, u32[]{:S(2)}, u32[]{:S(2)}) collective-permute-start(bf16[560,512]{1,0:T(8,128)(2,1)S(1)} %shard_map.83.d), channel_id=1, source_target_pairs={{0,16},{16,0},{1,17},{17,1},{2,18},{18,2},{3,19},{19,3},{4,20},{20... | collective-permute-start | bytes 1720328 | tf_op jit(solution)/shard_map/ppermute | solution.py:247
  81.3 1.1 shard_map.84.first
  82.4 0.5 collective-permute-done.21.d
  82.9 2.8 %shard_map.85 = bf16[16,72,560]{2,1,0:T(8,128)(2,1)} custom-call(s32[5]{0:T(128)S(1)} %stack.19.idx, f32[1152,560]{1,0:T(8,128)S(1)} %shard_map.84.first, bf16[1152,512]{1,0:T(8,128)(2,1)S(1)} %collective-permute-done.20.t, bf16[560,512]{1,0:T(8,128)(2,1)S(1)} %collective-permute-done.21.d), custom_call_target="tpu_custom_call" | custom-call | flops 660602880 | bytes 5000000 | tf_op jit(solution)/shard_map/pallas_call | solution.py:36
  85.7 7.2 %all-to-all-start.1 = ((bf16[16,72,560]{2,1,0:T(8,128)(2,1)}), bf16[16,72,560]{2,1,0:T(8,128)(2,1)S(1)}, u32[]{:S(2)}, u32[]{:S(2)}) async-start(bf16[16,72,560]{2,1,0:T(8,128)(2,1)} %shard_map.85), calls=%async_computation.1 | async-start | bytes 2949120 | tf_op jit(solution)/shard_map/all_to_all | solution.py:357
  92.9 1.8 %collective-permute-start.22 = (bf16[560,128]{1,0:T(8,128)(2,1)S(1)}, bf16[560,128]{1,0:T(8,128)(2,1)S(1)}, u32[]{:S(2)}, u32[]{:S(2)}) collective-permute-start(bf16[560,128]{1,0:T(8,128)(2,1)S(1)} %get-tuple-element.55), channel_id=1, source_target_pairs={{0,3},{1,0},{2,1},{3,2},{4,7},{5,4},{6,5},{7,6},{8,11},{9,8},{10,9... | collective-permute-start | bytes 430088 | tf_op jit(solution)/shard_map/ppermute | solution.py:247
  94.7 1.5 %collective-permute-start.23 = (bf16[560,128]{1,0:T(8,128)(2,1)S(1)}, bf16[560,128]{1,0:T(8,128)(2,1)S(1)}, u32[]{:S(2)}, u32[]{:S(2)}) collective-permute-start(bf16[560,128]{1,0:T(8,128)(2,1)S(1)} %get-tuple-element.56), channel_id=1, source_target_pairs={{0,2},{1,3},{2,0},{3,1},{4,6},{5,7},{6,4},{7,5},{8,10},{9,11},{10,... | collective-permute-start | bytes 430088 | tf_op jit(solution)/shard_map/ppermute | solution.py:247
  96.1 1.4 %collective-permute-start.24 = (bf16[560,128]{1,0:T(8,128)(2,1)S(1)}, bf16[560,128]{1,0:T(8,128)(2,1)S(1)}, u32[]{:S(2)}, u32[]{:S(2)}) collective-permute-start(bf16[560,128]{1,0:T(8,128)(2,1)S(1)} %get-tuple-element.57), channel_id=1, source_target_pairs={{0,1},{1,2},{2,3},{3,0},{4,5},{5,6},{6,7},{7,4},{8,9},{9,10},{10,1... | collective-permute-start | bytes 430088 | tf_op jit(solution)/shard_map/ppermute | solution.py:247
  97.5 1.2 collective-permute-done.22.g1
  98.8 3.6 %collective-permute-done.23.g2 = bf16[560,128]{1,0:T(8,128)(2,1)S(1)} collective-permute-done((bf16[560,128]{1,0:T(8,128)(2,1)S(1)}, bf16[560,128]{1,0:T(8,128)(2,1)S(1)}, u32[]{:S(2)}, u32[]{:S(2)}) %collective-permute-start.23) | collective-permute-done | bytes 143392 | tf_op jit(solution)/shard_map/ppermute | solution.py:247
  102.4 1.4 %shard_map.86 = bf16[2240,128]{1,0:T(8,128)(2,1)} custom-call(s32[5]{0:T(128)S(1)} %stack.19.idx, bf16[560,128]{1,0:T(8,128)(2,1)S(1)} %get-tuple-element.54.g0, bf16[560,128]{1,0:T(8,128)(2,1)S(1)} %collective-permute-done.22.g1, bf16[560,128]{1,0:T(8,128)(2,1)S(1)} %collective-permute-done.23.g2, bf16[560,128]{1,0:T(8,128)(2,1)S(1)} %collective-permute-done.24.g3), custom_call_target="tpu_custom_call" | custom-call | tf_op jit(solution)/shard_map/pallas_call | solution.py:36
  103.8 11.6 %all-to-all-done.1.g = bf16[16,72,560]{2,1,0:T(8,128)(2,1)S(1)} async-done(((bf16[16,72,560]{2,1,0:T(8,128)(2,1)}), bf16[16,72,560]{2,1,0:T(8,128)(2,1)S(1)}, u32[]{:S(2)}, u32[]{:S(2)}) %all-to-all-start.1) | async-done | bytes 1290272 | tf_op jit(solution)/shard_map/all_to_all | solution.py:357
  115.3 0.2 shard_map.87
  115.5 1.0 collective-permute-start.28
  116.6 3.0 %collective-permute-start.27 = (bf16[72,560]{1,0:T(8,128)(2,1)S(1)}, bf16[72,560]{1,0:T(8,128)(2,1)S(1)}, u32[]{:S(2)}, u32[]{:S(2)}) collective-permute-start(bf16[72,560]{1,0:T(8,128)(2,1)S(1)} %shard_map.87), channel_id=1, source_target_pairs={{0,64},{1,65},{2,66},{3,67},{32,97},{33,98},{34,99},{35,96},{64,2}... | collective-permute-start | bytes 241928 | tf_op jit(solution)/shard_map/ppermute | solution.py:362
  119.5 0.7 collective-permute-start.25
  120.2 2.8 %collective-permute-start.32 = (bf16[72,560]{1,0:T(8,128)(2,1)S(1)}, bf16[72,560]{1,0:T(8,128)(2,1)S(1)}, u32[]{:S(2)}, u32[]{:S(2)}) collective-permute-start(bf16[72,560]{1,0:T(8,128)(2,1)S(1)} %collective-permute-done.28.r3), channel_id=1, source_target_pairs={{0,16},{16,0},{1,17},{17,1},{2,18},{18,2},{3,19},{19,3},{4,20},{20... | collective-permute-start | bytes 241928 | tf_op jit(solution)/shard_map/ppermute | solution.py:247
  123.0 1.8 %collective-permute-done.27.r2 = bf16[72,560]{1,0:T(8,128)(2,1)S(1)} collective-permute-done((bf16[72,560]{1,0:T(8,128)(2,1)S(1)}, bf16[72,560]{1,0:T(8,128)(2,1)S(1)}, u32[]{:S(2)}, u32[]{:S(2)}) %collective-permute-start.27) | collective-permute-done | bytes 80672 | tf_op jit(solution)/shard_map/ppermute | solution.py:362
  124.8 3.1 %collective-permute-start.31 = (bf16[72,560]{1,0:T(8,128)(2,1)S(1)}, bf16[72,560]{1,0:T(8,128)(2,1)S(1)}, u32[]{:S(2)}, u32[]{:S(2)}) collective-permute-start(bf16[72,560]{1,0:T(8,128)(2,1)S(1)} %collective-permute-done.27.r2), channel_id=1, source_target_pairs={{0,16},{16,0},{1,17},{17,1},{2,18},{18,2},{3,19},{19,3},{4,20},{20... | collective-permute-start | bytes 241928 | tf_op jit(solution)/shard_map/ppermute | solution.py:247
  127.9 2.6 %collective-permute-start.30 = (bf16[72,560]{1,0:T(8,128)(2,1)S(1)}, bf16[72,560]{1,0:T(8,128)(2,1)S(1)}, u32[]{:S(2)}, u32[]{:S(2)}) collective-permute-start(bf16[72,560]{1,0:T(8,128)(2,1)S(1)} %collective-permute-done.26.r1), channel_id=1, source_target_pairs={{0,16},{16,0},{1,17},{17,1},{2,18},{18,2},{3,19},{19,3},{4,20},{20... | collective-permute-start | bytes 241928 | tf_op jit(solution)/shard_map/ppermute | solution.py:247
  130.5 0.9 collective-permute-done.30.o1
  131.4 0.4 collective-permute-done.29.o0
  131.8 2.1 %shard_map.88 = f32[140,2240]{1,0:T(8,128)} custom-call(s32[5]{0:T(128)S(1)} %stack.19.idx, bf16[72,560]{1,0:T(8,128)(2,1)S(1)} %collective-permute-done.25.r0, bf16[72,560]{1,0:T(8,128)(2,1)S(1)} %collective-permute-done.26.r1, bf16[72,560]{1,0:T(8,128)(2,1)S(1)} %collective-permute-done.27.r2, bf16[72,560]{1,0:T(8,128)(2,1)S(1)} %collective-permute-done.28.r3, ...), custom_call_target="tpu_custom_call" | custom-call | tf_op jit(solution)/shard_map/pallas_call | solution.py:36
  (43 shorter events, 0.3 us)
Async XLA Ops:
  0.6 6.7 %copy-start.2 = (bf16[1,128,2240]{1,2,0:T(8,128)(2,1)S(1)}, bf16[1,128,2240]{1,2,0:T(8,128)(2,1)}, u32[]{:S(2)}) copy-start(bf16[1,128,2240]{1,2,0:T(8,128)(2,1)} %param.6) | copy-start | bytes 1720324
  2.9 5.7 %copy-start = (bf16[1,128,2240]{1,2,0:T(8,128)(2,1)S(1)}, bf16[1,128,2240]{1,2,0:T(8,128)(2,1)}, u32[]{:S(2)}) copy-start(bf16[1,128,2240]{1,2,0:T(8,128)(2,1)} %param.7) | copy-start | bytes 1720324
  2.9 5.7 %copy-start.1 = (bf16[1,128,2240]{1,2,0:T(8,128)(2,1)S(1)}, bf16[1,128,2240]{1,2,0:T(8,128)(2,1)}, u32[]{:S(2)}) copy-start(bf16[1,128,2240]{1,2,0:T(8,128)(2,1)} %param.8) | copy-start | bytes 1720324
  2.9 13.5 %all-to-all-start = ((bf16[4,140,560]{2,1,0:T(8,128)(2,1)}), bf16[4,140,560]{2,1,0:T(8,128)(2,1)S(1)}, u32[]{:S(2)}, u32[]{:S(2)}) async-start(bf16[4,140,560]{2,1,0:T(8,128)(2,1)} %shard_map.77), calls=%async_computation | async-start | bytes 1474560 | tf_op jit(solution)/shard_map/all_to_all | solution.py:273
  7.3 20.5 %collective-permute-start.4 = (bf16[2240,128]{1,0:T(8,128)(2,1)S(1)}, bf16[2240,128]{1,0:T(8,128)(2,1)S(1)}, u32[]{:S(2)}, u32[]{:S(2)}) collective-permute-start(bf16[2240,128]{1,0:T(8,128)(2,1)S(1)} %bitcast.20), channel_id=1, source_target_pairs={{0,3},{1,0},{2,1},{3,2},{4,7},{5,4},{6,5},{7,6},{8,11},{9,8},{10,9... | collective-permute-start | bytes 1720328 | tf_op jit(solution)/shard_map/ppermute | solution.py:247
  10.7 0.7 copy-start.3
  11.5 0.7 copy-start.5
  12.2 0.7 copy-start.7
  16.4 11.4 %copy-start.6 = (bf16[2,560,128]{2,1,0:T(8,128)(2,1)S(1)}, bf16[2,560,128]{2,1,0:T(8,128)(2,1)}, u32[]{:S(2)}) copy-start(bf16[2,560,128]{2,1,0:T(8,128)(2,1)} %copy-done.5) | copy-start | bytes 860164
  16.4 12.7 %collective-permute-start.5 = (bf16[2240,128]{1,0:T(8,128)(2,1)S(1)}, bf16[2240,128]{1,0:T(8,128)(2,1)S(1)}, u32[]{:S(2)}, u32[]{:S(2)}) collective-permute-start(bf16[2240,128]{1,0:T(8,128)(2,1)S(1)} %bitcast.21), channel_id=1, source_target_pairs={{0,1},{1,2},{2,3},{3,0},{4,5},{5,6},{6,7},{7,4},{8,9},{9,10},{10,1... | collective-permute-start | bytes 1720328 | tf_op jit(solution)/shard_map/ppermute | solution.py:247
  18.4 10.7 %copy-start.4 = (bf16[2,560,128]{2,1,0:T(8,128)(2,1)S(1)}, bf16[2,560,128]{2,1,0:T(8,128)(2,1)}, u32[]{:S(2)}) copy-start(bf16[2,560,128]{2,1,0:T(8,128)(2,1)} %copy-done.3) | copy-start | bytes 860164
  18.4 19.3 %collective-permute-start.2 = (bf16[560,560]{1,0:T(8,128)(2,1)S(1)}, bf16[560,560]{1,0:T(8,128)(2,1)S(1)}, u32[]{:S(2)}, u32[]{:S(2)}) collective-permute-start(bf16[560,560]{1,0:T(8,128)(2,1)S(1)} %shard_map.79.w0), channel_id=1, source_target_pairs={{0,12},{4,0},{8,4},{12,8},{1,13},{5,1},{9,5},{13,9},{2,14},{6,2},{... | collective-permute-start | bytes 1881608 | tf_op jit(solution)/shard_map/ppermute | solution.py:247
  21.3 16.3 %collective-permute-start = (bf16[560,560]{1,0:T(8,128)(2,1)S(1)}, bf16[560,560]{1,0:T(8,128)(2,1)S(1)}, u32[]{:S(2)}, u32[]{:S(2)}) collective-permute-start(bf16[560,560]{1,0:T(8,128)(2,1)S(1)} %shard_map.79.w0), channel_id=1, source_target_pairs={{0,4},{4,8},{8,12},{12,0},{1,5},{5,9},{9,13},{13,1},{2,6},{6,10},{... | collective-permute-start | bytes 1881608 | tf_op jit(solution)/shard_map/ppermute | solution.py:247
  27.9 16.5 %collective-permute-start.7 = (bf16[2240,128]{1,0:T(8,128)(2,1)S(1)}, bf16[2240,128]{1,0:T(8,128)(2,1)S(1)}, u32[]{:S(2)}, u32[]{:S(2)}) collective-permute-start(bf16[2240,128]{1,0:T(8,128)(2,1)S(1)} %pad_maximum_fusion.1), channel_id=1, source_target_pairs={{0,3},{1,0},{2,1},{3,2},{4,7},{5,4},{6,5},{7,6},{8,11},{9,8},{10,9... | collective-permute-start | bytes 1720328 | tf_op jit(solution)/shard_map/ppermute | solution.py:247
  29.2 15.3 %collective-permute-start.6 = (bf16[2240,128]{1,0:T(8,128)(2,1)S(1)}, bf16[2240,128]{1,0:T(8,128)(2,1)S(1)}, u32[]{:S(2)}, u32[]{:S(2)}) collective-permute-start(bf16[2240,128]{1,0:T(8,128)(2,1)S(1)} %pad_maximum_fusion), channel_id=1, source_target_pairs={{0,1},{1,2},{2,3},{3,0},{4,5},{5,6},{6,7},{7,4},{8,9},{9,10},{10,1... | collective-permute-start | bytes 1720328 | tf_op jit(solution)/shard_map/ppermute | solution.py:247
  37.6 9.2 %collective-permute-start.1 = (bf16[288,560]{1,0:T(8,128)(2,1)S(1)}, bf16[288,560]{1,0:T(8,128)(2,1)S(1)}, u32[]{:S(2)}, u32[]{:S(2)}) collective-permute-start(bf16[288,560]{1,0:T(8,128)(2,1)S(1)} %slice.16), channel_id=1, source_target_pairs={{0,4},{4,8},{8,12},{12,0},{1,5},{5,9},{9,13},{13,1},{2,6},{6,10},{... | collective-permute-start | bytes 967688 | tf_op jit(solution)/shard_map/ppermute | solution.py:247
  37.7 9.1 %collective-permute-start.3 = (bf16[272,560]{1,0:T(8,128)(2,1)S(1)}, bf16[272,560]{1,0:T(8,128)(2,1)S(1)}, u32[]{:S(2)}, u32[]{:S(2)}) collective-permute-start(bf16[272,560]{1,0:T(8,128)(2,1)S(1)} %slice.17), channel_id=1, source_target_pairs={{0,12},{4,0},{8,4},{12,8},{1,13},{5,1},{9,5},{13,9},{2,14},{6,2},{... | collective-permute-start | bytes 913928 | tf_op jit(solution)/shard_map/ppermute | solution.py:247
  40.5 9.4 %collective-permute-start.8 = (bf16[560,560]{1,0:T(8,128)(2,1)S(1)}, bf16[560,560]{1,0:T(8,128)(2,1)S(1)}, u32[]{:S(2)}, u32[]{:S(2)}) collective-permute-start(bf16[560,560]{1,0:T(8,128)(2,1)S(1)} %shard_map.79.w0), channel_id=1, source_target_pairs={{0,16},{16,0},{1,17},{17,1},{2,18},{18,2},{3,19},{19,3},{4,20},{20... | collective-permute-start | bytes 1881608 | tf_op jit(solution)/shard_map/ppermute | solution.py:247
  44.4 6.0 %collective-permute-start.10 = (bf16[560,560]{1,0:T(8,128)(2,1)S(1)}, bf16[560,560]{1,0:T(8,128)(2,1)S(1)}, u32[]{:S(2)}, u32[]{:S(2)}) collective-permute-start(bf16[560,560]{1,0:T(8,128)(2,1)S(1)} %collective-permute-done.2.w_next), channel_id=1, source_target_pairs={{0,16},{16,0},{1,17},{17,1},{2,18},{18,2},{3,19},{19,3},{4,20},{20... | collective-permute-start | bytes 1881608 | tf_op jit(solution)/shard_map/ppermute | solution.py:247
  44.5 5.9 %collective-permute-start.9 = (bf16[560,560]{1,0:T(8,128)(2,1)S(1)}, bf16[560,560]{1,0:T(8,128)(2,1)S(1)}, u32[]{:S(2)}, u32[]{:S(2)}) collective-permute-start(bf16[560,560]{1,0:T(8,128)(2,1)S(1)} %collective-permute-done.w_prev), channel_id=1, source_target_pairs={{0,16},{16,0},{1,17},{17,1},{2,18},{18,2},{3,19},{19,3},{4,20},{20... | collective-permute-start | bytes 1881608 | tf_op jit(solution)/shard_map/ppermute | solution.py:247
  46.8 10.0 %copy-start.8 = (bf16[2,560,128]{2,1,0:T(8,128)(2,1)S(1)}, bf16[2,560,128]{2,1,0:T(8,128)(2,1)}, u32[]{:S(2)}) copy-start(bf16[2,560,128]{2,1,0:T(8,128)(2,1)} %copy-done.7) | copy-start | bytes 860164
  46.8 4.9 %collective-permute-start.11 = (bf16[288,560]{1,0:T(8,128)(2,1)S(1)}, bf16[288,560]{1,0:T(8,128)(2,1)S(1)}, u32[]{:S(2)}, u32[]{:S(2)}) collective-permute-start(bf16[288,560]{1,0:T(8,128)(2,1)S(1)} %collective-permute-done.1.w_lo), channel_id=1, source_target_pairs={{0,16},{16,0},{1,17},{17,1},{2,18},{18,2},{3,19},{19,3},{4,20},{20... | collective-permute-start | bytes 967688 | tf_op jit(solution)/shard_map/ppermute | solution.py:247
  49.9 1.8 %collective-permute-start.12 = (bf16[272,560]{1,0:T(8,128)(2,1)S(1)}, bf16[272,560]{1,0:T(8,128)(2,1)S(1)}, u32[]{:S(2)}, u32[]{:S(2)}) collective-permute-start(bf16[272,560]{1,0:T(8,128)(2,1)S(1)} %collective-permute-done.3.w_hi), channel_id=1, source_target_pairs={{0,16},{16,0},{1,17},{17,1},{2,18},{18,2},{3,19},{19,3},{4,20},{20... | collective-permute-start | bytes 913928 | tf_op jit(solution)/shard_map/ppermute | solution.py:247
  49.9 32.5 %collective-permute-start.20 = (bf16[1152,512]{1,0:T(8,128)(2,1)S(1)}, bf16[1152,512]{1,0:T(8,128)(2,1)S(1)}, u32[]{:S(2)}, u32[]{:S(2)}) collective-permute-start(bf16[1152,512]{1,0:T(8,128)(2,1)S(1)} %get-tuple-element.53), channel_id=1, source_target_pairs={{0,16},{16,0},{1,17},{17,1},{2,18},{18,2},{3,19},{19,3},{4,20},{20... | collective-permute-start | bytes 3538952 | tf_op jit(solution)/shard_map/ppermute | solution.py:247
  56.9 10.0 %collective-permute-start.16 = (bf16[2,560,128]{2,1,0:T(8,128)(2,1)S(1)}, bf16[2,560,128]{2,1,0:T(8,128)(2,1)S(1)}, u32[]{:S(2)}, u32[]{:S(2)}) collective-permute-start(bf16[2,560,128]{2,1,0:T(8,128)(2,1)S(1)} %copy-done.8), channel_id=1, source_target_pairs={{0,2},{1,3},{2,0},{3,1},{4,6},{5,7},{6,4},{7,5},{8,10},{9,11},{10,... | collective-permute-start | bytes 860168 | tf_op jit(solution)/shard_map/ppermute | solution.py:247
  57.0 6.4 %collective-permute-start.15 = (bf16[560,128]{1,0:T(8,128)(2,1)S(1)}, bf16[560,128]{1,0:T(8,128)(2,1)S(1)}, u32[]{:S(2)}, u32[]{:S(2)}) collective-permute-start(bf16[560,128]{1,0:T(8,128)(2,1)S(1)} %get-tuple-element.47.s0), channel_id=1, source_target_pairs={{0,8},{4,12},{8,0},{12,4},{1,9},{5,13},{9,1},{13,5},{2,10},{6,14},... | collective-permute-start | bytes 430088 | tf_op jit(solution)/shard_map/ppermute | solution.py:247
  59.2 7.5 %collective-permute-start.14 = (bf16[560,128]{1,0:T(8,128)(2,1)S(1)}, bf16[560,128]{1,0:T(8,128)(2,1)S(1)}, u32[]{:S(2)}, u32[]{:S(2)}) collective-permute-start(bf16[560,128]{1,0:T(8,128)(2,1)S(1)} %get-tuple-element.47.s0), channel_id=1, source_target_pairs={{0,12},{4,0},{8,4},{12,8},{1,13},{5,1},{9,5},{13,9},{2,14},{6,2},{... | collective-permute-start | bytes 430088 | tf_op jit(solution)/shard_map/ppermute | solution.py:247
  59.9 6.9 %collective-permute-start.13 = (bf16[560,128]{1,0:T(8,128)(2,1)S(1)}, bf16[560,128]{1,0:T(8,128)(2,1)S(1)}, u32[]{:S(2)}, u32[]{:S(2)}) collective-permute-start(bf16[560,128]{1,0:T(8,128)(2,1)S(1)} %get-tuple-element.47.s0), channel_id=1, source_target_pairs={{0,4},{4,8},{8,12},{12,0},{1,5},{5,9},{9,13},{13,1},{2,6},{6,10},{... | collective-permute-start | bytes 430088 | tf_op jit(solution)/shard_map/ppermute | solution.py:247
  68.8 5.5 %collective-permute-start.19 = (bf16[560,128]{1,0:T(8,128)(2,1)S(1)}, bf16[560,128]{1,0:T(8,128)(2,1)S(1)}, u32[]{:S(2)}, u32[]{:S(2)}) collective-permute-start(bf16[560,128]{1,0:T(8,128)(2,1)S(1)} %get-tuple-element.50.s0), channel_id=1, source_target_pairs={{0,8},{4,12},{8,0},{12,4},{1,9},{5,13},{9,1},{13,5},{2,10},{6,14},... | collective-permute-start | bytes 430088 | tf_op jit(solution)/shard_map/ppermute | solution.py:247
  71.1 7.8 %collective-permute-start.18 = (bf16[560,128]{1,0:T(8,128)(2,1)S(1)}, bf16[560,128]{1,0:T(8,128)(2,1)S(1)}, u32[]{:S(2)}, u32[]{:S(2)}) collective-permute-start(bf16[560,128]{1,0:T(8,128)(2,1)S(1)} %get-tuple-element.50.s0), channel_id=1, source_target_pairs={{0,12},{4,0},{8,4},{12,8},{1,13},{5,1},{9,5},{13,9},{2,14},{6,2},{... | collective-permute-start | bytes 430088 | tf_op jit(solution)/shard_map/ppermute | solution.py:247
  72.1 6.7 %collective-permute-start.17 = (bf16[560,128]{1,0:T(8,128)(2,1)S(1)}, bf16[560,128]{1,0:T(8,128)(2,1)S(1)}, u32[]{:S(2)}, u32[]{:S(2)}) collective-permute-start(bf16[560,128]{1,0:T(8,128)(2,1)S(1)} %get-tuple-element.50.s0), channel_id=1, source_target_pairs={{0,4},{4,8},{8,12},{12,0},{1,5},{5,9},{9,13},{13,1},{2,6},{6,10},{... | collective-permute-start | bytes 430088 | tf_op jit(solution)/shard_map/ppermute | solution.py:247
  79.8 3.1 %collective-permute-start.21 = (bf16[560,512]{1,0:T(8,128)(2,1)S(1)}, bf16[560,512]{1,0:T(8,128)(2,1)S(1)}, u32[]{:S(2)}, u32[]{:S(2)}) collective-permute-start(bf16[560,512]{1,0:T(8,128)(2,1)S(1)} %shard_map.83.d), channel_id=1, source_target_pairs={{0,16},{16,0},{1,17},{17,1},{2,18},{18,2},{3,19},{19,3},{4,20},{20... | collective-permute-start | bytes 1720328 | tf_op jit(solution)/shard_map/ppermute | solution.py:247
  85.7 29.6 %all-to-all-start.1 = ((bf16[16,72,560]{2,1,0:T(8,128)(2,1)}), bf16[16,72,560]{2,1,0:T(8,128)(2,1)S(1)}, u32[]{:S(2)}, u32[]{:S(2)}) async-start(bf16[16,72,560]{2,1,0:T(8,128)(2,1)} %shard_map.85), calls=%async_computation.1 | async-start | bytes 2949120 | tf_op jit(solution)/shard_map/all_to_all | solution.py:357
  92.9 5.9 %collective-permute-start.22 = (bf16[560,128]{1,0:T(8,128)(2,1)S(1)}, bf16[560,128]{1,0:T(8,128)(2,1)S(1)}, u32[]{:S(2)}, u32[]{:S(2)}) collective-permute-start(bf16[560,128]{1,0:T(8,128)(2,1)S(1)} %get-tuple-element.55), channel_id=1, source_target_pairs={{0,3},{1,0},{2,1},{3,2},{4,7},{5,4},{6,5},{7,6},{8,11},{9,8},{10,9... | collective-permute-start | bytes 430088 | tf_op jit(solution)/shard_map/ppermute | solution.py:247
  94.7 7.7 %collective-permute-start.23 = (bf16[560,128]{1,0:T(8,128)(2,1)S(1)}, bf16[560,128]{1,0:T(8,128)(2,1)S(1)}, u32[]{:S(2)}, u32[]{:S(2)}) collective-permute-start(bf16[560,128]{1,0:T(8,128)(2,1)S(1)} %get-tuple-element.56), channel_id=1, source_target_pairs={{0,2},{1,3},{2,0},{3,1},{4,6},{5,7},{6,4},{7,5},{8,10},{9,11},{10,... | collective-permute-start | bytes 430088 | tf_op jit(solution)/shard_map/ppermute | solution.py:247
  96.1 6.3 %collective-permute-start.24 = (bf16[560,128]{1,0:T(8,128)(2,1)S(1)}, bf16[560,128]{1,0:T(8,128)(2,1)S(1)}, u32[]{:S(2)}, u32[]{:S(2)}) collective-permute-start(bf16[560,128]{1,0:T(8,128)(2,1)S(1)} %get-tuple-element.57), channel_id=1, source_target_pairs={{0,1},{1,2},{2,3},{3,0},{4,5},{5,6},{6,7},{7,4},{8,9},{9,10},{10,1... | collective-permute-start | bytes 430088 | tf_op jit(solution)/shard_map/ppermute | solution.py:247
  115.5 4.7 %collective-permute-start.28 = (bf16[72,560]{1,0:T(8,128)(2,1)S(1)}, bf16[72,560]{1,0:T(8,128)(2,1)S(1)}, u32[]{:S(2)}, u32[]{:S(2)}) collective-permute-start(bf16[72,560]{1,0:T(8,128)(2,1)S(1)} %shard_map.87), channel_id=1, source_target_pairs={{0,96},{1,97},{2,98},{3,99},{32,1},{33,2},{34,3},{35,0},{64,34},{6... | collective-permute-start | bytes 241928 | tf_op jit(solution)/shard_map/ppermute | solution.py:362
  116.6 8.2 %collective-permute-start.27 = (bf16[72,560]{1,0:T(8,128)(2,1)S(1)}, bf16[72,560]{1,0:T(8,128)(2,1)S(1)}, u32[]{:S(2)}, u32[]{:S(2)}) collective-permute-start(bf16[72,560]{1,0:T(8,128)(2,1)S(1)} %shard_map.87), channel_id=1, source_target_pairs={{0,64},{1,65},{2,66},{3,67},{32,97},{33,98},{34,99},{35,96},{64,2}... | collective-permute-start | bytes 241928 | tf_op jit(solution)/shard_map/ppermute | solution.py:362
  119.5 8.4 %collective-permute-start.26 = (bf16[72,560]{1,0:T(8,128)(2,1)S(1)}, bf16[72,560]{1,0:T(8,128)(2,1)S(1)}, u32[]{:S(2)}, u32[]{:S(2)}) collective-permute-start(bf16[72,560]{1,0:T(8,128)(2,1)S(1)} %shard_map.87), channel_id=1, source_target_pairs={{0,32},{1,33},{2,34},{3,35},{32,65},{33,66},{34,67},{35,64},{64,98... | collective-permute-start | bytes 241928 | tf_op jit(solution)/shard_map/ppermute | solution.py:362
  119.5 11.0 %collective-permute-start.25 = (bf16[72,560]{1,0:T(8,128)(2,1)S(1)}, bf16[72,560]{1,0:T(8,128)(2,1)S(1)}, u32[]{:S(2)}, u32[]{:S(2)}) collective-permute-start(bf16[72,560]{1,0:T(8,128)(2,1)S(1)} %shard_map.87), channel_id=1, source_target_pairs={{0,0},{1,1},{2,2},{3,3},{32,33},{33,34},{34,35},{35,32},{64,66},{6... | collective-permute-start | bytes 241928 | tf_op jit(solution)/shard_map/ppermute | solution.py:362
  120.2 10.3 %collective-permute-start.32 = (bf16[72,560]{1,0:T(8,128)(2,1)S(1)}, bf16[72,560]{1,0:T(8,128)(2,1)S(1)}, u32[]{:S(2)}, u32[]{:S(2)}) collective-permute-start(bf16[72,560]{1,0:T(8,128)(2,1)S(1)} %collective-permute-done.28.r3), channel_id=1, source_target_pairs={{0,16},{16,0},{1,17},{17,1},{2,18},{18,2},{3,19},{19,3},{4,20},{20... | collective-permute-start | bytes 241928 | tf_op jit(solution)/shard_map/ppermute | solution.py:247
  124.8 5.7 %collective-permute-start.31 = (bf16[72,560]{1,0:T(8,128)(2,1)S(1)}, bf16[72,560]{1,0:T(8,128)(2,1)S(1)}, u32[]{:S(2)}, u32[]{:S(2)}) collective-permute-start(bf16[72,560]{1,0:T(8,128)(2,1)S(1)} %collective-permute-done.27.r2), channel_id=1, source_target_pairs={{0,16},{16,0},{1,17},{17,1},{2,18},{18,2},{3,19},{19,3},{4,20},{20... | collective-permute-start | bytes 241928 | tf_op jit(solution)/shard_map/ppermute | solution.py:247
  127.9 3.5 %collective-permute-start.30 = (bf16[72,560]{1,0:T(8,128)(2,1)S(1)}, bf16[72,560]{1,0:T(8,128)(2,1)S(1)}, u32[]{:S(2)}, u32[]{:S(2)}) collective-permute-start(bf16[72,560]{1,0:T(8,128)(2,1)S(1)} %collective-permute-done.26.r1), channel_id=1, source_target_pairs={{0,16},{16,0},{1,17},{17,1},{2,18},{18,2},{3,19},{19,3},{4,20},{20... | collective-permute-start | bytes 241928 | tf_op jit(solution)/shard_map/ppermute | solution.py:247
  130.5 1.3 collective-permute-start.29

commit v4 on v3

--- a/solution.py
+++ b/solution.py
@@ -19,6 +19,8 @@
 SH = D // 16
 HALF = SH // 2
 PAD = 72
+PR, PL = 64, 640
+EX = PL - GW
 SPLIT = 288
 BF = jnp.bfloat16
 F32 = jnp.float32
@@ -212,13 +214,19 @@
     out[...] = nt(t[...], d[...])
 
 
+def pack(p):
+    extra = [p[PR:PAD, EX * j : EX * (j + 1)] for j in range(GW // EX)]
+    extra.append(jnp.zeros((PAD - PR, EX), F32))
+    return jnp.concatenate([p[:PR], jnp.concatenate(extra, axis=0)], axis=1)
+
+
 def grad_second(idx, first, t, d, out):
-    part = (first[...] + nt(t[...], d[...])).astype(BF)
+    part = first[...] + nt(t[...], d[...])
     for y in range(NY):
         for x in range(NX):
             i = NX * y + x
             z = lax.rem(x - idx[3] + NX, NX)
-            out[z * NY + y] = part[PAD * i : PAD * (i + 1)]
+            out[z * NY + y] = pack(part[PAD * i : PAD * (i + 1)]).astype(BF)
 
 
 def sum_pieces(g, out):
@@ -235,7 +243,11 @@
         buf[1 - idx[1], k] = o[...].astype(F32)
     for c in range(2):
         for k in range(NX):
-            out[HALF * c : HALF * (c + 1), GW * k : GW * (k + 1)] = buf[c, k, :HALF]
+            lo, at = HALF * c, GW * k
+            out[lo : lo + PR, at : at + GW] = buf[c, k, :, :GW]
+            tail = [buf[c, k, 8 * j : 8 * (j + 1), GW:] for j in range(GW // EX)]
+            tail = jnp.concatenate(tail, axis=1)
+            out[lo + PR : lo + HALF, at : at + GW] = tail[: HALF - PR]
 
 
 def place_queries(idx, g0, g1, g2, g3, out):
@@ -348,7 +360,7 @@
     )
     part = call(
         grad_second,
-        sds((16, PAD, GW)),
+        sds((16, PR, PL)),
         [SMEM] + [VMEM] * 3,
         (idx, first, g_oth, swap(dkt)),
         flops=2 * 16 * PAD * TOK * GW,
@@ -357,7 +369,7 @@
     part = lax.all_to_all(part, ("z", "y"), 0, 0, tiled=True)
     grad_q = call(place_queries, sds((D, ROWS)), [SMEM] + [VMEM] * 4, (idx, *g_in))
     part, grad_q = lax.optimization_barrier((part, grad_q))
-    rows = call(sum_pieces, sds((PAD, GW)), [VMEM], (part,))
+    rows = call(sum_pieces, sds((PR, PL)), [VMEM], (part,))
     got = [
         lax.ppermute(
             rows,
@@ -375,7 +387,7 @@
         sds((SH, D), F32),
         [SMEM] + [VMEM] * 8,
         (idx, *got, *[swap(g) for g in got]),
-        scratch=[pltpu.VMEM((2, NX, PAD, GW), F32)],
+        scratch=[pltpu.VMEM((2, NX, PR, PL), F32)],
     )
     return grad_q.T[None], grad_rows
 

time: 136 us -> 134 us (0.985)
  waiting for transfers between devices: 49.3 us -> 45.7 us
    all_to_all x1, waiting for transfers between devices: 11.6 us -> 9.21 us  [per_device(): part = lax.all_to_all(part, ('z', 'y'), 0, 0, tiled=True)]
where the time goes in v4:
time: 134 us; the launch traced here: 131 us
  starting transfers between devices  59.4 us (44%)
  waiting for transfers between devices  45.7 us (34%)
  Pallas kernels  22.2 us (17%)
  local copies, waits for them, and re-layouts  2.33 us (2%)
  between operations  1.56 us (1%)
    ppermute x29, starting transfers between devices, shift(): return lax.ppermute(v, axis, [(i, (i + d) % n) for i in range(n)])  43.6 us
    ppermute x29, waiting for transfers between devices, shift(): return lax.ppermute(v, axis, [(i, (i + d) % n) for i in range(n)])  32.4 us
    pallas_call x12, Pallas kernels, call(): pl.pallas_call(body, out_shape=out_shape, in_specs=in_specs, out_specs=ja...  22.2 us
    all_to_all x1, waiting for transfers between devices, per_device(): part = lax.all_to_all(part, ('z', 'y'), 0, 0, tiled=True)  9.21 us
    all_to_all x1, starting transfers between devices, per_device(): part = lax.all_to_all(part, ('z', 'y'), 0, 0, tiled=True)  7.16 us
    all_to_all x1, starting transfers between devices, per_device(): merged = lax.all_to_all(pieces, 'x', 0, 0, tiled=True)  4.35 us
    ppermute x4, starting transfers between devices, per_device(): lax.ppermute(rows, ('z', 'x'), [(z_at * NX + x_at, (z_at + s) % NZ * NX +...  4.29 us
    all_to_all x1, waiting for transfers between devices, per_device(): merged = lax.all_to_all(pieces, 'x', 0, 0, tiled=True)  3.54 us
  transfers between devices with their start and end apart: 35, of which 16 were waited for; matrix products, arithmetic and copies ran while one was open for 0% of the time, Pallas kernels for 11%

profile of v4, /device:TPU:7, one launch (start us, length us, event | category | flops | bytes accessed | tf_op | source)
XLA Modules:
  0.0 131.3 jit_solution(15344083591863748058)
XLA Ops:
  0.6 2.3 %shard_map.77 = bf16[4,140,560]{2,1,0:T(8,128)(2,1)} custom-call(bf16[140,2240]{1,0:T(8,128)(2,1)} %wk.1, bf16[140,2240]{1,0:T(8,128)(2,1)} %wv.1), custom_call_target="tpu_custom_call" | custom-call | tf_op jit(solution)/shard_map/pallas_call | solution.py:38
  2.9 4.4 %all-to-all-start = ((bf16[4,140,560]{2,1,0:T(8,128)(2,1)}), bf16[4,140,560]{2,1,0:T(8,128)(2,1)S(1)}, u32[]{:S(2)}, u32[]{:S(2)}) async-start(bf16[4,140,560]{2,1,0:T(8,128)(2,1)} %shard_map.77), calls=%async_computation | async-start | bytes 1474560 | tf_op jit(solution)/shard_map/all_to_all | solution.py:285
  7.3 0.6 collective-permute-start.4
  8.5 0.1 stack.19.idx
  8.6 2.1 %shard_map.78 = (bf16[2,560,128]{2,1,0:T(8,128)(2,1)S(1)}, bf16[2,560,128]{2,1,0:T(8,128)(2,1)S(1)}, bf16[2,560,128]{2,1,0:T(8,128)(2,1)S(1)}, bf16[2,560,128]{2,1,0:T(8,128)(2,1)S(1)}) custom-call(s32[5]{0:T(128)S(1)} %stack.19.idx, bf16[2240,128]{1,0:T(8,128)(2,1)S(1)} %bitcast.18, bf16[2240,128]{1,0:T(8,128)(2,1)S(1)} %bitcast.19), custom_call_target="tpu_custom_call" | custom-call | tf_op jit(solution)/shard_map/pallas_call | solution.py:38
  10.7 0.7 copy-done.3
  11.5 0.7 copy-done.5
  12.2 0.7 copy-done.7
  12.9 3.5 %all-to-all-done.g = bf16[4,140,560]{2,1,0:T(8,128)(2,1)S(1)} async-done(((bf16[4,140,560]{2,1,0:T(8,128)(2,1)}), bf16[4,140,560]{2,1,0:T(8,128)(2,1)S(1)}, u32[]{:S(2)}, u32[]{:S(2)}) %all-to-all-start) | async-done | bytes 627232 | tf_op jit(solution)/shard_map/all_to_all | solution.py:285
  16.4 1.7 %collective-permute-start.5 = (bf16[2240,128]{1,0:T(8,128)(2,1)S(1)}, bf16[2240,128]{1,0:T(8,128)(2,1)S(1)}, u32[]{:S(2)}, u32[]{:S(2)}) collective-permute-start(bf16[2240,128]{1,0:T(8,128)(2,1)S(1)} %bitcast.21), channel_id=1, source_target_pairs={{0,1},{1,2},{2,3},{3,0},{4,5},{5,6},{6,7},{7,4},{8,9},{9,10},{10,1... | collective-permute-start | bytes 1720328 | tf_op jit(solution)/shard_map/ppermute | solution.py:259
  18.1 0.3 shard_map.79.w0
  18.4 2.8 %collective-permute-start.2 = (bf16[560,560]{1,0:T(8,128)(2,1)S(1)}, bf16[560,560]{1,0:T(8,128)(2,1)S(1)}, u32[]{:S(2)}, u32[]{:S(2)}) collective-permute-start(bf16[560,560]{1,0:T(8,128)(2,1)S(1)} %shard_map.79.w0), channel_id=1, source_target_pairs={{0,12},{4,0},{8,4},{12,8},{1,13},{5,1},{9,5},{13,9},{2,14},{6,2},{... | collective-permute-start | bytes 1881608 | tf_op jit(solution)/shard_map/ppermute | solution.py:259
  21.3 6.5 %collective-permute-done.4.t1 = bf16[2240,128]{1,0:T(8,128)(2,1)S(1)} collective-permute-done((bf16[2240,128]{1,0:T(8,128)(2,1)S(1)}, bf16[2240,128]{1,0:T(8,128)(2,1)S(1)}, u32[]{:S(2)}, u32[]{:S(2)}) %collective-permute-start.4) | collective-permute-done | bytes 573472 | tf_op jit(solution)/shard_map/ppermute | solution.py:259
  27.9 1.3 collective-permute-start.7
  29.2 2.9 %collective-permute-start.6 = (bf16[2240,128]{1,0:T(8,128)(2,1)S(1)}, bf16[2240,128]{1,0:T(8,128)(2,1)S(1)}, u32[]{:S(2)}, u32[]{:S(2)}) collective-permute-start(bf16[2240,128]{1,0:T(8,128)(2,1)S(1)} %pad_maximum_fusion), channel_id=1, source_target_pairs={{0,1},{1,2},{2,3},{3,0},{4,5},{5,6},{6,7},{7,4},{8,9},{9,10},{10,1... | collective-permute-start | bytes 1720328 | tf_op jit(solution)/shard_map/ppermute | solution.py:259
  32.1 5.5 %collective-permute-done.w_prev = bf16[560,560]{1,0:T(8,128)(2,1)S(1)} collective-permute-done((bf16[560,560]{1,0:T(8,128)(2,1)S(1)}, bf16[560,560]{1,0:T(8,128)(2,1)S(1)}, u32[]{:S(2)}, u32[]{:S(2)}) %collective-permute-start) | collective-permute-done | bytes 627232 | tf_op jit(solution)/shard_map/ppermute | solution.py:259
  37.6 0.1 collective-permute-start.1
  37.7 2.7 %collective-permute-start.3 = (bf16[272,560]{1,0:T(8,128)(2,1)S(1)}, bf16[272,560]{1,0:T(8,128)(2,1)S(1)}, u32[]{:S(2)}, u32[]{:S(2)}) collective-permute-start(bf16[272,560]{1,0:T(8,128)(2,1)S(1)} %slice.17), channel_id=1, source_target_pairs={{0,12},{4,0},{8,4},{12,8},{1,13},{5,1},{9,5},{13,9},{2,14},{6,2},{... | collective-permute-start | bytes 913928 | tf_op jit(solution)/shard_map/ppermute | solution.py:259
  40.5 3.9 %collective-permute-start.8 = (bf16[560,560]{1,0:T(8,128)(2,1)S(1)}, bf16[560,560]{1,0:T(8,128)(2,1)S(1)}, u32[]{:S(2)}, u32[]{:S(2)}) collective-permute-start(bf16[560,560]{1,0:T(8,128)(2,1)S(1)} %shard_map.79.w0), channel_id=1, source_target_pairs={{0,16},{16,0},{1,17},{17,1},{2,18},{18,2},{3,19},{19,3},{4,20},{20... | collective-permute-start | bytes 1881608 | tf_op jit(solution)/shard_map/ppermute | solution.py:259
  44.4 0.2 collective-permute-start.10
  44.5 0.8 collective-permute-start.9
  45.3 1.5 %shard_map.80 = (bf16[1152,512]{1,0:T(8,128)(2,1)S(1)}, bf16[1152,512]{1,0:T(8,128)(2,1)S(1)}) custom-call(s32[5]{0:T(128)S(1)} %stack.19.idx, bf16[2240,128]{1,0:T(8,128)(2,1)S(1)} %bitcast.22, bf16[2240,128]{1,0:T(8,128)(2,1)S(1)} %collective-permute-done.4.t1, bf16[2240,128]{1,0:T(8,128)(2,1)S(1)} %collective-permute-done.5.t3, ...), custom_call_target="tpu_custom_call" | custom-call | bytes 10000000 | tf_op jit(solution)/shard_map/pallas_call | solution.py:38
  46.8 3.1 %collective-permute-start.11 = (bf16[288,560]{1,0:T(8,128)(2,1)S(1)}, bf16[288,560]{1,0:T(8,128)(2,1)S(1)}, u32[]{:S(2)}, u32[]{:S(2)}) collective-permute-start(bf16[288,560]{1,0:T(8,128)(2,1)S(1)} %collective-permute-done.1.w_lo), channel_id=1, source_target_pairs={{0,16},{16,0},{1,17},{17,1},{2,18},{18,2},{3,19},{19,3},{4,20},{20... | collective-permute-start | bytes 967688 | tf_op jit(solution)/shard_map/ppermute | solution.py:259
  49.9 0.5 collective-permute-start.20
  50.4 1.3 collective-permute-done.12.v_hi
  51.7 5.1 %shard_map.81 = (bf16[560,512]{1,0:T(8,128)(2,1)S(1)}, bf16[560,512]{1,0:T(8,128)(2,1)S(1)}, bf16[560,128]{1,0:T(8,128)(2,1)S(1)}) custom-call(s32[5]{0:T(128)S(1)} %stack.19.idx, bf16[560,560]{1,0:T(8,128)(2,1)S(1)} %shard_map.79.w0, bf16[560,560]{1,0:T(8,128)(2,1)S(1)} %collective-permute-done.w_prev, bf16[560,560]{1,0:T(8,128)(2,1)S(1)} %collective-permute-done.2.w_next, ...), custom_call_target="tpu_custom_call" | custom-call | flops 2569011200 | bytes 5000000 | tf_op jit(solution)/shard_map/pallas_call | solution.py:38
  56.9 0.1 collective-permute-start.16
  57.0 2.2 %collective-permute-start.15 = (bf16[560,128]{1,0:T(8,128)(2,1)S(1)}, bf16[560,128]{1,0:T(8,128)(2,1)S(1)}, u32[]{:S(2)}, u32[]{:S(2)}) collective-permute-start(bf16[560,128]{1,0:T(8,128)(2,1)S(1)} %get-tuple-element.47.s0), channel_id=1, source_target_pairs={{0,8},{4,12},{8,0},{12,4},{1,9},{5,13},{9,1},{13,5},{2,10},{6,14},... | collective-permute-start | bytes 430088 | tf_op jit(solution)/shard_map/ppermute | solution.py:259
  59.2 0.8 collective-permute-start.14
  59.9 0.7 collective-permute-start.13
  60.6 2.7 %collective-permute-done.15.s3 = bf16[560,128]{1,0:T(8,128)(2,1)S(1)} collective-permute-done((bf16[560,128]{1,0:T(8,128)(2,1)S(1)}, bf16[560,128]{1,0:T(8,128)(2,1)S(1)}, u32[]{:S(2)}, u32[]{:S(2)}) %collective-permute-start.15) | collective-permute-done | bytes 143392 | tf_op jit(solution)/shard_map/ppermute | solution.py:259
  63.3 3.3 %collective-permute-done.14.s2 = bf16[560,128]{1,0:T(8,128)(2,1)S(1)} collective-permute-done((bf16[560,128]{1,0:T(8,128)(2,1)S(1)}, bf16[560,128]{1,0:T(8,128)(2,1)S(1)}, u32[]{:S(2)}, u32[]{:S(2)}) %collective-permute-start.14) | collective-permute-done | bytes 143392 | tf_op jit(solution)/shard_map/ppermute | solution.py:259
  66.7 0.1 collective-permute-done.13.s1
  66.8 2.0 %shard_map.82 = (bf16[560,128]{1,0:T(8,128)(2,1)S(1)}, bf16[560,128]{1,0:T(8,128)(2,1)S(1)}, bf16[560,128]{1,0:T(8,128)(2,1)S(1)}, bf16[560,128]{1,0:T(8,128)(2,1)S(1)}, bf16[560,128]{1,0:T(8,128)(2,1)S(1)}) custom-call(s32[5]{0:T(128)S(1)} %stack.19.idx, bf16[560,128]{1,0:T(8,128)(2,1)S(1)} %get-tuple-element.47.s0, ...), custom_call_target="tpu_custom_call" | custom-call | flops 220200960 | bytes 4000000 | tf_op jit(solution)/shard_map/pallas_call | solution.py:38
  68.8 2.3 %collective-permute-start.19 = (bf16[560,128]{1,0:T(8,128)(2,1)S(1)}, bf16[560,128]{1,0:T(8,128)(2,1)S(1)}, u32[]{:S(2)}, u32[]{:S(2)}) collective-permute-start(bf16[560,128]{1,0:T(8,128)(2,1)S(1)} %get-tuple-element.50.s0), channel_id=1, source_target_pairs={{0,8},{4,12},{8,0},{12,4},{1,9},{5,13},{9,1},{13,5},{2,10},{6,14},... | collective-permute-start | bytes 430088 | tf_op jit(solution)/shard_map/ppermute | solution.py:259
  71.1 1.1 collective-permute-start.18
  72.1 0.4 collective-permute-start.17
  72.5 1.8 %collective-permute-done.19.s3 = bf16[560,128]{1,0:T(8,128)(2,1)S(1)} collective-permute-done((bf16[560,128]{1,0:T(8,128)(2,1)S(1)}, bf16[560,128]{1,0:T(8,128)(2,1)S(1)}, u32[]{:S(2)}, u32[]{:S(2)}) %collective-permute-start.19) | collective-permute-done | bytes 143392 | tf_op jit(solution)/shard_map/ppermute | solution.py:259
  74.3 4.5 %collective-permute-done.18.s2 = bf16[560,128]{1,0:T(8,128)(2,1)S(1)} collective-permute-done((bf16[560,128]{1,0:T(8,128)(2,1)S(1)}, bf16[560,128]{1,0:T(8,128)(2,1)S(1)}, u32[]{:S(2)}, u32[]{:S(2)}) %collective-permute-start.18) | collective-permute-done | bytes 143392 | tf_op jit(solution)/shard_map/ppermute | solution.py:259
  78.8 0.9 shard_map.83.d
  79.8 1.5 %collective-permute-start.21 = (bf16[560,512]{1,0:T(8,128)(2,1)S(1)}, bf16[560,512]{1,0:T(8,128)(2,1)S(1)}, u32[]{:S(2)}, u32[]{:S(2)}) collective-permute-start(bf16[560,512]{1,0:T(8,128)(2,1)S(1)} %shard_map.83.d), channel_id=1, source_target_pairs={{0,16},{16,0},{1,17},{17,1},{2,18},{18,2},{3,19},{19,3},{4,20},{20... | collective-permute-start | bytes 1720328 | tf_op jit(solution)/shard_map/ppermute | solution.py:259
  81.3 1.1 shard_map.84.first
  82.4 0.5 collective-permute-done.21.d
  82.9 2.9 %shard_map.85 = bf16[16,64,640]{2,1,0:T(8,128)(2,1)} custom-call(s32[5]{0:T(128)S(1)} %stack.19.idx, f32[1152,560]{1,0:T(8,128)S(1)} %shard_map.84.first, bf16[1152,512]{1,0:T(8,128)(2,1)S(1)} %collective-permute-done.20.t, bf16[560,512]{1,0:T(8,128)(2,1)S(1)} %collective-permute-done.21.d), custom_call_target="tpu_custom_call" | custom-call | flops 660602880 | bytes 5000000 | tf_op jit(solution)/shard_map/pallas_call | solution.py:38
  85.8 7.2 %all-to-all-start.1 = ((bf16[16,64,640]{2,1,0:T(8,128)(2,1)}), bf16[16,64,640]{2,1,0:T(8,128)(2,1)S(1)}, u32[]{:S(2)}, u32[]{:S(2)}) async-start(bf16[16,64,640]{2,1,0:T(8,128)(2,1)} %shard_map.85), calls=%async_computation.1 | async-start | bytes 2621440 | tf_op jit(solution)/shard_map/all_to_all | solution.py:369
  92.9 1.8 %collective-permute-start.22 = (bf16[560,128]{1,0:T(8,128)(2,1)S(1)}, bf16[560,128]{1,0:T(8,128)(2,1)S(1)}, u32[]{:S(2)}, u32[]{:S(2)}) collective-permute-start(bf16[560,128]{1,0:T(8,128)(2,1)S(1)} %get-tuple-element.55), channel_id=1, source_target_pairs={{0,3},{1,0},{2,1},{3,2},{4,7},{5,4},{6,5},{7,6},{8,11},{9,8},{10,9... | collective-permute-start | bytes 430088 | tf_op jit(solution)/shard_map/ppermute | solution.py:259
  94.7 1.5 %collective-permute-start.23 = (bf16[560,128]{1,0:T(8,128)(2,1)S(1)}, bf16[560,128]{1,0:T(8,128)(2,1)S(1)}, u32[]{:S(2)}, u32[]{:S(2)}) collective-permute-start(bf16[560,128]{1,0:T(8,128)(2,1)S(1)} %get-tuple-element.56), channel_id=1, source_target_pairs={{0,2},{1,3},{2,0},{3,1},{4,6},{5,7},{6,4},{7,5},{8,10},{9,11},{10,... | collective-permute-start | bytes 430088 | tf_op jit(solution)/shard_map/ppermute | solution.py:259
  96.2 1.4 %collective-permute-start.24 = (bf16[560,128]{1,0:T(8,128)(2,1)S(1)}, bf16[560,128]{1,0:T(8,128)(2,1)S(1)}, u32[]{:S(2)}, u32[]{:S(2)}) collective-permute-start(bf16[560,128]{1,0:T(8,128)(2,1)S(1)} %get-tuple-element.57), channel_id=1, source_target_pairs={{0,1},{1,2},{2,3},{3,0},{4,5},{5,6},{6,7},{7,4},{8,9},{9,10},{10,1... | collective-permute-start | bytes 430088 | tf_op jit(solution)/shard_map/ppermute | solution.py:259
  97.6 1.2 collective-permute-done.22.g1
  98.8 3.6 %collective-permute-done.23.g2 = bf16[560,128]{1,0:T(8,128)(2,1)S(1)} collective-permute-done((bf16[560,128]{1,0:T(8,128)(2,1)S(1)}, bf16[560,128]{1,0:T(8,128)(2,1)S(1)}, u32[]{:S(2)}, u32[]{:S(2)}) %collective-permute-start.23) | collective-permute-done | bytes 143392 | tf_op jit(solution)/shard_map/ppermute | solution.py:259
  102.4 1.4 %shard_map.86 = bf16[2240,128]{1,0:T(8,128)(2,1)} custom-call(s32[5]{0:T(128)S(1)} %stack.19.idx, bf16[560,128]{1,0:T(8,128)(2,1)S(1)} %get-tuple-element.54.g0, bf16[560,128]{1,0:T(8,128)(2,1)S(1)} %collective-permute-done.22.g1, bf16[560,128]{1,0:T(8,128)(2,1)S(1)} %collective-permute-done.23.g2, bf16[560,128]{1,0:T(8,128)(2,1)S(1)} %collective-permute-done.24.g3), custom_call_target="tpu_custom_call" | custom-call | tf_op jit(solution)/shard_map/pallas_call | solution.py:38
  103.8 9.2 %all-to-all-done.1.g = bf16[16,64,640]{2,1,0:T(8,128)(2,1)S(1)} async-done(((bf16[16,64,640]{2,1,0:T(8,128)(2,1)}), bf16[16,64,640]{2,1,0:T(8,128)(2,1)S(1)}, u32[]{:S(2)}, u32[]{:S(2)}) %all-to-all-start.1) | async-done | bytes 1310752 | tf_op jit(solution)/shard_map/all_to_all | solution.py:369
  113.0 0.2 shard_map.87
  113.2 0.3 collective-permute-start.28
  113.5 3.1 %collective-permute-start.27 = (bf16[64,640]{1,0:T(8,128)(2,1)S(1)}, bf16[64,640]{1,0:T(8,128)(2,1)S(1)}, u32[]{:S(2)}, u32[]{:S(2)}) collective-permute-start(bf16[64,640]{1,0:T(8,128)(2,1)S(1)} %shard_map.87), channel_id=1, source_target_pairs={{0,64},{1,65},{2,66},{3,67},{32,97},{33,98},{34,99},{35,96},{64,2}... | collective-permute-start | bytes 245768 | tf_op jit(solution)/shard_map/ppermute | solution.py:374
  116.6 0.2 collective-permute-start.26
  116.8 0.7 collective-permute-start.25
  117.5 3.2 %collective-permute-start.32 = (bf16[64,640]{1,0:T(8,128)(2,1)S(1)}, bf16[64,640]{1,0:T(8,128)(2,1)S(1)}, u32[]{:S(2)}, u32[]{:S(2)}) collective-permute-start(bf16[64,640]{1,0:T(8,128)(2,1)S(1)} %collective-permute-done.28.r3), channel_id=1, source_target_pairs={{0,16},{16,0},{1,17},{17,1},{2,18},{18,2},{3,19},{19,3},{4,20},{20... | collective-permute-start | bytes 245768 | tf_op jit(solution)/shard_map/ppermute | solution.py:259
  120.7 0.6 collective-permute-done.27.r2
  121.3 3.8 %collective-permute-start.31 = (bf16[64,640]{1,0:T(8,128)(2,1)S(1)}, bf16[64,640]{1,0:T(8,128)(2,1)S(1)}, u32[]{:S(2)}, u32[]{:S(2)}) collective-permute-start(bf16[64,640]{1,0:T(8,128)(2,1)S(1)} %collective-permute-done.27.r2), channel_id=1, source_target_pairs={{0,16},{16,0},{1,17},{17,1},{2,18},{18,2},{3,19},{19,3},{4,20},{20... | collective-permute-start | bytes 245768 | tf_op jit(solution)/shard_map/ppermute | solution.py:259
  125.1 2.4 %collective-permute-start.30 = (bf16[64,640]{1,0:T(8,128)(2,1)S(1)}, bf16[64,640]{1,0:T(8,128)(2,1)S(1)}, u32[]{:S(2)}, u32[]{:S(2)}) collective-permute-start(bf16[64,640]{1,0:T(8,128)(2,1)S(1)} %collective-permute-done.26.r1), channel_id=1, source_target_pairs={{0,16},{16,0},{1,17},{17,1},{2,18},{18,2},{3,19},{19,3},{4,20},{20... | collective-permute-start | bytes 245768 | tf_op jit(solution)/shard_map/ppermute | solution.py:259
  127.6 0.9 collective-permute-done.30.o1
  128.5 0.4 collective-permute-done.29.o0
  128.8 2.4 %shard_map.88 = f32[140,2240]{1,0:T(8,128)} custom-call(s32[5]{0:T(128)S(1)} %stack.19.idx, bf16[64,640]{1,0:T(8,128)(2,1)S(1)} %collective-permute-done.25.r0, bf16[64,640]{1,0:T(8,128)(2,1)S(1)} %collective-permute-done.26.r1, bf16[64,640]{1,0:T(8,128)(2,1)S(1)} %collective-permute-done.27.r2, bf16[64,640]{1,0:T(8,128)(2,1)S(1)} %collective-permute-done.28.r3, ...), custom_call_target="tpu_custom_call" | custom-call | tf_op jit(solution)/shard_map/pallas_call | solution.py:38
  (43 shorter events, 0.3 us)
Async XLA Ops:
  0.6 6.7 %copy-start.2 = (bf16[1,128,2240]{1,2,0:T(8,128)(2,1)S(1)}, bf16[1,128,2240]{1,2,0:T(8,128)(2,1)}, u32[]{:S(2)}) copy-start(bf16[1,128,2240]{1,2,0:T(8,128)(2,1)} %param.6) | copy-start | bytes 1720324
  2.9 5.7 %copy-start = (bf16[1,128,2240]{1,2,0:T(8,128)(2,1)S(1)}, bf16[1,128,2240]{1,2,0:T(8,128)(2,1)}, u32[]{:S(2)}) copy-start(bf16[1,128,2240]{1,2,0:T(8,128)(2,1)} %param.7) | copy-start | bytes 1720324
  2.9 5.7 %copy-start.1 = (bf16[1,128,2240]{1,2,0:T(8,128)(2,1)S(1)}, bf16[1,128,2240]{1,2,0:T(8,128)(2,1)}, u32[]{:S(2)}) copy-start(bf16[1,128,2240]{1,2,0:T(8,128)(2,1)} %param.8) | copy-start | bytes 1720324
  2.9 13.5 %all-to-all-start = ((bf16[4,140,560]{2,1,0:T(8,128)(2,1)}), bf16[4,140,560]{2,1,0:T(8,128)(2,1)S(1)}, u32[]{:S(2)}, u32[]{:S(2)}) async-start(bf16[4,140,560]{2,1,0:T(8,128)(2,1)} %shard_map.77), calls=%async_computation | async-start | bytes 1474560 | tf_op jit(solution)/shard_map/all_to_all | solution.py:285
  7.3 20.5 %collective-permute-start.4 = (bf16[2240,128]{1,0:T(8,128)(2,1)S(1)}, bf16[2240,128]{1,0:T(8,128)(2,1)S(1)}, u32[]{:S(2)}, u32[]{:S(2)}) collective-permute-start(bf16[2240,128]{1,0:T(8,128)(2,1)S(1)} %bitcast.20), channel_id=1, source_target_pairs={{0,3},{1,0},{2,1},{3,2},{4,7},{5,4},{6,5},{7,6},{8,11},{9,8},{10,9... | collective-permute-start | bytes 1720328 | tf_op jit(solution)/shard_map/ppermute | solution.py:259
  10.7 0.7 copy-start.3
  11.5 0.7 copy-start.5
  12.2 0.7 copy-start.7
  16.4 11.4 %copy-start.6 = (bf16[2,560,128]{2,1,0:T(8,128)(2,1)S(1)}, bf16[2,560,128]{2,1,0:T(8,128)(2,1)}, u32[]{:S(2)}) copy-start(bf16[2,560,128]{2,1,0:T(8,128)(2,1)} %copy-done.5) | copy-start | bytes 860164
  16.4 12.7 %collective-permute-start.5 = (bf16[2240,128]{1,0:T(8,128)(2,1)S(1)}, bf16[2240,128]{1,0:T(8,128)(2,1)S(1)}, u32[]{:S(2)}, u32[]{:S(2)}) collective-permute-start(bf16[2240,128]{1,0:T(8,128)(2,1)S(1)} %bitcast.21), channel_id=1, source_target_pairs={{0,1},{1,2},{2,3},{3,0},{4,5},{5,6},{6,7},{7,4},{8,9},{9,10},{10,1... | collective-permute-start | bytes 1720328 | tf_op jit(solution)/shard_map/ppermute | solution.py:259
  18.4 10.7 %copy-start.4 = (bf16[2,560,128]{2,1,0:T(8,128)(2,1)S(1)}, bf16[2,560,128]{2,1,0:T(8,128)(2,1)}, u32[]{:S(2)}) copy-start(bf16[2,560,128]{2,1,0:T(8,128)(2,1)} %copy-done.3) | copy-start | bytes 860164
  18.4 19.3 %collective-permute-start.2 = (bf16[560,560]{1,0:T(8,128)(2,1)S(1)}, bf16[560,560]{1,0:T(8,128)(2,1)S(1)}, u32[]{:S(2)}, u32[]{:S(2)}) collective-permute-start(bf16[560,560]{1,0:T(8,128)(2,1)S(1)} %shard_map.79.w0), channel_id=1, source_target_pairs={{0,12},{4,0},{8,4},{12,8},{1,13},{5,1},{9,5},{13,9},{2,14},{6,2},{... | collective-permute-start | bytes 1881608 | tf_op jit(solution)/shard_map/ppermute | solution.py:259
  21.3 16.3 %collective-permute-start = (bf16[560,560]{1,0:T(8,128)(2,1)S(1)}, bf16[560,560]{1,0:T(8,128)(2,1)S(1)}, u32[]{:S(2)}, u32[]{:S(2)}) collective-permute-start(bf16[560,560]{1,0:T(8,128)(2,1)S(1)} %shard_map.79.w0), channel_id=1, source_target_pairs={{0,4},{4,8},{8,12},{12,0},{1,5},{5,9},{9,13},{13,1},{2,6},{6,10},{... | collective-permute-start | bytes 1881608 | tf_op jit(solution)/shard_map/ppermute | solution.py:259
  27.9 16.5 %collective-permute-start.7 = (bf16[2240,128]{1,0:T(8,128)(2,1)S(1)}, bf16[2240,128]{1,0:T(8,128)(2,1)S(1)}, u32[]{:S(2)}, u32[]{:S(2)}) collective-permute-start(bf16[2240,128]{1,0:T(8,128)(2,1)S(1)} %pad_maximum_fusion.1), channel_id=1, source_target_pairs={{0,3},{1,0},{2,1},{3,2},{4,7},{5,4},{6,5},{7,6},{8,11},{9,8},{10,9... | collective-permute-start | bytes 1720328 | tf_op jit(solution)/shard_map/ppermute | solution.py:259
  29.2 15.3 %collective-permute-start.6 = (bf16[2240,128]{1,0:T(8,128)(2,1)S(1)}, bf16[2240,128]{1,0:T(8,128)(2,1)S(1)}, u32[]{:S(2)}, u32[]{:S(2)}) collective-permute-start(bf16[2240,128]{1,0:T(8,128)(2,1)S(1)} %pad_maximum_fusion), channel_id=1, source_target_pairs={{0,1},{1,2},{2,3},{3,0},{4,5},{5,6},{6,7},{7,4},{8,9},{9,10},{10,1... | collective-permute-start | bytes 1720328 | tf_op jit(solution)/shard_map/ppermute | solution.py:259
  37.6 9.2 %collective-permute-start.1 = (bf16[288,560]{1,0:T(8,128)(2,1)S(1)}, bf16[288,560]{1,0:T(8,128)(2,1)S(1)}, u32[]{:S(2)}, u32[]{:S(2)}) collective-permute-start(bf16[288,560]{1,0:T(8,128)(2,1)S(1)} %slice.16), channel_id=1, source_target_pairs={{0,4},{4,8},{8,12},{12,0},{1,5},{5,9},{9,13},{13,1},{2,6},{6,10},{... | collective-permute-start | bytes 967688 | tf_op jit(solution)/shard_map/ppermute | solution.py:259
  37.7 9.1 %collective-permute-start.3 = (bf16[272,560]{1,0:T(8,128)(2,1)S(1)}, bf16[272,560]{1,0:T(8,128)(2,1)S(1)}, u32[]{:S(2)}, u32[]{:S(2)}) collective-permute-start(bf16[272,560]{1,0:T(8,128)(2,1)S(1)} %slice.17), channel_id=1, source_target_pairs={{0,12},{4,0},{8,4},{12,8},{1,13},{5,1},{9,5},{13,9},{2,14},{6,2},{... | collective-permute-start | bytes 913928 | tf_op jit(solution)/shard_map/ppermute | solution.py:259
  40.5 9.4 %collective-permute-start.8 = (bf16[560,560]{1,0:T(8,128)(2,1)S(1)}, bf16[560,560]{1,0:T(8,128)(2,1)S(1)}, u32[]{:S(2)}, u32[]{:S(2)}) collective-permute-start(bf16[560,560]{1,0:T(8,128)(2,1)S(1)} %shard_map.79.w0), channel_id=1, source_target_pairs={{0,16},{16,0},{1,17},{17,1},{2,18},{18,2},{3,19},{19,3},{4,20},{20... | collective-permute-start | bytes 1881608 | tf_op jit(solution)/shard_map/ppermute | solution.py:259
  44.4 6.0 %collective-permute-start.10 = (bf16[560,560]{1,0:T(8,128)(2,1)S(1)}, bf16[560,560]{1,0:T(8,128)(2,1)S(1)}, u32[]{:S(2)}, u32[]{:S(2)}) collective-permute-start(bf16[560,560]{1,0:T(8,128)(2,1)S(1)} %collective-permute-done.2.w_next), channel_id=1, source_target_pairs={{0,16},{16,0},{1,17},{17,1},{2,18},{18,2},{3,19},{19,3},{4,20},{20... | collective-permute-start | bytes 1881608 | tf_op jit(solution)/shard_map/ppermute | solution.py:259
  44.5 5.9 %collective-permute-start.9 = (bf16[560,560]{1,0:T(8,128)(2,1)S(1)}, bf16[560,560]{1,0:T(8,128)(2,1)S(1)}, u32[]{:S(2)}, u32[]{:S(2)}) collective-permute-start(bf16[560,560]{1,0:T(8,128)(2,1)S(1)} %collective-permute-done.w_prev), channel_id=1, source_target_pairs={{0,16},{16,0},{1,17},{17,1},{2,18},{18,2},{3,19},{19,3},{4,20},{20... | collective-permute-start | bytes 1881608 | tf_op jit(solution)/shard_map/ppermute | solution.py:259
  46.8 10.0 %copy-start.8 = (bf16[2,560,128]{2,1,0:T(8,128)(2,1)S(1)}, bf16[2,560,128]{2,1,0:T(8,128)(2,1)}, u32[]{:S(2)}) copy-start(bf16[2,560,128]{2,1,0:T(8,128)(2,1)} %copy-done.7) | copy-start | bytes 860164
  46.8 4.9 %collective-permute-start.11 = (bf16[288,560]{1,0:T(8,128)(2,1)S(1)}, bf16[288,560]{1,0:T(8,128)(2,1)S(1)}, u32[]{:S(2)}, u32[]{:S(2)}) collective-permute-start(bf16[288,560]{1,0:T(8,128)(2,1)S(1)} %collective-permute-done.1.w_lo), channel_id=1, source_target_pairs={{0,16},{16,0},{1,17},{17,1},{2,18},{18,2},{3,19},{19,3},{4,20},{20... | collective-permute-start | bytes 967688 | tf_op jit(solution)/shard_map/ppermute | solution.py:259
  49.9 1.8 %collective-permute-start.12 = (bf16[272,560]{1,0:T(8,128)(2,1)S(1)}, bf16[272,560]{1,0:T(8,128)(2,1)S(1)}, u32[]{:S(2)}, u32[]{:S(2)}) collective-permute-start(bf16[272,560]{1,0:T(8,128)(2,1)S(1)} %collective-permute-done.3.w_hi), channel_id=1, source_target_pairs={{0,16},{16,0},{1,17},{17,1},{2,18},{18,2},{3,19},{19,3},{4,20},{20... | collective-permute-start | bytes 913928 | tf_op jit(solution)/shard_map/ppermute | solution.py:259
  49.9 32.5 %collective-permute-start.20 = (bf16[1152,512]{1,0:T(8,128)(2,1)S(1)}, bf16[1152,512]{1,0:T(8,128)(2,1)S(1)}, u32[]{:S(2)}, u32[]{:S(2)}) collective-permute-start(bf16[1152,512]{1,0:T(8,128)(2,1)S(1)} %get-tuple-element.53), channel_id=1, source_target_pairs={{0,16},{16,0},{1,17},{17,1},{2,18},{18,2},{3,19},{19,3},{4,20},{20... | collective-permute-start | bytes 3538952 | tf_op jit(solution)/shard_map/ppermute | solution.py:259
  56.9 10.0 %collective-permute-start.16 = (bf16[2,560,128]{2,1,0:T(8,128)(2,1)S(1)}, bf16[2,560,128]{2,1,0:T(8,128)(2,1)S(1)}, u32[]{:S(2)}, u32[]{:S(2)}) collective-permute-start(bf16[2,560,128]{2,1,0:T(8,128)(2,1)S(1)} %copy-done.8), channel_id=1, source_target_pairs={{0,2},{1,3},{2,0},{3,1},{4,6},{5,7},{6,4},{7,5},{8,10},{9,11},{10,... | collective-permute-start | bytes 860168 | tf_op jit(solution)/shard_map/ppermute | solution.py:259
  57.0 6.4 %collective-permute-start.15 = (bf16[560,128]{1,0:T(8,128)(2,1)S(1)}, bf16[560,128]{1,0:T(8,128)(2,1)S(1)}, u32[]{:S(2)}, u32[]{:S(2)}) collective-permute-start(bf16[560,128]{1,0:T(8,128)(2,1)S(1)} %get-tuple-element.47.s0), channel_id=1, source_target_pairs={{0,8},{4,12},{8,0},{12,4},{1,9},{5,13},{9,1},{13,5},{2,10},{6,14},... | collective-permute-start | bytes 430088 | tf_op jit(solution)/shard_map/ppermute | solution.py:259
  59.2 7.5 %collective-permute-start.14 = (bf16[560,128]{1,0:T(8,128)(2,1)S(1)}, bf16[560,128]{1,0:T(8,128)(2,1)S(1)}, u32[]{:S(2)}, u32[]{:S(2)}) collective-permute-start(bf16[560,128]{1,0:T(8,128)(2,1)S(1)} %get-tuple-element.47.s0), channel_id=1, source_target_pairs={{0,12},{4,0},{8,4},{12,8},{1,13},{5,1},{9,5},{13,9},{2,14},{6,2},{... | collective-permute-start | bytes 430088 | tf_op jit(solution)/shard_map/ppermute | solution.py:259
  59.9 6.9 %collective-permute-start.13 = (bf16[560,128]{1,0:T(8,128)(2,1)S(1)}, bf16[560,128]{1,0:T(8,128)(2,1)S(1)}, u32[]{:S(2)}, u32[]{:S(2)}) collective-permute-start(bf16[560,128]{1,0:T(8,128)(2,1)S(1)} %get-tuple-element.47.s0), channel_id=1, source_target_pairs={{0,4},{4,8},{8,12},{12,0},{1,5},{5,9},{9,13},{13,1},{2,6},{6,10},{... | collective-permute-start | bytes 430088 | tf_op jit(solution)/shard_map/ppermute | solution.py:259
  68.8 5.5 %collective-permute-start.19 = (bf16[560,128]{1,0:T(8,128)(2,1)S(1)}, bf16[560,128]{1,0:T(8,128)(2,1)S(1)}, u32[]{:S(2)}, u32[]{:S(2)}) collective-permute-start(bf16[560,128]{1,0:T(8,128)(2,1)S(1)} %get-tuple-element.50.s0), channel_id=1, source_target_pairs={{0,8},{4,12},{8,0},{12,4},{1,9},{5,13},{9,1},{13,5},{2,10},{6,14},... | collective-permute-start | bytes 430088 | tf_op jit(solution)/shard_map/ppermute | solution.py:259
  71.1 7.8 %collective-permute-start.18 = (bf16[560,128]{1,0:T(8,128)(2,1)S(1)}, bf16[560,128]{1,0:T(8,128)(2,1)S(1)}, u32[]{:S(2)}, u32[]{:S(2)}) collective-permute-start(bf16[560,128]{1,0:T(8,128)(2,1)S(1)} %get-tuple-element.50.s0), channel_id=1, source_target_pairs={{0,12},{4,0},{8,4},{12,8},{1,13},{5,1},{9,5},{13,9},{2,14},{6,2},{... | collective-permute-start | bytes 430088 | tf_op jit(solution)/shard_map/ppermute | solution.py:259
  72.1 6.7 %collective-permute-start.17 = (bf16[560,128]{1,0:T(8,128)(2,1)S(1)}, bf16[560,128]{1,0:T(8,128)(2,1)S(1)}, u32[]{:S(2)}, u32[]{:S(2)}) collective-permute-start(bf16[560,128]{1,0:T(8,128)(2,1)S(1)} %get-tuple-element.50.s0), channel_id=1, source_target_pairs={{0,4},{4,8},{8,12},{12,0},{1,5},{5,9},{9,13},{13,1},{2,6},{6,10},{... | collective-permute-start | bytes 430088 | tf_op jit(solution)/shard_map/ppermute | solution.py:259
  79.8 3.1 %collective-permute-start.21 = (bf16[560,512]{1,0:T(8,128)(2,1)S(1)}, bf16[560,512]{1,0:T(8,128)(2,1)S(1)}, u32[]{:S(2)}, u32[]{:S(2)}) collective-permute-start(bf16[560,512]{1,0:T(8,128)(2,1)S(1)} %shard_map.83.d), channel_id=1, source_target_pairs={{0,16},{16,0},{1,17},{17,1},{2,18},{18,2},{3,19},{19,3},{4,20},{20... | collective-permute-start | bytes 1720328 | tf_op jit(solution)/shard_map/ppermute | solution.py:259
  85.8 27.3 %all-to-all-start.1 = ((bf16[16,64,640]{2,1,0:T(8,128)(2,1)}), bf16[16,64,640]{2,1,0:T(8,128)(2,1)S(1)}, u32[]{:S(2)}, u32[]{:S(2)}) async-start(bf16[16,64,640]{2,1,0:T(8,128)(2,1)} %shard_map.85), calls=%async_computation.1 | async-start | bytes 2621440 | tf_op jit(solution)/shard_map/all_to_all | solution.py:369
  92.9 5.9 %collective-permute-start.22 = (bf16[560,128]{1,0:T(8,128)(2,1)S(1)}, bf16[560,128]{1,0:T(8,128)(2,1)S(1)}, u32[]{:S(2)}, u32[]{:S(2)}) collective-permute-start(bf16[560,128]{1,0:T(8,128)(2,1)S(1)} %get-tuple-element.55), channel_id=1, source_target_pairs={{0,3},{1,0},{2,1},{3,2},{4,7},{5,4},{6,5},{7,6},{8,11},{9,8},{10,9... | collective-permute-start | bytes 430088 | tf_op jit(solution)/shard_map/ppermute | solution.py:259
  94.7 7.7 %collective-permute-start.23 = (bf16[560,128]{1,0:T(8,128)(2,1)S(1)}, bf16[560,128]{1,0:T(8,128)(2,1)S(1)}, u32[]{:S(2)}, u32[]{:S(2)}) collective-permute-start(bf16[560,128]{1,0:T(8,128)(2,1)S(1)} %get-tuple-element.56), channel_id=1, source_target_pairs={{0,2},{1,3},{2,0},{3,1},{4,6},{5,7},{6,4},{7,5},{8,10},{9,11},{10,... | collective-permute-start | bytes 430088 | tf_op jit(solution)/shard_map/ppermute | solution.py:259
  96.2 6.3 %collective-permute-start.24 = (bf16[560,128]{1,0:T(8,128)(2,1)S(1)}, bf16[560,128]{1,0:T(8,128)(2,1)S(1)}, u32[]{:S(2)}, u32[]{:S(2)}) collective-permute-start(bf16[560,128]{1,0:T(8,128)(2,1)S(1)} %get-tuple-element.57), channel_id=1, source_target_pairs={{0,1},{1,2},{2,3},{3,0},{4,5},{5,6},{6,7},{7,4},{8,9},{9,10},{10,1... | collective-permute-start | bytes 430088 | tf_op jit(solution)/shard_map/ppermute | solution.py:259
  113.2 4.3 %collective-permute-start.28 = (bf16[64,640]{1,0:T(8,128)(2,1)S(1)}, bf16[64,640]{1,0:T(8,128)(2,1)S(1)}, u32[]{:S(2)}, u32[]{:S(2)}) collective-permute-start(bf16[64,640]{1,0:T(8,128)(2,1)S(1)} %shard_map.87), channel_id=1, source_target_pairs={{0,96},{1,97},{2,98},{3,99},{32,1},{33,2},{34,3},{35,0},{64,34},{6... | collective-permute-start | bytes 245768 | tf_op jit(solution)/shard_map/ppermute | solution.py:374
  113.5 7.8 %collective-permute-start.27 = (bf16[64,640]{1,0:T(8,128)(2,1)S(1)}, bf16[64,640]{1,0:T(8,128)(2,1)S(1)}, u32[]{:S(2)}, u32[]{:S(2)}) collective-permute-start(bf16[64,640]{1,0:T(8,128)(2,1)S(1)} %shard_map.87), channel_id=1, source_target_pairs={{0,64},{1,65},{2,66},{3,67},{32,97},{33,98},{34,99},{35,96},{64,2}... | collective-permute-start | bytes 245768 | tf_op jit(solution)/shard_map/ppermute | solution.py:374
  116.6 8.5 %collective-permute-start.26 = (bf16[64,640]{1,0:T(8,128)(2,1)S(1)}, bf16[64,640]{1,0:T(8,128)(2,1)S(1)}, u32[]{:S(2)}, u32[]{:S(2)}) collective-permute-start(bf16[64,640]{1,0:T(8,128)(2,1)S(1)} %shard_map.87), channel_id=1, source_target_pairs={{0,32},{1,33},{2,34},{3,35},{32,65},{33,66},{34,67},{35,64},{64,98... | collective-permute-start | bytes 245768 | tf_op jit(solution)/shard_map/ppermute | solution.py:374
  116.8 10.7 %collective-permute-start.25 = (bf16[64,640]{1,0:T(8,128)(2,1)S(1)}, bf16[64,640]{1,0:T(8,128)(2,1)S(1)}, u32[]{:S(2)}, u32[]{:S(2)}) collective-permute-start(bf16[64,640]{1,0:T(8,128)(2,1)S(1)} %shard_map.87), channel_id=1, source_target_pairs={{0,0},{1,1},{2,2},{3,3},{32,33},{33,34},{34,35},{35,32},{64,66},{6... | collective-permute-start | bytes 245768 | tf_op jit(solution)/shard_map/ppermute | solution.py:374
  117.5 10.1 %collective-permute-start.32 = (bf16[64,640]{1,0:T(8,128)(2,1)S(1)}, bf16[64,640]{1,0:T(8,128)(2,1)S(1)}, u32[]{:S(2)}, u32[]{:S(2)}) collective-permute-start(bf16[64,640]{1,0:T(8,128)(2,1)S(1)} %collective-permute-done.28.r3), channel_id=1, source_target_pairs={{0,16},{16,0},{1,17},{17,1},{2,18},{18,2},{3,19},{19,3},{4,20},{20... | collective-permute-start | bytes 245768 | tf_op jit(solution)/shard_map/ppermute | solution.py:259
  121.3 6.3 %collective-permute-start.31 = (bf16[64,640]{1,0:T(8,128)(2,1)S(1)}, bf16[64,640]{1,0:T(8,128)(2,1)S(1)}, u32[]{:S(2)}, u32[]{:S(2)}) collective-permute-start(bf16[64,640]{1,0:T(8,128)(2,1)S(1)} %collective-permute-done.27.r2), channel_id=1, source_target_pairs={{0,16},{16,0},{1,17},{17,1},{2,18},{18,2},{3,19},{19,3},{4,20},{20... | collective-permute-start | bytes 245768 | tf_op jit(solution)/shard_map/ppermute | solution.py:259
  125.1 3.3 %collective-permute-start.30 = (bf16[64,640]{1,0:T(8,128)(2,1)S(1)}, bf16[64,640]{1,0:T(8,128)(2,1)S(1)}, u32[]{:S(2)}, u32[]{:S(2)}) collective-permute-start(bf16[64,640]{1,0:T(8,128)(2,1)S(1)} %collective-permute-done.26.r1), channel_id=1, source_target_pairs={{0,16},{16,0},{1,17},{17,1},{2,18},{18,2},{3,19},{19,3},{4,20},{20... | collective-permute-start | bytes 245768 | tf_op jit(solution)/shard_map/ppermute | solution.py:259
  127.6 1.3 collective-permute-start.29

commit v5 on v4

--- a/solution.py
+++ b/solution.py
@@ -74,7 +74,9 @@
 
 
 def merge_weights(g, full):
-    full[...] = jnp.concatenate([g[k].astype(F32) for k in range(NX)], axis=0).T.astype(BF)
+    w = jnp.concatenate([g[k].astype(F32) for k in range(NX)], axis=0).T
+    full[:, :GW] = w.astype(BF)
+    full[:, GW:] = jnp.zeros((GW, PL - GW), BF)
 
 
 def run_copies(pairs, sems):
@@ -116,23 +118,26 @@
     for i, off in enumerate((0, 3, 1, 2)):
         block = lax.rem(idx[2] + off, NY)
         start = pl.multiple_of(block * GW, 16)
+        at = PL * i
         for d, t in ((0, t0), (1, t1), (3, t3)):
-            tbuf[i, :, ROWS * d : ROWS * (d + 1)] = t[pl.ds(start, GW)]
+            tbuf[at : at + GW, ROWS * d : ROWS * (d + 1)] = t[pl.ds(start, GW)]
         near = pl.multiple_of(lax.rem(block, 2) * GW, 16)
         for lo, t in ((True, t2_lo), (False, t2_hi)):
 
             @pl.when((block < 2) == lo)
             def _():
-                tbuf[i, :, 2 * ROWS : 3 * ROWS] = t[pl.ds(near, GW)]
+                tbuf[at : at + GW, 2 * ROWS : 3 * ROWS] = t[pl.ds(near, GW)]
+
+        tbuf[at + GW : at + PL] = jnp.zeros((PL - GW, TOK), BF)
 
     c = idx[1]
-    for g, ws in ((c, (w0, w_prev, w_next)), (1 - c, (v0, v_prev, v_next))):
-        lo, hi = (w_lo, w_hi) if ws[0] is w0 else (v_lo, v_hi)
-        far = jnp.concatenate([lo[...], hi[...]], axis=0)
-        total = nn(far, tbuf[3])
-        for i, w in enumerate(ws):
-            total = total + nn(w[...], tbuf[i])
-        acc[g] = total.astype(BF)
+    for g, ws, halves in (
+        (c, (w0, w_prev, w_next), (w_lo, w_hi)),
+        (1 - c, (v0, v_prev, v_next), (v_lo, v_hi)),
+    ):
+        far = jnp.concatenate([r[...] for r in halves], axis=0)
+        rows = jnp.concatenate([w[...] for w in ws] + [far], axis=1)
+        acc[g] = nn(rows, tbuf[...]).astype(BF)
     live = live_mask(idx, idx[3])
     one = jnp.ones((1, TOK), F32)
     for h in range(GH):
@@ -293,7 +298,7 @@
     )
     merged, *qc = lax.optimization_barrier((merged, *qc))
     t_late, _ = lax.optimization_barrier((t_own, merged))
-    w_own = call(merge_weights, sds((GW, GW)), [VMEM], (merged,))
+    w_own = call(merge_weights, sds((GW, PL)), [VMEM], (merged,))
     w_prev = shift(w_own, "y", 1)
     w_next = shift(w_own, "y", -1)
     t_prev = shift(t_late, "x", 1)
@@ -319,12 +324,12 @@
         [sds((GW, TOK)), sds((GW, TOK)), sds((GW, 128))],
         [SMEM] + [VMEM] * 15,
         (idx, *ws, *[swap(w) for w in ws], *ts),
-        scratch=[pltpu.VMEM((NY, GW, TOK), BF), pltpu.VMEM((2, GW, TOK), BF)],
+        scratch=[pltpu.VMEM((NY * PL, TOK), BF), pltpu.VMEM((2, GW, TOK), BF)],
         vmem=16,
         flops=4 * TOK * D * GW,
         nbytes=5_000_000,
     )
-    summ, far = lax.optimization_barrier((summ, qc[2]))
+    far, _, _ = lax.optimization_barrier((qc[2], t_lo, t_hi))
     parts = sum_parts(summ)
     q_in = (qc[0], t_hi, shift(far, "x", 2), t_lo)
     g_oth = swap(g_oth)

time: 134 us -> 132 us (0.985)
  transfers between devices with their start and end apart: 35 -> 35, of which waited for: 16 -> 18; matrix products, arithmetic and copies ran while one was open for 0% -> 0% of each run, Pallas kernels for 11% -> 11%
where the time goes in v5:
time: 132 us; the launch traced here: 130 us
  starting transfers between devices  59.2 us (45%)
  waiting for transfers between devices  45.6 us (35%)
  Pallas kernels  21.6 us (16%)
  local copies, waits for them, and re-layouts  2.33 us (2%)
  between operations  1.55 us (1%)
    ppermute x29, starting transfers between devices, shift(): return lax.ppermute(v, axis, [(i, (i + d) % n) for i in range(n)])  43.6 us
    ppermute x29, waiting for transfers between devices, shift(): return lax.ppermute(v, axis, [(i, (i + d) % n) for i in range(n)])  32.5 us
    pallas_call x12, Pallas kernels, call(): pl.pallas_call(body, out_shape=out_shape, in_specs=in_specs, out_specs=ja...  21.6 us
    all_to_all x1, waiting for transfers between devices, per_device(): part = lax.all_to_all(part, ('z', 'y'), 0, 0, tiled=True)  9.51 us
    all_to_all x1, starting transfers between devices, per_device(): part = lax.all_to_all(part, ('z', 'y'), 0, 0, tiled=True)  6.94 us
    all_to_all x1, starting transfers between devices, per_device(): merged = lax.all_to_all(pieces, 'x', 0, 0, tiled=True)  4.35 us
    ppermute x4, starting transfers between devices, per_device(): lax.ppermute(rows, ('z', 'x'), [(z_at * NX + x_at, (z_at + s) % NZ * NX +...  4.29 us
    all_to_all x1, waiting for transfers between devices, per_device(): merged = lax.all_to_all(pieces, 'x', 0, 0, tiled=True)  3.54 us
  transfers between devices with their start and end apart: 35, of which 18 were waited for; matrix products, arithmetic and copies ran while one was open for 0% of the time, Pallas kernels for 11%

profile of v5, /device:TPU:7, one launch (start us, length us, event | category | flops | bytes accessed | tf_op | source)
XLA Modules:
  0.0 130.3 jit_solution(459816399719614301)
XLA Ops:
  0.6 2.3 %shard_map.77 = bf16[4,140,560]{2,1,0:T(8,128)(2,1)} custom-call(bf16[140,2240]{1,0:T(8,128)(2,1)} %wk.1, bf16[140,2240]{1,0:T(8,128)(2,1)} %wv.1), custom_call_target="tpu_custom_call" | custom-call | tf_op jit(solution)/shard_map/pallas_call | solution.py:38
  2.9 4.4 %all-to-all-start = ((bf16[4,140,560]{2,1,0:T(8,128)(2,1)}), bf16[4,140,560]{2,1,0:T(8,128)(2,1)S(1)}, u32[]{:S(2)}, u32[]{:S(2)}) async-start(bf16[4,140,560]{2,1,0:T(8,128)(2,1)} %shard_map.77), calls=%async_computation | async-start | bytes 1474560 | tf_op jit(solution)/shard_map/all_to_all | solution.py:290
  7.3 0.6 collective-permute-start.4
  8.5 0.1 stack.19.idx
  8.6 2.1 %shard_map.78 = (bf16[2,560,128]{2,1,0:T(8,128)(2,1)S(1)}, bf16[2,560,128]{2,1,0:T(8,128)(2,1)S(1)}, bf16[2,560,128]{2,1,0:T(8,128)(2,1)S(1)}, bf16[2,560,128]{2,1,0:T(8,128)(2,1)S(1)}) custom-call(s32[5]{0:T(128)S(1)} %stack.19.idx, bf16[2240,128]{1,0:T(8,128)(2,1)S(1)} %bitcast.18, bf16[2240,128]{1,0:T(8,128)(2,1)S(1)} %bitcast.19), custom_call_target="tpu_custom_call" | custom-call | tf_op jit(solution)/shard_map/pallas_call | solution.py:38
  10.7 0.7 copy-done.3
  11.5 0.7 copy-done.5
  12.2 0.7 copy-done.7
  12.9 3.5 %all-to-all-done.g = bf16[4,140,560]{2,1,0:T(8,128)(2,1)S(1)} async-done(((bf16[4,140,560]{2,1,0:T(8,128)(2,1)}), bf16[4,140,560]{2,1,0:T(8,128)(2,1)S(1)}, u32[]{:S(2)}, u32[]{:S(2)}) %all-to-all-start) | async-done | bytes 627232 | tf_op jit(solution)/shard_map/all_to_all | solution.py:290
  16.4 1.7 %collective-permute-start.5 = (bf16[2240,128]{1,0:T(8,128)(2,1)S(1)}, bf16[2240,128]{1,0:T(8,128)(2,1)S(1)}, u32[]{:S(2)}, u32[]{:S(2)}) collective-permute-start(bf16[2240,128]{1,0:T(8,128)(2,1)S(1)} %bitcast.21), channel_id=1, source_target_pairs={{0,1},{1,2},{2,3},{3,0},{4,5},{5,6},{6,7},{7,4},{8,9},{9,10},{10,1... | collective-permute-start | bytes 1720328 | tf_op jit(solution)/shard_map/ppermute | solution.py:264
  18.1 0.3 shard_map.79.w0
  18.4 2.8 %collective-permute-start.2 = (bf16[560,640]{1,0:T(8,128)(2,1)S(1)}, bf16[560,640]{1,0:T(8,128)(2,1)S(1)}, u32[]{:S(2)}, u32[]{:S(2)}) collective-permute-start(bf16[560,640]{1,0:T(8,128)(2,1)S(1)} %shard_map.79.w0), channel_id=1, source_target_pairs={{0,12},{4,0},{8,4},{12,8},{1,13},{5,1},{9,5},{13,9},{2,14},{6,2},{... | collective-permute-start | bytes 2150408 | tf_op jit(solution)/shard_map/ppermute | solution.py:264
  21.3 6.5 %collective-permute-done.4.t1 = bf16[2240,128]{1,0:T(8,128)(2,1)S(1)} collective-permute-done((bf16[2240,128]{1,0:T(8,128)(2,1)S(1)}, bf16[2240,128]{1,0:T(8,128)(2,1)S(1)}, u32[]{:S(2)}, u32[]{:S(2)}) %collective-permute-start.4) | collective-permute-done | bytes 573472 | tf_op jit(solution)/shard_map/ppermute | solution.py:264
  27.9 1.3 collective-permute-start.7
  29.2 2.9 %collective-permute-start.6 = (bf16[2240,128]{1,0:T(8,128)(2,1)S(1)}, bf16[2240,128]{1,0:T(8,128)(2,1)S(1)}, u32[]{:S(2)}, u32[]{:S(2)}) collective-permute-start(bf16[2240,128]{1,0:T(8,128)(2,1)S(1)} %pad_maximum_fusion), channel_id=1, source_target_pairs={{0,1},{1,2},{2,3},{3,0},{4,5},{5,6},{6,7},{7,4},{8,9},{9,10},{10,1... | collective-permute-start | bytes 1720328 | tf_op jit(solution)/shard_map/ppermute | solution.py:264
  32.1 3.1 %collective-permute-start.8 = (bf16[560,640]{1,0:T(8,128)(2,1)S(1)}, bf16[560,640]{1,0:T(8,128)(2,1)S(1)}, u32[]{:S(2)}, u32[]{:S(2)}) collective-permute-start(bf16[560,640]{1,0:T(8,128)(2,1)S(1)} %shard_map.79.w0), channel_id=1, source_target_pairs={{0,16},{16,0},{1,17},{17,1},{2,18},{18,2},{3,19},{19,3},{4,20},{20... | collective-permute-start | bytes 2150408 | tf_op jit(solution)/shard_map/ppermute | solution.py:264
  35.2 2.4 %collective-permute-done.w_prev = bf16[560,640]{1,0:T(8,128)(2,1)S(1)} collective-permute-done((bf16[560,640]{1,0:T(8,128)(2,1)S(1)}, bf16[560,640]{1,0:T(8,128)(2,1)S(1)}, u32[]{:S(2)}, u32[]{:S(2)}) %collective-permute-start) | collective-permute-done | bytes 716832 | tf_op jit(solution)/shard_map/ppermute | solution.py:264
  37.8 2.7 %collective-permute-start.3 = (bf16[272,640]{1,0:T(8,128)(2,1)S(1)}, bf16[272,640]{1,0:T(8,128)(2,1)S(1)}, u32[]{:S(2)}, u32[]{:S(2)}) collective-permute-start(bf16[272,640]{1,0:T(8,128)(2,1)S(1)} %slice.17), channel_id=1, source_target_pairs={{0,12},{4,0},{8,4},{12,8},{1,13},{5,1},{9,5},{13,9},{2,14},{6,2},{... | collective-permute-start | bytes 1044488 | tf_op jit(solution)/shard_map/ppermute | solution.py:264
  40.5 1.6 %collective-permute-done.7.t2_hi.q1 = bf16[2240,128]{1,0:T(8,128)(2,1)S(1)} collective-permute-done((bf16[2240,128]{1,0:T(8,128)(2,1)S(1)}, bf16[2240,128]{1,0:T(8,128)(2,1)S(1)}, u32[]{:S(2)}, u32[]{:S(2)}) %collective-permute-start.7) | collective-permute-done | bytes 573472 | tf_op jit(solution)/shard_map/ppermute | solution.py:264
  42.1 2.5 %collective-permute-start.10 = (bf16[560,640]{1,0:T(8,128)(2,1)S(1)}, bf16[560,640]{1,0:T(8,128)(2,1)S(1)}, u32[]{:S(2)}, u32[]{:S(2)}) collective-permute-start(bf16[560,640]{1,0:T(8,128)(2,1)S(1)} %collective-permute-done.2.w_next), channel_id=1, source_target_pairs={{0,16},{16,0},{1,17},{17,1},{2,18},{18,2},{3,19},{19,3},{4,20},{20... | collective-permute-start | bytes 2150408 | tf_op jit(solution)/shard_map/ppermute | solution.py:264
  44.5 0.8 collective-permute-start.9
  45.3 1.5 %shard_map.80 = (bf16[1152,512]{1,0:T(8,128)(2,1)S(1)}, bf16[1152,512]{1,0:T(8,128)(2,1)S(1)}) custom-call(s32[5]{0:T(128)S(1)} %stack.19.idx, bf16[2240,128]{1,0:T(8,128)(2,1)S(1)} %bitcast.22, bf16[2240,128]{1,0:T(8,128)(2,1)S(1)} %collective-permute-done.4.t1, bf16[2240,128]{1,0:T(8,128)(2,1)S(1)} %collective-permute-done.5.t3, ...), custom_call_target="tpu_custom_call" | custom-call | bytes 10000000 | tf_op jit(solution)/shard_map/pallas_call | solution.py:38
  46.8 3.1 %collective-permute-start.11 = (bf16[288,640]{1,0:T(8,128)(2,1)S(1)}, bf16[288,640]{1,0:T(8,128)(2,1)S(1)}, u32[]{:S(2)}, u32[]{:S(2)}) collective-permute-start(bf16[288,640]{1,0:T(8,128)(2,1)S(1)} %collective-permute-done.1.w_lo), channel_id=1, source_target_pairs={{0,16},{16,0},{1,17},{17,1},{2,18},{18,2},{3,19},{19,3},{4,20},{20... | collective-permute-start | bytes 1105928 | tf_op jit(solution)/shard_map/ppermute | solution.py:264
  49.9 0.5 collective-permute-start.20
  50.4 1.3 collective-permute-done.12.v_hi
  51.7 4.6 %shard_map.81 = (bf16[560,512]{1,0:T(8,128)(2,1)S(1)}, bf16[560,512]{1,0:T(8,128)(2,1)S(1)}, bf16[560,128]{1,0:T(8,128)(2,1)S(1)}) custom-call(s32[5]{0:T(128)S(1)} %stack.19.idx, bf16[560,640]{1,0:T(8,128)(2,1)S(1)} %shard_map.79.w0, bf16[560,640]{1,0:T(8,128)(2,1)S(1)} %collective-permute-done.w_prev, bf16[560,640]{1,0:T(8,128)(2,1)S(1)} %collective-permute-done.2.w_next, ...), custom_call_target="tpu_custom_call" | custom-call | flops 2569011200 | bytes 5000000 | tf_op jit(solution)/shard_map/pallas_call | solution.py:38
  56.3 1.0 collective-permute-start.15
  57.3 1.9 %collective-permute-start.14 = (bf16[560,128]{1,0:T(8,128)(2,1)S(1)}, bf16[560,128]{1,0:T(8,128)(2,1)S(1)}, u32[]{:S(2)}, u32[]{:S(2)}) collective-permute-start(bf16[560,128]{1,0:T(8,128)(2,1)S(1)} %get-tuple-element.44.s0), channel_id=1, source_target_pairs={{0,12},{4,0},{8,4},{12,8},{1,13},{5,1},{9,5},{13,9},{2,14},{6,2},{... | collective-permute-start | bytes 430088 | tf_op jit(solution)/shard_map/ppermute | solution.py:264
  59.2 0.5 collective-permute-start.13
  59.7 0.7 collective-permute-done.16.q2
  60.3 2.5 %collective-permute-done.15.s3 = bf16[560,128]{1,0:T(8,128)(2,1)S(1)} collective-permute-done((bf16[560,128]{1,0:T(8,128)(2,1)S(1)}, bf16[560,128]{1,0:T(8,128)(2,1)S(1)}, u32[]{:S(2)}, u32[]{:S(2)}) %collective-permute-start.15) | collective-permute-done | bytes 143392 | tf_op jit(solution)/shard_map/ppermute | solution.py:264
  62.8 3.4 %collective-permute-done.14.s2 = bf16[560,128]{1,0:T(8,128)(2,1)S(1)} collective-permute-done((bf16[560,128]{1,0:T(8,128)(2,1)S(1)}, bf16[560,128]{1,0:T(8,128)(2,1)S(1)}, u32[]{:S(2)}, u32[]{:S(2)}) %collective-permute-start.14) | collective-permute-done | bytes 143392 | tf_op jit(solution)/shard_map/ppermute | solution.py:264
  66.3 2.0 %shard_map.82 = (bf16[560,128]{1,0:T(8,128)(2,1)S(1)}, bf16[560,128]{1,0:T(8,128)(2,1)S(1)}, bf16[560,128]{1,0:T(8,128)(2,1)S(1)}, bf16[560,128]{1,0:T(8,128)(2,1)S(1)}, bf16[560,128]{1,0:T(8,128)(2,1)S(1)}) custom-call(s32[5]{0:T(128)S(1)} %stack.19.idx, bf16[560,128]{1,0:T(8,128)(2,1)S(1)} %get-tuple-element.44.s0, ...), custom_call_target="tpu_custom_call" | custom-call | flops 220200960 | bytes 4000000 | tf_op jit(solution)/shard_map/pallas_call | solution.py:38
  68.3 1.1 collective-permute-start.19
  69.4 2.2 %collective-permute-start.18 = (bf16[560,128]{1,0:T(8,128)(2,1)S(1)}, bf16[560,128]{1,0:T(8,128)(2,1)S(1)}, u32[]{:S(2)}, u32[]{:S(2)}) collective-permute-start(bf16[560,128]{1,0:T(8,128)(2,1)S(1)} %get-tuple-element.48.s0), channel_id=1, source_target_pairs={{0,12},{4,0},{8,4},{12,8},{1,13},{5,1},{9,5},{13,9},{2,14},{6,2},{... | collective-permute-start | bytes 430088 | tf_op jit(solution)/shard_map/ppermute | solution.py:264
  71.6 0.1 collective-permute-start.17
  71.7 2.2 %collective-permute-done.19.s3 = bf16[560,128]{1,0:T(8,128)(2,1)S(1)} collective-permute-done((bf16[560,128]{1,0:T(8,128)(2,1)S(1)}, bf16[560,128]{1,0:T(8,128)(2,1)S(1)}, u32[]{:S(2)}, u32[]{:S(2)}) %collective-permute-start.19) | collective-permute-done | bytes 143392 | tf_op jit(solution)/shard_map/ppermute | solution.py:264
  74.0 4.0 %collective-permute-done.18.s2 = bf16[560,128]{1,0:T(8,128)(2,1)S(1)} collective-permute-done((bf16[560,128]{1,0:T(8,128)(2,1)S(1)}, bf16[560,128]{1,0:T(8,128)(2,1)S(1)}, u32[]{:S(2)}, u32[]{:S(2)}) %collective-permute-start.18) | collective-permute-done | bytes 143392 | tf_op jit(solution)/shard_map/ppermute | solution.py:264
  78.0 0.6 collective-permute-done.17.s1
  78.6 0.9 shard_map.83.d
  79.5 1.3 collective-permute-start.21
  80.8 1.1 shard_map.84.first
  81.9 0.5 collective-permute-done.21.d
  82.4 2.9 %shard_map.85 = bf16[16,64,640]{2,1,0:T(8,128)(2,1)} custom-call(s32[5]{0:T(128)S(1)} %stack.19.idx, f32[1152,560]{1,0:T(8,128)S(1)} %shard_map.84.first, bf16[1152,512]{1,0:T(8,128)(2,1)S(1)} %collective-permute-done.20.t, bf16[560,512]{1,0:T(8,128)(2,1)S(1)} %collective-permute-done.21.d), custom_call_target="tpu_custom_call" | custom-call | flops 660602880 | bytes 5000000 | tf_op jit(solution)/shard_map/pallas_call | solution.py:38
  85.3 6.9 %all-to-all-start.1 = ((bf16[16,64,640]{2,1,0:T(8,128)(2,1)}), bf16[16,64,640]{2,1,0:T(8,128)(2,1)S(1)}, u32[]{:S(2)}, u32[]{:S(2)}) async-start(bf16[16,64,640]{2,1,0:T(8,128)(2,1)} %shard_map.85), calls=%async_computation.1 | async-start | bytes 2621440 | tf_op jit(solution)/shard_map/all_to_all | solution.py:374
  92.3 0.5 collective-permute-start.22
  92.8 2.3 %collective-permute-start.23 = (bf16[560,128]{1,0:T(8,128)(2,1)S(1)}, bf16[560,128]{1,0:T(8,128)(2,1)S(1)}, u32[]{:S(2)}, u32[]{:S(2)}) collective-permute-start(bf16[560,128]{1,0:T(8,128)(2,1)S(1)} %get-tuple-element.54), channel_id=1, source_target_pairs={{0,2},{1,3},{2,0},{3,1},{4,6},{5,7},{6,4},{7,5},{8,10},{9,11},{10,... | collective-permute-start | bytes 430088 | tf_op jit(solution)/shard_map/ppermute | solution.py:264
  95.1 1.0 collective-permute-start.24
  96.1 2.1 %collective-permute-done.22.g1 = bf16[560,128]{1,0:T(8,128)(2,1)S(1)} collective-permute-done((bf16[560,128]{1,0:T(8,128)(2,1)S(1)}, bf16[560,128]{1,0:T(8,128)(2,1)S(1)}, u32[]{:S(2)}, u32[]{:S(2)}) %collective-permute-start.22) | collective-permute-done | bytes 143392 | tf_op jit(solution)/shard_map/ppermute | solution.py:264
  98.2 3.2 %collective-permute-done.23.g2 = bf16[560,128]{1,0:T(8,128)(2,1)S(1)} collective-permute-done((bf16[560,128]{1,0:T(8,128)(2,1)S(1)}, bf16[560,128]{1,0:T(8,128)(2,1)S(1)}, u32[]{:S(2)}, u32[]{:S(2)}) %collective-permute-start.23) | collective-permute-done | bytes 143392 | tf_op jit(solution)/shard_map/ppermute | solution.py:264
  101.4 0.1 collective-permute-done.24.g3
  101.5 1.4 %shard_map.86 = bf16[2240,128]{1,0:T(8,128)(2,1)} custom-call(s32[5]{0:T(128)S(1)} %stack.19.idx, bf16[560,128]{1,0:T(8,128)(2,1)S(1)} %get-tuple-element.52.g0, bf16[560,128]{1,0:T(8,128)(2,1)S(1)} %collective-permute-done.22.g1, bf16[560,128]{1,0:T(8,128)(2,1)S(1)} %collective-permute-done.23.g2, bf16[560,128]{1,0:T(8,128)(2,1)S(1)} %collective-permute-done.24.g3), custom_call_target="tpu_custom_call" | custom-call | tf_op jit(solution)/shard_map/pallas_call | solution.py:38
  102.9 9.5 %all-to-all-done.1.g = bf16[16,64,640]{2,1,0:T(8,128)(2,1)S(1)} async-done(((bf16[16,64,640]{2,1,0:T(8,128)(2,1)}), bf16[16,64,640]{2,1,0:T(8,128)(2,1)S(1)}, u32[]{:S(2)}, u32[]{:S(2)}) %all-to-all-start.1) | async-done | bytes 1310752 | tf_op jit(solution)/shard_map/all_to_all | solution.py:374
  112.4 0.2 shard_map.87
  112.6 0.3 collective-permute-start.28
  112.9 2.3 %collective-permute-start.27 = (bf16[64,640]{1,0:T(8,128)(2,1)S(1)}, bf16[64,640]{1,0:T(8,128)(2,1)S(1)}, u32[]{:S(2)}, u32[]{:S(2)}) collective-permute-start(bf16[64,640]{1,0:T(8,128)(2,1)S(1)} %shard_map.87), channel_id=1, source_target_pairs={{0,64},{1,65},{2,66},{3,67},{32,97},{33,98},{34,99},{35,96},{64,2}... | collective-permute-start | bytes 245768 | tf_op jit(solution)/shard_map/ppermute | solution.py:379
  115.2 1.1 collective-permute-start.26
  116.2 0.7 collective-permute-start.25
  116.9 3.7 %collective-permute-start.32 = (bf16[64,640]{1,0:T(8,128)(2,1)S(1)}, bf16[64,640]{1,0:T(8,128)(2,1)S(1)}, u32[]{:S(2)}, u32[]{:S(2)}) collective-permute-start(bf16[64,640]{1,0:T(8,128)(2,1)S(1)} %collective-permute-done.28.r3), channel_id=1, source_target_pairs={{0,16},{16,0},{1,17},{17,1},{2,18},{18,2},{3,19},{19,3},{4,20},{20... | collective-permute-start | bytes 245768 | tf_op jit(solution)/shard_map/ppermute | solution.py:264
  120.7 3.7 %collective-permute-start.31 = (bf16[64,640]{1,0:T(8,128)(2,1)S(1)}, bf16[64,640]{1,0:T(8,128)(2,1)S(1)}, u32[]{:S(2)}, u32[]{:S(2)}) collective-permute-start(bf16[64,640]{1,0:T(8,128)(2,1)S(1)} %collective-permute-done.27.r2), channel_id=1, source_target_pairs={{0,16},{16,0},{1,17},{17,1},{2,18},{18,2},{3,19},{19,3},{4,20},{20... | collective-permute-start | bytes 245768 | tf_op jit(solution)/shard_map/ppermute | solution.py:264
  124.4 2.2 %collective-permute-start.30 = (bf16[64,640]{1,0:T(8,128)(2,1)S(1)}, bf16[64,640]{1,0:T(8,128)(2,1)S(1)}, u32[]{:S(2)}, u32[]{:S(2)}) collective-permute-start(bf16[64,640]{1,0:T(8,128)(2,1)S(1)} %collective-permute-done.26.r1), channel_id=1, source_target_pairs={{0,16},{16,0},{1,17},{17,1},{2,18},{18,2},{3,19},{19,3},{4,20},{20... | collective-permute-start | bytes 245768 | tf_op jit(solution)/shard_map/ppermute | solution.py:264
  126.6 0.9 collective-permute-done.30.o1
  127.5 0.4 collective-permute-done.29.o0
  127.9 2.4 %shard_map.88 = f32[140,2240]{1,0:T(8,128)} custom-call(s32[5]{0:T(128)S(1)} %stack.19.idx, bf16[64,640]{1,0:T(8,128)(2,1)S(1)} %collective-permute-done.25.r0, bf16[64,640]{1,0:T(8,128)(2,1)S(1)} %collective-permute-done.26.r1, bf16[64,640]{1,0:T(8,128)(2,1)S(1)} %collective-permute-done.27.r2, bf16[64,640]{1,0:T(8,128)(2,1)S(1)} %collective-permute-done.28.r3, ...), custom_call_target="tpu_custom_call" | custom-call | tf_op jit(solution)/shard_map/pallas_call | solution.py:38
  (43 shorter events, 0.4 us)
Async XLA Ops:
  0.6 6.7 %copy-start.2 = (bf16[1,128,2240]{1,2,0:T(8,128)(2,1)S(1)}, bf16[1,128,2240]{1,2,0:T(8,128)(2,1)}, u32[]{:S(2)}) copy-start(bf16[1,128,2240]{1,2,0:T(8,128)(2,1)} %param.6) | copy-start | bytes 1720324
  2.9 5.7 %copy-start = (bf16[1,128,2240]{1,2,0:T(8,128)(2,1)S(1)}, bf16[1,128,2240]{1,2,0:T(8,128)(2,1)}, u32[]{:S(2)}) copy-start(bf16[1,128,2240]{1,2,0:T(8,128)(2,1)} %param.7) | copy-start | bytes 1720324
  2.9 5.7 %copy-start.1 = (bf16[1,128,2240]{1,2,0:T(8,128)(2,1)S(1)}, bf16[1,128,2240]{1,2,0:T(8,128)(2,1)}, u32[]{:S(2)}) copy-start(bf16[1,128,2240]{1,2,0:T(8,128)(2,1)} %param.8) | copy-start | bytes 1720324
  2.9 13.5 %all-to-all-start = ((bf16[4,140,560]{2,1,0:T(8,128)(2,1)}), bf16[4,140,560]{2,1,0:T(8,128)(2,1)S(1)}, u32[]{:S(2)}, u32[]{:S(2)}) async-start(bf16[4,140,560]{2,1,0:T(8,128)(2,1)} %shard_map.77), calls=%async_computation | async-start | bytes 1474560 | tf_op jit(solution)/shard_map/all_to_all | solution.py:290
  7.3 20.5 %collective-permute-start.4 = (bf16[2240,128]{1,0:T(8,128)(2,1)S(1)}, bf16[2240,128]{1,0:T(8,128)(2,1)S(1)}, u32[]{:S(2)}, u32[]{:S(2)}) collective-permute-start(bf16[2240,128]{1,0:T(8,128)(2,1)S(1)} %bitcast.20), channel_id=1, source_target_pairs={{0,3},{1,0},{2,1},{3,2},{4,7},{5,4},{6,5},{7,6},{8,11},{9,8},{10,9... | collective-permute-start | bytes 1720328 | tf_op jit(solution)/shard_map/ppermute | solution.py:264
  10.7 0.7 copy-start.3
  11.5 0.7 copy-start.5
  12.2 0.7 copy-start.7
  16.4 11.4 %copy-start.6 = (bf16[2,560,128]{2,1,0:T(8,128)(2,1)S(1)}, bf16[2,560,128]{2,1,0:T(8,128)(2,1)}, u32[]{:S(2)}) copy-start(bf16[2,560,128]{2,1,0:T(8,128)(2,1)} %copy-done.5) | copy-start | bytes 860164
  16.4 12.7 %collective-permute-start.5 = (bf16[2240,128]{1,0:T(8,128)(2,1)S(1)}, bf16[2240,128]{1,0:T(8,128)(2,1)S(1)}, u32[]{:S(2)}, u32[]{:S(2)}) collective-permute-start(bf16[2240,128]{1,0:T(8,128)(2,1)S(1)} %bitcast.21), channel_id=1, source_target_pairs={{0,1},{1,2},{2,3},{3,0},{4,5},{5,6},{6,7},{7,4},{8,9},{9,10},{10,1... | collective-permute-start | bytes 1720328 | tf_op jit(solution)/shard_map/ppermute | solution.py:264
  18.4 10.7 %copy-start.4 = (bf16[2,560,128]{2,1,0:T(8,128)(2,1)S(1)}, bf16[2,560,128]{2,1,0:T(8,128)(2,1)}, u32[]{:S(2)}) copy-start(bf16[2,560,128]{2,1,0:T(8,128)(2,1)} %copy-done.3) | copy-start | bytes 860164
  18.4 19.3 %collective-permute-start.2 = (bf16[560,640]{1,0:T(8,128)(2,1)S(1)}, bf16[560,640]{1,0:T(8,128)(2,1)S(1)}, u32[]{:S(2)}, u32[]{:S(2)}) collective-permute-start(bf16[560,640]{1,0:T(8,128)(2,1)S(1)} %shard_map.79.w0), channel_id=1, source_target_pairs={{0,12},{4,0},{8,4},{12,8},{1,13},{5,1},{9,5},{13,9},{2,14},{6,2},{... | collective-permute-start | bytes 2150408 | tf_op jit(solution)/shard_map/ppermute | solution.py:264
  21.3 16.3 %collective-permute-start = (bf16[560,640]{1,0:T(8,128)(2,1)S(1)}, bf16[560,640]{1,0:T(8,128)(2,1)S(1)}, u32[]{:S(2)}, u32[]{:S(2)}) collective-permute-start(bf16[560,640]{1,0:T(8,128)(2,1)S(1)} %shard_map.79.w0), channel_id=1, source_target_pairs={{0,4},{4,8},{8,12},{12,0},{1,5},{5,9},{9,13},{13,1},{2,6},{6,10},{... | collective-permute-start | bytes 2150408 | tf_op jit(solution)/shard_map/ppermute | solution.py:264
  27.9 14.2 %collective-permute-start.7 = (bf16[2240,128]{1,0:T(8,128)(2,1)S(1)}, bf16[2240,128]{1,0:T(8,128)(2,1)S(1)}, u32[]{:S(2)}, u32[]{:S(2)}) collective-permute-start(bf16[2240,128]{1,0:T(8,128)(2,1)S(1)} %pad_maximum_fusion.1), channel_id=1, source_target_pairs={{0,3},{1,0},{2,1},{3,2},{4,7},{5,4},{6,5},{7,6},{8,11},{9,8},{10,9... | collective-permute-start | bytes 1720328 | tf_op jit(solution)/shard_map/ppermute | solution.py:264
  29.2 15.3 %collective-permute-start.6 = (bf16[2240,128]{1,0:T(8,128)(2,1)S(1)}, bf16[2240,128]{1,0:T(8,128)(2,1)S(1)}, u32[]{:S(2)}, u32[]{:S(2)}) collective-permute-start(bf16[2240,128]{1,0:T(8,128)(2,1)S(1)} %pad_maximum_fusion), channel_id=1, source_target_pairs={{0,1},{1,2},{2,3},{3,0},{4,5},{5,6},{6,7},{7,4},{8,9},{9,10},{10,1... | collective-permute-start | bytes 1720328 | tf_op jit(solution)/shard_map/ppermute | solution.py:264
  32.1 17.8 %collective-permute-start.8 = (bf16[560,640]{1,0:T(8,128)(2,1)S(1)}, bf16[560,640]{1,0:T(8,128)(2,1)S(1)}, u32[]{:S(2)}, u32[]{:S(2)}) collective-permute-start(bf16[560,640]{1,0:T(8,128)(2,1)S(1)} %shard_map.79.w0), channel_id=1, source_target_pairs={{0,16},{16,0},{1,17},{17,1},{2,18},{18,2},{3,19},{19,3},{4,20},{20... | collective-permute-start | bytes 2150408 | tf_op jit(solution)/shard_map/ppermute | solution.py:264
  37.6 9.2 %collective-permute-start.1 = (bf16[288,640]{1,0:T(8,128)(2,1)S(1)}, bf16[288,640]{1,0:T(8,128)(2,1)S(1)}, u32[]{:S(2)}, u32[]{:S(2)}) collective-permute-start(bf16[288,640]{1,0:T(8,128)(2,1)S(1)} %slice.16), channel_id=1, source_target_pairs={{0,4},{4,8},{8,12},{12,0},{1,5},{5,9},{9,13},{13,1},{2,6},{6,10},{... | collective-permute-start | bytes 1105928 | tf_op jit(solution)/shard_map/ppermute | solution.py:264
  37.8 12.7 %copy-start.8 = (bf16[2,560,128]{2,1,0:T(8,128)(2,1)S(1)}, bf16[2,560,128]{2,1,0:T(8,128)(2,1)}, u32[]{:S(2)}) copy-start(bf16[2,560,128]{2,1,0:T(8,128)(2,1)} %copy-done.7) | copy-start | bytes 860164
  37.8 9.0 %collective-permute-start.3 = (bf16[272,640]{1,0:T(8,128)(2,1)S(1)}, bf16[272,640]{1,0:T(8,128)(2,1)S(1)}, u32[]{:S(2)}, u32[]{:S(2)}) collective-permute-start(bf16[272,640]{1,0:T(8,128)(2,1)S(1)} %slice.17), channel_id=1, source_target_pairs={{0,12},{4,0},{8,4},{12,8},{1,13},{5,1},{9,5},{13,9},{2,14},{6,2},{... | collective-permute-start | bytes 1044488 | tf_op jit(solution)/shard_map/ppermute | solution.py:264
  42.1 8.3 %collective-permute-start.10 = (bf16[560,640]{1,0:T(8,128)(2,1)S(1)}, bf16[560,640]{1,0:T(8,128)(2,1)S(1)}, u32[]{:S(2)}, u32[]{:S(2)}) collective-permute-start(bf16[560,640]{1,0:T(8,128)(2,1)S(1)} %collective-permute-done.2.w_next), channel_id=1, source_target_pairs={{0,16},{16,0},{1,17},{17,1},{2,18},{18,2},{3,19},{19,3},{4,20},{20... | collective-permute-start | bytes 2150408 | tf_op jit(solution)/shard_map/ppermute | solution.py:264
  44.5 5.9 %collective-permute-start.9 = (bf16[560,640]{1,0:T(8,128)(2,1)S(1)}, bf16[560,640]{1,0:T(8,128)(2,1)S(1)}, u32[]{:S(2)}, u32[]{:S(2)}) collective-permute-start(bf16[560,640]{1,0:T(8,128)(2,1)S(1)} %collective-permute-done.w_prev), channel_id=1, source_target_pairs={{0,16},{16,0},{1,17},{17,1},{2,18},{18,2},{3,19},{19,3},{4,20},{20... | collective-permute-start | bytes 2150408 | tf_op jit(solution)/shard_map/ppermute | solution.py:264
  46.8 4.9 %collective-permute-start.11 = (bf16[288,640]{1,0:T(8,128)(2,1)S(1)}, bf16[288,640]{1,0:T(8,128)(2,1)S(1)}, u32[]{:S(2)}, u32[]{:S(2)}) collective-permute-start(bf16[288,640]{1,0:T(8,128)(2,1)S(1)} %collective-permute-done.1.w_lo), channel_id=1, source_target_pairs={{0,16},{16,0},{1,17},{17,1},{2,18},{18,2},{3,19},{19,3},{4,20},{20... | collective-permute-start | bytes 1105928 | tf_op jit(solution)/shard_map/ppermute | solution.py:264
  49.9 1.8 %collective-permute-start.12 = (bf16[272,640]{1,0:T(8,128)(2,1)S(1)}, bf16[272,640]{1,0:T(8,128)(2,1)S(1)}, u32[]{:S(2)}, u32[]{:S(2)}) collective-permute-start(bf16[272,640]{1,0:T(8,128)(2,1)S(1)} %collective-permute-done.3.w_hi), channel_id=1, source_target_pairs={{0,16},{16,0},{1,17},{17,1},{2,18},{18,2},{3,19},{19,3},{4,20},{20... | collective-permute-start | bytes 1044488 | tf_op jit(solution)/shard_map/ppermute | solution.py:264
  49.9 32.0 %collective-permute-start.20 = (bf16[1152,512]{1,0:T(8,128)(2,1)S(1)}, bf16[1152,512]{1,0:T(8,128)(2,1)S(1)}, u32[]{:S(2)}, u32[]{:S(2)}) collective-permute-start(bf16[1152,512]{1,0:T(8,128)(2,1)S(1)} %get-tuple-element.51), channel_id=1, source_target_pairs={{0,16},{16,0},{1,17},{17,1},{2,18},{18,2},{3,19},{19,3},{4,20},{20... | collective-permute-start | bytes 3538952 | tf_op jit(solution)/shard_map/ppermute | solution.py:264
  50.4 9.9 %collective-permute-start.16 = (bf16[2,560,128]{2,1,0:T(8,128)(2,1)S(1)}, bf16[2,560,128]{2,1,0:T(8,128)(2,1)S(1)}, u32[]{:S(2)}, u32[]{:S(2)}) collective-permute-start(bf16[2,560,128]{2,1,0:T(8,128)(2,1)S(1)} %copy-done.8), channel_id=1, source_target_pairs={{0,2},{1,3},{2,0},{3,1},{4,6},{5,7},{6,4},{7,5},{8,10},{9,11},{10,... | collective-permute-start | bytes 860168 | tf_op jit(solution)/shard_map/ppermute | solution.py:264
  56.3 6.6 %collective-permute-start.15 = (bf16[560,128]{1,0:T(8,128)(2,1)S(1)}, bf16[560,128]{1,0:T(8,128)(2,1)S(1)}, u32[]{:S(2)}, u32[]{:S(2)}) collective-permute-start(bf16[560,128]{1,0:T(8,128)(2,1)S(1)} %get-tuple-element.44.s0), channel_id=1, source_target_pairs={{0,8},{4,12},{8,0},{12,4},{1,9},{5,13},{9,1},{13,5},{2,10},{6,14},... | collective-permute-start | bytes 430088 | tf_op jit(solution)/shard_map/ppermute | solution.py:264
  57.3 9.0 %collective-permute-start.14 = (bf16[560,128]{1,0:T(8,128)(2,1)S(1)}, bf16[560,128]{1,0:T(8,128)(2,1)S(1)}, u32[]{:S(2)}, u32[]{:S(2)}) collective-permute-start(bf16[560,128]{1,0:T(8,128)(2,1)S(1)} %get-tuple-element.44.s0), channel_id=1, source_target_pairs={{0,12},{4,0},{8,4},{12,8},{1,13},{5,1},{9,5},{13,9},{2,14},{6,2},{... | collective-permute-start | bytes 430088 | tf_op jit(solution)/shard_map/ppermute | solution.py:264
  59.2 7.1 %collective-permute-start.13 = (bf16[560,128]{1,0:T(8,128)(2,1)S(1)}, bf16[560,128]{1,0:T(8,128)(2,1)S(1)}, u32[]{:S(2)}, u32[]{:S(2)}) collective-permute-start(bf16[560,128]{1,0:T(8,128)(2,1)S(1)} %get-tuple-element.44.s0), channel_id=1, source_target_pairs={{0,4},{4,8},{8,12},{12,0},{1,5},{5,9},{9,13},{13,1},{2,6},{6,10},{... | collective-permute-start | bytes 430088 | tf_op jit(solution)/shard_map/ppermute | solution.py:264
  68.3 5.7 %collective-permute-start.19 = (bf16[560,128]{1,0:T(8,128)(2,1)S(1)}, bf16[560,128]{1,0:T(8,128)(2,1)S(1)}, u32[]{:S(2)}, u32[]{:S(2)}) collective-permute-start(bf16[560,128]{1,0:T(8,128)(2,1)S(1)} %get-tuple-element.48.s0), channel_id=1, source_target_pairs={{0,8},{4,12},{8,0},{12,4},{1,9},{5,13},{9,1},{13,5},{2,10},{6,14},... | collective-permute-start | bytes 430088 | tf_op jit(solution)/shard_map/ppermute | solution.py:264
  69.4 8.6 %collective-permute-start.18 = (bf16[560,128]{1,0:T(8,128)(2,1)S(1)}, bf16[560,128]{1,0:T(8,128)(2,1)S(1)}, u32[]{:S(2)}, u32[]{:S(2)}) collective-permute-start(bf16[560,128]{1,0:T(8,128)(2,1)S(1)} %get-tuple-element.48.s0), channel_id=1, source_target_pairs={{0,12},{4,0},{8,4},{12,8},{1,13},{5,1},{9,5},{13,9},{2,14},{6,2},{... | collective-permute-start | bytes 430088 | tf_op jit(solution)/shard_map/ppermute | solution.py:264
  71.6 7.0 %collective-permute-start.17 = (bf16[560,128]{1,0:T(8,128)(2,1)S(1)}, bf16[560,128]{1,0:T(8,128)(2,1)S(1)}, u32[]{:S(2)}, u32[]{:S(2)}) collective-permute-start(bf16[560,128]{1,0:T(8,128)(2,1)S(1)} %get-tuple-element.48.s0), channel_id=1, source_target_pairs={{0,4},{4,8},{8,12},{12,0},{1,5},{5,9},{9,13},{13,1},{2,6},{6,10},{... | collective-permute-start | bytes 430088 | tf_op jit(solution)/shard_map/ppermute | solution.py:264
  79.5 2.9 %collective-permute-start.21 = (bf16[560,512]{1,0:T(8,128)(2,1)S(1)}, bf16[560,512]{1,0:T(8,128)(2,1)S(1)}, u32[]{:S(2)}, u32[]{:S(2)}) collective-permute-start(bf16[560,512]{1,0:T(8,128)(2,1)S(1)} %shard_map.83.d), channel_id=1, source_target_pairs={{0,16},{16,0},{1,17},{17,1},{2,18},{18,2},{3,19},{19,3},{4,20},{20... | collective-permute-start | bytes 1720328 | tf_op jit(solution)/shard_map/ppermute | solution.py:264
  85.3 27.1 %all-to-all-start.1 = ((bf16[16,64,640]{2,1,0:T(8,128)(2,1)}), bf16[16,64,640]{2,1,0:T(8,128)(2,1)S(1)}, u32[]{:S(2)}, u32[]{:S(2)}) async-start(bf16[16,64,640]{2,1,0:T(8,128)(2,1)} %shard_map.85), calls=%async_computation.1 | async-start | bytes 2621440 | tf_op jit(solution)/shard_map/all_to_all | solution.py:374
  92.3 5.9 %collective-permute-start.22 = (bf16[560,128]{1,0:T(8,128)(2,1)S(1)}, bf16[560,128]{1,0:T(8,128)(2,1)S(1)}, u32[]{:S(2)}, u32[]{:S(2)}) collective-permute-start(bf16[560,128]{1,0:T(8,128)(2,1)S(1)} %get-tuple-element.53), channel_id=1, source_target_pairs={{0,3},{1,0},{2,1},{3,2},{4,7},{5,4},{6,5},{7,6},{8,11},{9,8},{10,9... | collective-permute-start | bytes 430088 | tf_op jit(solution)/shard_map/ppermute | solution.py:264
  92.8 8.6 %collective-permute-start.23 = (bf16[560,128]{1,0:T(8,128)(2,1)S(1)}, bf16[560,128]{1,0:T(8,128)(2,1)S(1)}, u32[]{:S(2)}, u32[]{:S(2)}) collective-permute-start(bf16[560,128]{1,0:T(8,128)(2,1)S(1)} %get-tuple-element.54), channel_id=1, source_target_pairs={{0,2},{1,3},{2,0},{3,1},{4,6},{5,7},{6,4},{7,5},{8,10},{9,11},{10,... | collective-permute-start | bytes 430088 | tf_op jit(solution)/shard_map/ppermute | solution.py:264
  95.1 6.4 %collective-permute-start.24 = (bf16[560,128]{1,0:T(8,128)(2,1)S(1)}, bf16[560,128]{1,0:T(8,128)(2,1)S(1)}, u32[]{:S(2)}, u32[]{:S(2)}) collective-permute-start(bf16[560,128]{1,0:T(8,128)(2,1)S(1)} %get-tuple-element.55), channel_id=1, source_target_pairs={{0,1},{1,2},{2,3},{3,0},{4,5},{5,6},{6,7},{7,4},{8,9},{9,10},{10,1... | collective-permute-start | bytes 430088 | tf_op jit(solution)/shard_map/ppermute | solution.py:264
  112.6 4.3 %collective-permute-start.28 = (bf16[64,640]{1,0:T(8,128)(2,1)S(1)}, bf16[64,640]{1,0:T(8,128)(2,1)S(1)}, u32[]{:S(2)}, u32[]{:S(2)}) collective-permute-start(bf16[64,640]{1,0:T(8,128)(2,1)S(1)} %shard_map.87), channel_id=1, source_target_pairs={{0,96},{1,97},{2,98},{3,99},{32,1},{33,2},{34,3},{35,0},{64,34},{6... | collective-permute-start | bytes 245768 | tf_op jit(solution)/shard_map/ppermute | solution.py:379
  112.9 7.8 %collective-permute-start.27 = (bf16[64,640]{1,0:T(8,128)(2,1)S(1)}, bf16[64,640]{1,0:T(8,128)(2,1)S(1)}, u32[]{:S(2)}, u32[]{:S(2)}) collective-permute-start(bf16[64,640]{1,0:T(8,128)(2,1)S(1)} %shard_map.87), channel_id=1, source_target_pairs={{0,64},{1,65},{2,66},{3,67},{32,97},{33,98},{34,99},{35,96},{64,2}... | collective-permute-start | bytes 245768 | tf_op jit(solution)/shard_map/ppermute | solution.py:379
  115.2 9.2 %collective-permute-start.26 = (bf16[64,640]{1,0:T(8,128)(2,1)S(1)}, bf16[64,640]{1,0:T(8,128)(2,1)S(1)}, u32[]{:S(2)}, u32[]{:S(2)}) collective-permute-start(bf16[64,640]{1,0:T(8,128)(2,1)S(1)} %shard_map.87), channel_id=1, source_target_pairs={{0,32},{1,33},{2,34},{3,35},{32,65},{33,66},{34,67},{35,64},{64,98... | collective-permute-start | bytes 245768 | tf_op jit(solution)/shard_map/ppermute | solution.py:379
  116.2 10.4 %collective-permute-start.25 = (bf16[64,640]{1,0:T(8,128)(2,1)S(1)}, bf16[64,640]{1,0:T(8,128)(2,1)S(1)}, u32[]{:S(2)}, u32[]{:S(2)}) collective-permute-start(bf16[64,640]{1,0:T(8,128)(2,1)S(1)} %shard_map.87), channel_id=1, source_target_pairs={{0,0},{1,1},{2,2},{3,3},{32,33},{33,34},{34,35},{35,32},{64,66},{6... | collective-permute-start | bytes 245768 | tf_op jit(solution)/shard_map/ppermute | solution.py:379
  116.9 9.7 %collective-permute-start.32 = (bf16[64,640]{1,0:T(8,128)(2,1)S(1)}, bf16[64,640]{1,0:T(8,128)(2,1)S(1)}, u32[]{:S(2)}, u32[]{:S(2)}) collective-permute-start(bf16[64,640]{1,0:T(8,128)(2,1)S(1)} %collective-permute-done.28.r3), channel_id=1, source_target_pairs={{0,16},{16,0},{1,17},{17,1},{2,18},{18,2},{3,19},{19,3},{4,20},{20... | collective-permute-start | bytes 245768 | tf_op jit(solution)/shard_map/ppermute | solution.py:264
  120.7 5.9 %collective-permute-start.31 = (bf16[64,640]{1,0:T(8,128)(2,1)S(1)}, bf16[64,640]{1,0:T(8,128)(2,1)S(1)}, u32[]{:S(2)}, u32[]{:S(2)}) collective-permute-start(bf16[64,640]{1,0:T(8,128)(2,1)S(1)} %collective-permute-done.27.r2), channel_id=1, source_target_pairs={{0,16},{16,0},{1,17},{17,1},{2,18},{18,2},{3,19},{19,3},{4,20},{20... | collective-permute-start | bytes 245768 | tf_op jit(solution)/shard_map/ppermute | solution.py:264
  124.4 3.1 %collective-permute-start.30 = (bf16[64,640]{1,0:T(8,128)(2,1)S(1)}, bf16[64,640]{1,0:T(8,128)(2,1)S(1)}, u32[]{:S(2)}, u32[]{:S(2)}) collective-permute-start(bf16[64,640]{1,0:T(8,128)(2,1)S(1)} %collective-permute-done.26.r1), channel_id=1, source_target_pairs={{0,16},{16,0},{1,17},{17,1},{2,18},{18,2},{3,19},{19,3},{4,20},{20... | collective-permute-start | bytes 245768 | tf_op jit(solution)/shard_map/ppermute | solution.py:264
  126.6 1.3 collective-permute-start.29

commit v6 on v5

--- a/solution.py
+++ b/solution.py
@@ -244,13 +244,14 @@
 def place_rows(idx, r0, r1, r2, r3, o0, o1, o2, o3, out, buf):
     for step, (r, o) in enumerate(((r0, o0), (r1, o1), (r2, o2), (r3, o3))):
         k = lax.rem(idx[3] - idx[0] + step + NX, NX)
-        buf[idx[1], k] = r[...].astype(F32)
-        buf[1 - idx[1], k] = o[...].astype(F32)
+        buf[idx[1], k] = r[...]
+        buf[1 - idx[1], k] = o[...]
     for c in range(2):
         for k in range(NX):
             lo, at = HALF * c, GW * k
-            out[lo : lo + PR, at : at + GW] = buf[c, k, :, :GW]
-            tail = [buf[c, k, 8 * j : 8 * (j + 1), GW:] for j in range(GW // EX)]
+            block = buf[c, k].astype(F32)
+            out[lo : lo + PR, at : at + GW] = block[:, :GW]
+            tail = [block[8 * j : 8 * (j + 1), GW:] for j in range(GW // EX)]
             tail = jnp.concatenate(tail, axis=1)
             out[lo + PR : lo + HALF, at : at + GW] = tail[: HALF - PR]
 
@@ -375,24 +376,21 @@
     grad_q = call(place_queries, sds((D, ROWS)), [SMEM] + [VMEM] * 4, (idx, *g_in))
     part, grad_q = lax.optimization_barrier((part, grad_q))
     rows = call(sum_pieces, sds((PR, PL)), [VMEM], (part,))
-    got = [
-        lax.ppermute(
-            rows,
-            ("z", "x"),
-            [
-                (z_at * NX + x_at, (z_at + s) % NZ * NX + (x_at + z_at) % NX)
-                for z_at in range(NZ)
-                for x_at in range(NX)
-            ],
-        )
-        for s in range(NZ)
-    ]
+    got = {}
+    for s in (0, 1, 3, 2):
+        pairs = [
+            (z_at * NX + x_at, (z_at + s) % NZ * NX + (x_at + z_at) % NX)
+            for z_at in range(NZ)
+            for x_at in range(NX)
+        ]
+        got[s] = lax.ppermute(rows, ("z", "x"), pairs)
+    got = [got[s] for s in range(NZ)]
     grad_rows = call(
         place_rows,
         sds((SH, D), F32),
         [SMEM] + [VMEM] * 8,
         (idx, *got, *[swap(g) for g in got]),
-        scratch=[pltpu.VMEM((2, NX, PR, PL), F32)],
+        scratch=[pltpu.VMEM((2, NX, PR, PL), BF)],
     )
     return grad_q.T[None], grad_rows
 

time: 132 us -> 132 us (level)
  no operation moved by 1% of the time
where the time goes in v6:
time: 132 us; the launch traced here: 130 us
  starting transfers between devices  59.2 us (45%)
  waiting for transfers between devices  45.6 us (35%)
  Pallas kernels  21.4 us (16%)
  local copies, waits for them, and re-layouts  2.33 us (2%)
  between operations  1.55 us (1%)
    ppermute x29, starting transfers between devices, shift(): return lax.ppermute(v, axis, [(i, (i + d) % n) for i in range(n)])  43.6 us
    ppermute x29, waiting for transfers between devices, shift(): return lax.ppermute(v, axis, [(i, (i + d) % n) for i in range(n)])  32.5 us
    pallas_call x12, Pallas kernels, call(): pl.pallas_call(body, out_shape=out_shape, in_specs=in_specs, out_specs=ja...  21.4 us
    all_to_all x1, waiting for transfers between devices, per_device(): part = lax.all_to_all(part, ('z', 'y'), 0, 0, tiled=True)  9.51 us
    all_to_all x1, starting transfers between devices, per_device(): part = lax.all_to_all(part, ('z', 'y'), 0, 0, tiled=True)  6.94 us
    all_to_all x1, starting transfers between devices, per_device(): merged = lax.all_to_all(pieces, 'x', 0, 0, tiled=True)  4.35 us
    ppermute x4, starting transfers between devices, per_device(): got[s] = lax.ppermute(rows, ('z', 'x'), pairs)  4.29 us
    all_to_all x1, waiting for transfers between devices, per_device(): merged = lax.all_to_all(pieces, 'x', 0, 0, tiled=True)  3.54 us
  transfers between devices with their start and end apart: 35, of which 18 were waited for; matrix products, arithmetic and copies ran while one was open for 0% of the time, Pallas kernels for 11%

profile of v6, /device:TPU:7, one launch (start us, length us, event | category | flops | bytes accessed | tf_op | source)
XLA Modules:
  0.0 130.1 jit_solution(14312682630524599347)
XLA Ops:
  0.6 2.3 %shard_map.77 = bf16[4,140,560]{2,1,0:T(8,128)(2,1)} custom-call(bf16[140,2240]{1,0:T(8,128)(2,1)} %wk.1, bf16[140,2240]{1,0:T(8,128)(2,1)} %wv.1), custom_call_target="tpu_custom_call" | custom-call | tf_op jit(solution)/shard_map/pallas_call | solution.py:38
  2.9 4.4 %all-to-all-start = ((bf16[4,140,560]{2,1,0:T(8,128)(2,1)}), bf16[4,140,560]{2,1,0:T(8,128)(2,1)S(1)}, u32[]{:S(2)}, u32[]{:S(2)}) async-start(bf16[4,140,560]{2,1,0:T(8,128)(2,1)} %shard_map.77), calls=%async_computation | async-start | bytes 1474560 | tf_op jit(solution)/shard_map/all_to_all | solution.py:291
  7.3 0.6 collective-permute-start.4
  8.5 0.1 stack.19.idx
  8.6 2.1 %shard_map.78 = (bf16[2,560,128]{2,1,0:T(8,128)(2,1)S(1)}, bf16[2,560,128]{2,1,0:T(8,128)(2,1)S(1)}, bf16[2,560,128]{2,1,0:T(8,128)(2,1)S(1)}, bf16[2,560,128]{2,1,0:T(8,128)(2,1)S(1)}) custom-call(s32[5]{0:T(128)S(1)} %stack.19.idx, bf16[2240,128]{1,0:T(8,128)(2,1)S(1)} %bitcast.18, bf16[2240,128]{1,0:T(8,128)(2,1)S(1)} %bitcast.19), custom_call_target="tpu_custom_call" | custom-call | tf_op jit(solution)/shard_map/pallas_call | solution.py:38
  10.7 0.7 copy-done.3
  11.5 0.7 copy-done.5
  12.2 0.7 copy-done.7
  12.9 3.5 %all-to-all-done.g = bf16[4,140,560]{2,1,0:T(8,128)(2,1)S(1)} async-done(((bf16[4,140,560]{2,1,0:T(8,128)(2,1)}), bf16[4,140,560]{2,1,0:T(8,128)(2,1)S(1)}, u32[]{:S(2)}, u32[]{:S(2)}) %all-to-all-start) | async-done | bytes 627232 | tf_op jit(solution)/shard_map/all_to_all | solution.py:291
  16.4 1.7 %collective-permute-start.5 = (bf16[2240,128]{1,0:T(8,128)(2,1)S(1)}, bf16[2240,128]{1,0:T(8,128)(2,1)S(1)}, u32[]{:S(2)}, u32[]{:S(2)}) collective-permute-start(bf16[2240,128]{1,0:T(8,128)(2,1)S(1)} %bitcast.21), channel_id=1, source_target_pairs={{0,1},{1,2},{2,3},{3,0},{4,5},{5,6},{6,7},{7,4},{8,9},{9,10},{10,1... | collective-permute-start | bytes 1720328 | tf_op jit(solution)/shard_map/ppermute | solution.py:265
  18.1 0.3 shard_map.79.w0
  18.4 2.8 %collective-permute-start.2 = (bf16[560,640]{1,0:T(8,128)(2,1)S(1)}, bf16[560,640]{1,0:T(8,128)(2,1)S(1)}, u32[]{:S(2)}, u32[]{:S(2)}) collective-permute-start(bf16[560,640]{1,0:T(8,128)(2,1)S(1)} %shard_map.79.w0), channel_id=1, source_target_pairs={{0,12},{4,0},{8,4},{12,8},{1,13},{5,1},{9,5},{13,9},{2,14},{6,2},{... | collective-permute-start | bytes 2150408 | tf_op jit(solution)/shard_map/ppermute | solution.py:265
  21.3 6.5 %collective-permute-done.4.t1 = bf16[2240,128]{1,0:T(8,128)(2,1)S(1)} collective-permute-done((bf16[2240,128]{1,0:T(8,128)(2,1)S(1)}, bf16[2240,128]{1,0:T(8,128)(2,1)S(1)}, u32[]{:S(2)}, u32[]{:S(2)}) %collective-permute-start.4) | collective-permute-done | bytes 573472 | tf_op jit(solution)/shard_map/ppermute | solution.py:265
  27.9 1.3 collective-permute-start.7
  29.2 2.9 %collective-permute-start.6 = (bf16[2240,128]{1,0:T(8,128)(2,1)S(1)}, bf16[2240,128]{1,0:T(8,128)(2,1)S(1)}, u32[]{:S(2)}, u32[]{:S(2)}) collective-permute-start(bf16[2240,128]{1,0:T(8,128)(2,1)S(1)} %pad_maximum_fusion), channel_id=1, source_target_pairs={{0,1},{1,2},{2,3},{3,0},{4,5},{5,6},{6,7},{7,4},{8,9},{9,10},{10,1... | collective-permute-start | bytes 1720328 | tf_op jit(solution)/shard_map/ppermute | solution.py:265
  32.1 3.1 %collective-permute-start.8 = (bf16[560,640]{1,0:T(8,128)(2,1)S(1)}, bf16[560,640]{1,0:T(8,128)(2,1)S(1)}, u32[]{:S(2)}, u32[]{:S(2)}) collective-permute-start(bf16[560,640]{1,0:T(8,128)(2,1)S(1)} %shard_map.79.w0), channel_id=1, source_target_pairs={{0,16},{16,0},{1,17},{17,1},{2,18},{18,2},{3,19},{19,3},{4,20},{20... | collective-permute-start | bytes 2150408 | tf_op jit(solution)/shard_map/ppermute | solution.py:265
  35.2 2.4 %collective-permute-done.w_prev = bf16[560,640]{1,0:T(8,128)(2,1)S(1)} collective-permute-done((bf16[560,640]{1,0:T(8,128)(2,1)S(1)}, bf16[560,640]{1,0:T(8,128)(2,1)S(1)}, u32[]{:S(2)}, u32[]{:S(2)}) %collective-permute-start) | collective-permute-done | bytes 716832 | tf_op jit(solution)/shard_map/ppermute | solution.py:265
  37.8 2.7 %collective-permute-start.3 = (bf16[272,640]{1,0:T(8,128)(2,1)S(1)}, bf16[272,640]{1,0:T(8,128)(2,1)S(1)}, u32[]{:S(2)}, u32[]{:S(2)}) collective-permute-start(bf16[272,640]{1,0:T(8,128)(2,1)S(1)} %slice.17), channel_id=1, source_target_pairs={{0,12},{4,0},{8,4},{12,8},{1,13},{5,1},{9,5},{13,9},{2,14},{6,2},{... | collective-permute-start | bytes 1044488 | tf_op jit(solution)/shard_map/ppermute | solution.py:265
  40.5 1.6 %collective-permute-done.7.t2_hi.q1 = bf16[2240,128]{1,0:T(8,128)(2,1)S(1)} collective-permute-done((bf16[2240,128]{1,0:T(8,128)(2,1)S(1)}, bf16[2240,128]{1,0:T(8,128)(2,1)S(1)}, u32[]{:S(2)}, u32[]{:S(2)}) %collective-permute-start.7) | collective-permute-done | bytes 573472 | tf_op jit(solution)/shard_map/ppermute | solution.py:265
  42.1 2.5 %collective-permute-start.10 = (bf16[560,640]{1,0:T(8,128)(2,1)S(1)}, bf16[560,640]{1,0:T(8,128)(2,1)S(1)}, u32[]{:S(2)}, u32[]{:S(2)}) collective-permute-start(bf16[560,640]{1,0:T(8,128)(2,1)S(1)} %collective-permute-done.2.w_next), channel_id=1, source_target_pairs={{0,16},{16,0},{1,17},{17,1},{2,18},{18,2},{3,19},{19,3},{4,20},{20... | collective-permute-start | bytes 2150408 | tf_op jit(solution)/shard_map/ppermute | solution.py:265
  44.5 0.8 collective-permute-start.9
  45.3 1.5 %shard_map.80 = (bf16[1152,512]{1,0:T(8,128)(2,1)S(1)}, bf16[1152,512]{1,0:T(8,128)(2,1)S(1)}) custom-call(s32[5]{0:T(128)S(1)} %stack.19.idx, bf16[2240,128]{1,0:T(8,128)(2,1)S(1)} %bitcast.22, bf16[2240,128]{1,0:T(8,128)(2,1)S(1)} %collective-permute-done.4.t1, bf16[2240,128]{1,0:T(8,128)(2,1)S(1)} %collective-permute-done.5.t3, ...), custom_call_target="tpu_custom_call" | custom-call | bytes 10000000 | tf_op jit(solution)/shard_map/pallas_call | solution.py:38
  46.8 3.1 %collective-permute-start.11 = (bf16[288,640]{1,0:T(8,128)(2,1)S(1)}, bf16[288,640]{1,0:T(8,128)(2,1)S(1)}, u32[]{:S(2)}, u32[]{:S(2)}) collective-permute-start(bf16[288,640]{1,0:T(8,128)(2,1)S(1)} %collective-permute-done.1.w_lo), channel_id=1, source_target_pairs={{0,16},{16,0},{1,17},{17,1},{2,18},{18,2},{3,19},{19,3},{4,20},{20... | collective-permute-start | bytes 1105928 | tf_op jit(solution)/shard_map/ppermute | solution.py:265
  49.9 0.5 collective-permute-start.20
  50.4 1.3 collective-permute-done.12.v_hi
  51.7 4.6 %shard_map.81 = (bf16[560,512]{1,0:T(8,128)(2,1)S(1)}, bf16[560,512]{1,0:T(8,128)(2,1)S(1)}, bf16[560,128]{1,0:T(8,128)(2,1)S(1)}) custom-call(s32[5]{0:T(128)S(1)} %stack.19.idx, bf16[560,640]{1,0:T(8,128)(2,1)S(1)} %shard_map.79.w0, bf16[560,640]{1,0:T(8,128)(2,1)S(1)} %collective-permute-done.w_prev, bf16[560,640]{1,0:T(8,128)(2,1)S(1)} %collective-permute-done.2.w_next, ...), custom_call_target="tpu_custom_call" | custom-call | flops 2569011200 | bytes 5000000 | tf_op jit(solution)/shard_map/pallas_call | solution.py:38
  56.3 1.0 collective-permute-start.15
  57.3 1.9 %collective-permute-start.14 = (bf16[560,128]{1,0:T(8,128)(2,1)S(1)}, bf16[560,128]{1,0:T(8,128)(2,1)S(1)}, u32[]{:S(2)}, u32[]{:S(2)}) collective-permute-start(bf16[560,128]{1,0:T(8,128)(2,1)S(1)} %get-tuple-element.44.s0), channel_id=1, source_target_pairs={{0,12},{4,0},{8,4},{12,8},{1,13},{5,1},{9,5},{13,9},{2,14},{6,2},{... | collective-permute-start | bytes 430088 | tf_op jit(solution)/shard_map/ppermute | solution.py:265
  59.2 0.5 collective-permute-start.13
  59.7 0.7 collective-permute-done.16.q2
  60.3 2.5 %collective-permute-done.15.s3 = bf16[560,128]{1,0:T(8,128)(2,1)S(1)} collective-permute-done((bf16[560,128]{1,0:T(8,128)(2,1)S(1)}, bf16[560,128]{1,0:T(8,128)(2,1)S(1)}, u32[]{:S(2)}, u32[]{:S(2)}) %collective-permute-start.15) | collective-permute-done | bytes 143392 | tf_op jit(solution)/shard_map/ppermute | solution.py:265
  62.8 3.4 %collective-permute-done.14.s2 = bf16[560,128]{1,0:T(8,128)(2,1)S(1)} collective-permute-done((bf16[560,128]{1,0:T(8,128)(2,1)S(1)}, bf16[560,128]{1,0:T(8,128)(2,1)S(1)}, u32[]{:S(2)}, u32[]{:S(2)}) %collective-permute-start.14) | collective-permute-done | bytes 143392 | tf_op jit(solution)/shard_map/ppermute | solution.py:265
  66.3 2.0 %shard_map.82 = (bf16[560,128]{1,0:T(8,128)(2,1)S(1)}, bf16[560,128]{1,0:T(8,128)(2,1)S(1)}, bf16[560,128]{1,0:T(8,128)(2,1)S(1)}, bf16[560,128]{1,0:T(8,128)(2,1)S(1)}, bf16[560,128]{1,0:T(8,128)(2,1)S(1)}) custom-call(s32[5]{0:T(128)S(1)} %stack.19.idx, bf16[560,128]{1,0:T(8,128)(2,1)S(1)} %get-tuple-element.44.s0, ...), custom_call_target="tpu_custom_call" | custom-call | flops 220200960 | bytes 4000000 | tf_op jit(solution)/shard_map/pallas_call | solution.py:38
  68.3 1.1 collective-permute-start.19
  69.4 2.2 %collective-permute-start.18 = (bf16[560,128]{1,0:T(8,128)(2,1)S(1)}, bf16[560,128]{1,0:T(8,128)(2,1)S(1)}, u32[]{:S(2)}, u32[]{:S(2)}) collective-permute-start(bf16[560,128]{1,0:T(8,128)(2,1)S(1)} %get-tuple-element.48.s0), channel_id=1, source_target_pairs={{0,12},{4,0},{8,4},{12,8},{1,13},{5,1},{9,5},{13,9},{2,14},{6,2},{... | collective-permute-start | bytes 430088 | tf_op jit(solution)/shard_map/ppermute | solution.py:265
  71.6 0.1 collective-permute-start.17
  71.7 2.2 %collective-permute-done.19.s3 = bf16[560,128]{1,0:T(8,128)(2,1)S(1)} collective-permute-done((bf16[560,128]{1,0:T(8,128)(2,1)S(1)}, bf16[560,128]{1,0:T(8,128)(2,1)S(1)}, u32[]{:S(2)}, u32[]{:S(2)}) %collective-permute-start.19) | collective-permute-done | bytes 143392 | tf_op jit(solution)/shard_map/ppermute | solution.py:265
  74.0 4.0 %collective-permute-done.18.s2 = bf16[560,128]{1,0:T(8,128)(2,1)S(1)} collective-permute-done((bf16[560,128]{1,0:T(8,128)(2,1)S(1)}, bf16[560,128]{1,0:T(8,128)(2,1)S(1)}, u32[]{:S(2)}, u32[]{:S(2)}) %collective-permute-start.18) | collective-permute-done | bytes 143392 | tf_op jit(solution)/shard_map/ppermute | solution.py:265
  78.0 0.6 collective-permute-done.17.s1
  78.6 0.9 shard_map.83.d
  79.5 1.3 collective-permute-start.21
  80.8 1.1 shard_map.84.first
  81.9 0.5 collective-permute-done.21.d
  82.4 2.9 %shard_map.85 = bf16[16,64,640]{2,1,0:T(8,128)(2,1)} custom-call(s32[5]{0:T(128)S(1)} %stack.19.idx, f32[1152,560]{1,0:T(8,128)S(1)} %shard_map.84.first, bf16[1152,512]{1,0:T(8,128)(2,1)S(1)} %collective-permute-done.20.t, bf16[560,512]{1,0:T(8,128)(2,1)S(1)} %collective-permute-done.21.d), custom_call_target="tpu_custom_call" | custom-call | flops 660602880 | bytes 5000000 | tf_op jit(solution)/shard_map/pallas_call | solution.py:38
  85.3 6.9 %all-to-all-start.1 = ((bf16[16,64,640]{2,1,0:T(8,128)(2,1)}), bf16[16,64,640]{2,1,0:T(8,128)(2,1)S(1)}, u32[]{:S(2)}, u32[]{:S(2)}) async-start(bf16[16,64,640]{2,1,0:T(8,128)(2,1)} %shard_map.85), calls=%async_computation.1 | async-start | bytes 2621440 | tf_op jit(solution)/shard_map/all_to_all | solution.py:375
  92.3 0.5 collective-permute-start.22
  92.8 2.3 %collective-permute-start.23 = (bf16[560,128]{1,0:T(8,128)(2,1)S(1)}, bf16[560,128]{1,0:T(8,128)(2,1)S(1)}, u32[]{:S(2)}, u32[]{:S(2)}) collective-permute-start(bf16[560,128]{1,0:T(8,128)(2,1)S(1)} %get-tuple-element.54), channel_id=1, source_target_pairs={{0,2},{1,3},{2,0},{3,1},{4,6},{5,7},{6,4},{7,5},{8,10},{9,11},{10,... | collective-permute-start | bytes 430088 | tf_op jit(solution)/shard_map/ppermute | solution.py:265
  95.1 1.0 collective-permute-start.24
  96.1 2.1 %collective-permute-done.22.g1 = bf16[560,128]{1,0:T(8,128)(2,1)S(1)} collective-permute-done((bf16[560,128]{1,0:T(8,128)(2,1)S(1)}, bf16[560,128]{1,0:T(8,128)(2,1)S(1)}, u32[]{:S(2)}, u32[]{:S(2)}) %collective-permute-start.22) | collective-permute-done | bytes 143392 | tf_op jit(solution)/shard_map/ppermute | solution.py:265
  98.2 3.2 %collective-permute-done.23.g2 = bf16[560,128]{1,0:T(8,128)(2,1)S(1)} collective-permute-done((bf16[560,128]{1,0:T(8,128)(2,1)S(1)}, bf16[560,128]{1,0:T(8,128)(2,1)S(1)}, u32[]{:S(2)}, u32[]{:S(2)}) %collective-permute-start.23) | collective-permute-done | bytes 143392 | tf_op jit(solution)/shard_map/ppermute | solution.py:265
  101.4 0.1 collective-permute-done.24.g3
  101.5 1.4 %shard_map.86 = bf16[2240,128]{1,0:T(8,128)(2,1)} custom-call(s32[5]{0:T(128)S(1)} %stack.19.idx, bf16[560,128]{1,0:T(8,128)(2,1)S(1)} %get-tuple-element.52.g0, bf16[560,128]{1,0:T(8,128)(2,1)S(1)} %collective-permute-done.22.g1, bf16[560,128]{1,0:T(8,128)(2,1)S(1)} %collective-permute-done.23.g2, bf16[560,128]{1,0:T(8,128)(2,1)S(1)} %collective-permute-done.24.g3), custom_call_target="tpu_custom_call" | custom-call | tf_op jit(solution)/shard_map/pallas_call | solution.py:38
  102.9 9.5 %all-to-all-done.1.g = bf16[16,64,640]{2,1,0:T(8,128)(2,1)S(1)} async-done(((bf16[16,64,640]{2,1,0:T(8,128)(2,1)}), bf16[16,64,640]{2,1,0:T(8,128)(2,1)S(1)}, u32[]{:S(2)}, u32[]{:S(2)}) %all-to-all-start.1) | async-done | bytes 1310752 | tf_op jit(solution)/shard_map/all_to_all | solution.py:375
  112.4 0.2 shard_map.87
  112.6 0.3 collective-permute-start.28
  112.9 2.3 %collective-permute-start.27 = (bf16[64,640]{1,0:T(8,128)(2,1)S(1)}, bf16[64,640]{1,0:T(8,128)(2,1)S(1)}, u32[]{:S(2)}, u32[]{:S(2)}) collective-permute-start(bf16[64,640]{1,0:T(8,128)(2,1)S(1)} %shard_map.87), channel_id=1, source_target_pairs={{0,64},{1,65},{2,66},{3,67},{32,97},{33,98},{34,99},{35,96},{64,2}... | collective-permute-start | bytes 245768 | tf_op jit(solution)/shard_map/ppermute | solution.py:386
  115.2 1.1 collective-permute-start.26
  116.2 0.7 collective-permute-start.25
  116.9 3.7 %collective-permute-start.32 = (bf16[64,640]{1,0:T(8,128)(2,1)S(1)}, bf16[64,640]{1,0:T(8,128)(2,1)S(1)}, u32[]{:S(2)}, u32[]{:S(2)}) collective-permute-start(bf16[64,640]{1,0:T(8,128)(2,1)S(1)} %collective-permute-done.28.r3), channel_id=1, source_target_pairs={{0,16},{16,0},{1,17},{17,1},{2,18},{18,2},{3,19},{19,3},{4,20},{20... | collective-permute-start | bytes 245768 | tf_op jit(solution)/shard_map/ppermute | solution.py:265
  120.7 3.7 %collective-permute-start.31 = (bf16[64,640]{1,0:T(8,128)(2,1)S(1)}, bf16[64,640]{1,0:T(8,128)(2,1)S(1)}, u32[]{:S(2)}, u32[]{:S(2)}) collective-permute-start(bf16[64,640]{1,0:T(8,128)(2,1)S(1)} %collective-permute-done.27.r2), channel_id=1, source_target_pairs={{0,16},{16,0},{1,17},{17,1},{2,18},{18,2},{3,19},{19,3},{4,20},{20... | collective-permute-start | bytes 245768 | tf_op jit(solution)/shard_map/ppermute | solution.py:265
  124.4 2.2 %collective-permute-start.30 = (bf16[64,640]{1,0:T(8,128)(2,1)S(1)}, bf16[64,640]{1,0:T(8,128)(2,1)S(1)}, u32[]{:S(2)}, u32[]{:S(2)}) collective-permute-start(bf16[64,640]{1,0:T(8,128)(2,1)S(1)} %collective-permute-done.26.r1), channel_id=1, source_target_pairs={{0,16},{16,0},{1,17},{17,1},{2,18},{18,2},{3,19},{19,3},{4,20},{20... | collective-permute-start | bytes 245768 | tf_op jit(solution)/shard_map/ppermute | solution.py:265
  126.6 0.9 collective-permute-done.30.o1
  127.5 0.4 collective-permute-done.29.o0
  127.9 2.2 %shard_map.88 = f32[140,2240]{1,0:T(8,128)} custom-call(s32[5]{0:T(128)S(1)} %stack.19.idx, bf16[64,640]{1,0:T(8,128)(2,1)S(1)} %collective-permute-done.25.r0, bf16[64,640]{1,0:T(8,128)(2,1)S(1)} %collective-permute-done.26.r1, bf16[64,640]{1,0:T(8,128)(2,1)S(1)} %collective-permute-done.27.r2, bf16[64,640]{1,0:T(8,128)(2,1)S(1)} %collective-permute-done.28.r3, ...), custom_call_target="tpu_custom_call" | custom-call | tf_op jit(solution)/shard_map/pallas_call | solution.py:38
  (43 shorter events, 0.4 us)
Async XLA Ops:
  0.6 6.7 %copy-start.2 = (bf16[1,128,2240]{1,2,0:T(8,128)(2,1)S(1)}, bf16[1,128,2240]{1,2,0:T(8,128)(2,1)}, u32[]{:S(2)}) copy-start(bf16[1,128,2240]{1,2,0:T(8,128)(2,1)} %param.6) | copy-start | bytes 1720324
  2.9 5.7 %copy-start = (bf16[1,128,2240]{1,2,0:T(8,128)(2,1)S(1)}, bf16[1,128,2240]{1,2,0:T(8,128)(2,1)}, u32[]{:S(2)}) copy-start(bf16[1,128,2240]{1,2,0:T(8,128)(2,1)} %param.7) | copy-start | bytes 1720324
  2.9 5.7 %copy-start.1 = (bf16[1,128,2240]{1,2,0:T(8,128)(2,1)S(1)}, bf16[1,128,2240]{1,2,0:T(8,128)(2,1)}, u32[]{:S(2)}) copy-start(bf16[1,128,2240]{1,2,0:T(8,128)(2,1)} %param.8) | copy-start | bytes 1720324
  2.9 13.5 %all-to-all-start = ((bf16[4,140,560]{2,1,0:T(8,128)(2,1)}), bf16[4,140,560]{2,1,0:T(8,128)(2,1)S(1)}, u32[]{:S(2)}, u32[]{:S(2)}) async-start(bf16[4,140,560]{2,1,0:T(8,128)(2,1)} %shard_map.77), calls=%async_computation | async-start | bytes 1474560 | tf_op jit(solution)/shard_map/all_to_all | solution.py:291
  7.3 20.5 %collective-permute-start.4 = (bf16[2240,128]{1,0:T(8,128)(2,1)S(1)}, bf16[2240,128]{1,0:T(8,128)(2,1)S(1)}, u32[]{:S(2)}, u32[]{:S(2)}) collective-permute-start(bf16[2240,128]{1,0:T(8,128)(2,1)S(1)} %bitcast.20), channel_id=1, source_target_pairs={{0,3},{1,0},{2,1},{3,2},{4,7},{5,4},{6,5},{7,6},{8,11},{9,8},{10,9... | collective-permute-start | bytes 1720328 | tf_op jit(solution)/shard_map/ppermute | solution.py:265
  10.7 0.7 copy-start.3
  11.5 0.7 copy-start.5
  12.2 0.7 copy-start.7
  16.4 11.4 %copy-start.6 = (bf16[2,560,128]{2,1,0:T(8,128)(2,1)S(1)}, bf16[2,560,128]{2,1,0:T(8,128)(2,1)}, u32[]{:S(2)}) copy-start(bf16[2,560,128]{2,1,0:T(8,128)(2,1)} %copy-done.5) | copy-start | bytes 860164
  16.4 12.7 %collective-permute-start.5 = (bf16[2240,128]{1,0:T(8,128)(2,1)S(1)}, bf16[2240,128]{1,0:T(8,128)(2,1)S(1)}, u32[]{:S(2)}, u32[]{:S(2)}) collective-permute-start(bf16[2240,128]{1,0:T(8,128)(2,1)S(1)} %bitcast.21), channel_id=1, source_target_pairs={{0,1},{1,2},{2,3},{3,0},{4,5},{5,6},{6,7},{7,4},{8,9},{9,10},{10,1... | collective-permute-start | bytes 1720328 | tf_op jit(solution)/shard_map/ppermute | solution.py:265
  18.4 10.7 %copy-start.4 = (bf16[2,560,128]{2,1,0:T(8,128)(2,1)S(1)}, bf16[2,560,128]{2,1,0:T(8,128)(2,1)}, u32[]{:S(2)}) copy-start(bf16[2,560,128]{2,1,0:T(8,128)(2,1)} %copy-done.3) | copy-start | bytes 860164
  18.4 19.3 %collective-permute-start.2 = (bf16[560,640]{1,0:T(8,128)(2,1)S(1)}, bf16[560,640]{1,0:T(8,128)(2,1)S(1)}, u32[]{:S(2)}, u32[]{:S(2)}) collective-permute-start(bf16[560,640]{1,0:T(8,128)(2,1)S(1)} %shard_map.79.w0), channel_id=1, source_target_pairs={{0,12},{4,0},{8,4},{12,8},{1,13},{5,1},{9,5},{13,9},{2,14},{6,2},{... | collective-permute-start | bytes 2150408 | tf_op jit(solution)/shard_map/ppermute | solution.py:265
  21.3 16.3 %collective-permute-start = (bf16[560,640]{1,0:T(8,128)(2,1)S(1)}, bf16[560,640]{1,0:T(8,128)(2,1)S(1)}, u32[]{:S(2)}, u32[]{:S(2)}) collective-permute-start(bf16[560,640]{1,0:T(8,128)(2,1)S(1)} %shard_map.79.w0), channel_id=1, source_target_pairs={{0,4},{4,8},{8,12},{12,0},{1,5},{5,9},{9,13},{13,1},{2,6},{6,10},{... | collective-permute-start | bytes 2150408 | tf_op jit(solution)/shard_map/ppermute | solution.py:265
  27.9 14.2 %collective-permute-start.7 = (bf16[2240,128]{1,0:T(8,128)(2,1)S(1)}, bf16[2240,128]{1,0:T(8,128)(2,1)S(1)}, u32[]{:S(2)}, u32[]{:S(2)}) collective-permute-start(bf16[2240,128]{1,0:T(8,128)(2,1)S(1)} %pad_maximum_fusion.1), channel_id=1, source_target_pairs={{0,3},{1,0},{2,1},{3,2},{4,7},{5,4},{6,5},{7,6},{8,11},{9,8},{10,9... | collective-permute-start | bytes 1720328 | tf_op jit(solution)/shard_map/ppermute | solution.py:265
  29.2 15.3 %collective-permute-start.6 = (bf16[2240,128]{1,0:T(8,128)(2,1)S(1)}, bf16[2240,128]{1,0:T(8,128)(2,1)S(1)}, u32[]{:S(2)}, u32[]{:S(2)}) collective-permute-start(bf16[2240,128]{1,0:T(8,128)(2,1)S(1)} %pad_maximum_fusion), channel_id=1, source_target_pairs={{0,1},{1,2},{2,3},{3,0},{4,5},{5,6},{6,7},{7,4},{8,9},{9,10},{10,1... | collective-permute-start | bytes 1720328 | tf_op jit(solution)/shard_map/ppermute | solution.py:265
  32.1 17.8 %collective-permute-start.8 = (bf16[560,640]{1,0:T(8,128)(2,1)S(1)}, bf16[560,640]{1,0:T(8,128)(2,1)S(1)}, u32[]{:S(2)}, u32[]{:S(2)}) collective-permute-start(bf16[560,640]{1,0:T(8,128)(2,1)S(1)} %shard_map.79.w0), channel_id=1, source_target_pairs={{0,16},{16,0},{1,17},{17,1},{2,18},{18,2},{3,19},{19,3},{4,20},{20... | collective-permute-start | bytes 2150408 | tf_op jit(solution)/shard_map/ppermute | solution.py:265
  37.6 9.2 %collective-permute-start.1 = (bf16[288,640]{1,0:T(8,128)(2,1)S(1)}, bf16[288,640]{1,0:T(8,128)(2,1)S(1)}, u32[]{:S(2)}, u32[]{:S(2)}) collective-permute-start(bf16[288,640]{1,0:T(8,128)(2,1)S(1)} %slice.16), channel_id=1, source_target_pairs={{0,4},{4,8},{8,12},{12,0},{1,5},{5,9},{9,13},{13,1},{2,6},{6,10},{... | collective-permute-start | bytes 1105928 | tf_op jit(solution)/shard_map/ppermute | solution.py:265
  37.8 12.7 %copy-start.8 = (bf16[2,560,128]{2,1,0:T(8,128)(2,1)S(1)}, bf16[2,560,128]{2,1,0:T(8,128)(2,1)}, u32[]{:S(2)}) copy-start(bf16[2,560,128]{2,1,0:T(8,128)(2,1)} %copy-done.7) | copy-start | bytes 860164
  37.8 9.0 %collective-permute-start.3 = (bf16[272,640]{1,0:T(8,128)(2,1)S(1)}, bf16[272,640]{1,0:T(8,128)(2,1)S(1)}, u32[]{:S(2)}, u32[]{:S(2)}) collective-permute-start(bf16[272,640]{1,0:T(8,128)(2,1)S(1)} %slice.17), channel_id=1, source_target_pairs={{0,12},{4,0},{8,4},{12,8},{1,13},{5,1},{9,5},{13,9},{2,14},{6,2},{... | collective-permute-start | bytes 1044488 | tf_op jit(solution)/shard_map/ppermute | solution.py:265
  42.1 8.3 %collective-permute-start.10 = (bf16[560,640]{1,0:T(8,128)(2,1)S(1)}, bf16[560,640]{1,0:T(8,128)(2,1)S(1)}, u32[]{:S(2)}, u32[]{:S(2)}) collective-permute-start(bf16[560,640]{1,0:T(8,128)(2,1)S(1)} %collective-permute-done.2.w_next), channel_id=1, source_target_pairs={{0,16},{16,0},{1,17},{17,1},{2,18},{18,2},{3,19},{19,3},{4,20},{20... | collective-permute-start | bytes 2150408 | tf_op jit(solution)/shard_map/ppermute | solution.py:265
  44.5 5.9 %collective-permute-start.9 = (bf16[560,640]{1,0:T(8,128)(2,1)S(1)}, bf16[560,640]{1,0:T(8,128)(2,1)S(1)}, u32[]{:S(2)}, u32[]{:S(2)}) collective-permute-start(bf16[560,640]{1,0:T(8,128)(2,1)S(1)} %collective-permute-done.w_prev), channel_id=1, source_target_pairs={{0,16},{16,0},{1,17},{17,1},{2,18},{18,2},{3,19},{19,3},{4,20},{20... | collective-permute-start | bytes 2150408 | tf_op jit(solution)/shard_map/ppermute | solution.py:265
  46.8 4.9 %collective-permute-start.11 = (bf16[288,640]{1,0:T(8,128)(2,1)S(1)}, bf16[288,640]{1,0:T(8,128)(2,1)S(1)}, u32[]{:S(2)}, u32[]{:S(2)}) collective-permute-start(bf16[288,640]{1,0:T(8,128)(2,1)S(1)} %collective-permute-done.1.w_lo), channel_id=1, source_target_pairs={{0,16},{16,0},{1,17},{17,1},{2,18},{18,2},{3,19},{19,3},{4,20},{20... | collective-permute-start | bytes 1105928 | tf_op jit(solution)/shard_map/ppermute | solution.py:265
  49.9 1.8 %collective-permute-start.12 = (bf16[272,640]{1,0:T(8,128)(2,1)S(1)}, bf16[272,640]{1,0:T(8,128)(2,1)S(1)}, u32[]{:S(2)}, u32[]{:S(2)}) collective-permute-start(bf16[272,640]{1,0:T(8,128)(2,1)S(1)} %collective-permute-done.3.w_hi), channel_id=1, source_target_pairs={{0,16},{16,0},{1,17},{17,1},{2,18},{18,2},{3,19},{19,3},{4,20},{20... | collective-permute-start | bytes 1044488 | tf_op jit(solution)/shard_map/ppermute | solution.py:265
  49.9 32.0 %collective-permute-start.20 = (bf16[1152,512]{1,0:T(8,128)(2,1)S(1)}, bf16[1152,512]{1,0:T(8,128)(2,1)S(1)}, u32[]{:S(2)}, u32[]{:S(2)}) collective-permute-start(bf16[1152,512]{1,0:T(8,128)(2,1)S(1)} %get-tuple-element.51), channel_id=1, source_target_pairs={{0,16},{16,0},{1,17},{17,1},{2,18},{18,2},{3,19},{19,3},{4,20},{20... | collective-permute-start | bytes 3538952 | tf_op jit(solution)/shard_map/ppermute | solution.py:265
  50.4 9.9 %collective-permute-start.16 = (bf16[2,560,128]{2,1,0:T(8,128)(2,1)S(1)}, bf16[2,560,128]{2,1,0:T(8,128)(2,1)S(1)}, u32[]{:S(2)}, u32[]{:S(2)}) collective-permute-start(bf16[2,560,128]{2,1,0:T(8,128)(2,1)S(1)} %copy-done.8), channel_id=1, source_target_pairs={{0,2},{1,3},{2,0},{3,1},{4,6},{5,7},{6,4},{7,5},{8,10},{9,11},{10,... | collective-permute-start | bytes 860168 | tf_op jit(solution)/shard_map/ppermute | solution.py:265
  56.3 6.6 %collective-permute-start.15 = (bf16[560,128]{1,0:T(8,128)(2,1)S(1)}, bf16[560,128]{1,0:T(8,128)(2,1)S(1)}, u32[]{:S(2)}, u32[]{:S(2)}) collective-permute-start(bf16[560,128]{1,0:T(8,128)(2,1)S(1)} %get-tuple-element.44.s0), channel_id=1, source_target_pairs={{0,8},{4,12},{8,0},{12,4},{1,9},{5,13},{9,1},{13,5},{2,10},{6,14},... | collective-permute-start | bytes 430088 | tf_op jit(solution)/shard_map/ppermute | solution.py:265
  57.3 9.0 %collective-permute-start.14 = (bf16[560,128]{1,0:T(8,128)(2,1)S(1)}, bf16[560,128]{1,0:T(8,128)(2,1)S(1)}, u32[]{:S(2)}, u32[]{:S(2)}) collective-permute-start(bf16[560,128]{1,0:T(8,128)(2,1)S(1)} %get-tuple-element.44.s0), channel_id=1, source_target_pairs={{0,12},{4,0},{8,4},{12,8},{1,13},{5,1},{9,5},{13,9},{2,14},{6,2},{... | collective-permute-start | bytes 430088 | tf_op jit(solution)/shard_map/ppermute | solution.py:265
  59.2 7.1 %collective-permute-start.13 = (bf16[560,128]{1,0:T(8,128)(2,1)S(1)}, bf16[560,128]{1,0:T(8,128)(2,1)S(1)}, u32[]{:S(2)}, u32[]{:S(2)}) collective-permute-start(bf16[560,128]{1,0:T(8,128)(2,1)S(1)} %get-tuple-element.44.s0), channel_id=1, source_target_pairs={{0,4},{4,8},{8,12},{12,0},{1,5},{5,9},{9,13},{13,1},{2,6},{6,10},{... | collective-permute-start | bytes 430088 | tf_op jit(solution)/shard_map/ppermute | solution.py:265
  68.3 5.7 %collective-permute-start.19 = (bf16[560,128]{1,0:T(8,128)(2,1)S(1)}, bf16[560,128]{1,0:T(8,128)(2,1)S(1)}, u32[]{:S(2)}, u32[]{:S(2)}) collective-permute-start(bf16[560,128]{1,0:T(8,128)(2,1)S(1)} %get-tuple-element.48.s0), channel_id=1, source_target_pairs={{0,8},{4,12},{8,0},{12,4},{1,9},{5,13},{9,1},{13,5},{2,10},{6,14},... | collective-permute-start | bytes 430088 | tf_op jit(solution)/shard_map/ppermute | solution.py:265
  69.4 8.6 %collective-permute-start.18 = (bf16[560,128]{1,0:T(8,128)(2,1)S(1)}, bf16[560,128]{1,0:T(8,128)(2,1)S(1)}, u32[]{:S(2)}, u32[]{:S(2)}) collective-permute-start(bf16[560,128]{1,0:T(8,128)(2,1)S(1)} %get-tuple-element.48.s0), channel_id=1, source_target_pairs={{0,12},{4,0},{8,4},{12,8},{1,13},{5,1},{9,5},{13,9},{2,14},{6,2},{... | collective-permute-start | bytes 430088 | tf_op jit(solution)/shard_map/ppermute | solution.py:265
  71.6 7.0 %collective-permute-start.17 = (bf16[560,128]{1,0:T(8,128)(2,1)S(1)}, bf16[560,128]{1,0:T(8,128)(2,1)S(1)}, u32[]{:S(2)}, u32[]{:S(2)}) collective-permute-start(bf16[560,128]{1,0:T(8,128)(2,1)S(1)} %get-tuple-element.48.s0), channel_id=1, source_target_pairs={{0,4},{4,8},{8,12},{12,0},{1,5},{5,9},{9,13},{13,1},{2,6},{6,10},{... | collective-permute-start | bytes 430088 | tf_op jit(solution)/shard_map/ppermute | solution.py:265
  79.5 2.9 %collective-permute-start.21 = (bf16[560,512]{1,0:T(8,128)(2,1)S(1)}, bf16[560,512]{1,0:T(8,128)(2,1)S(1)}, u32[]{:S(2)}, u32[]{:S(2)}) collective-permute-start(bf16[560,512]{1,0:T(8,128)(2,1)S(1)} %shard_map.83.d), channel_id=1, source_target_pairs={{0,16},{16,0},{1,17},{17,1},{2,18},{18,2},{3,19},{19,3},{4,20},{20... | collective-permute-start | bytes 1720328 | tf_op jit(solution)/shard_map/ppermute | solution.py:265
  85.3 27.1 %all-to-all-start.1 = ((bf16[16,64,640]{2,1,0:T(8,128)(2,1)}), bf16[16,64,640]{2,1,0:T(8,128)(2,1)S(1)}, u32[]{:S(2)}, u32[]{:S(2)}) async-start(bf16[16,64,640]{2,1,0:T(8,128)(2,1)} %shard_map.85), calls=%async_computation.1 | async-start | bytes 2621440 | tf_op jit(solution)/shard_map/all_to_all | solution.py:375
  92.3 5.9 %collective-permute-start.22 = (bf16[560,128]{1,0:T(8,128)(2,1)S(1)}, bf16[560,128]{1,0:T(8,128)(2,1)S(1)}, u32[]{:S(2)}, u32[]{:S(2)}) collective-permute-start(bf16[560,128]{1,0:T(8,128)(2,1)S(1)} %get-tuple-element.53), channel_id=1, source_target_pairs={{0,3},{1,0},{2,1},{3,2},{4,7},{5,4},{6,5},{7,6},{8,11},{9,8},{10,9... | collective-permute-start | bytes 430088 | tf_op jit(solution)/shard_map/ppermute | solution.py:265
  92.8 8.6 %collective-permute-start.23 = (bf16[560,128]{1,0:T(8,128)(2,1)S(1)}, bf16[560,128]{1,0:T(8,128)(2,1)S(1)}, u32[]{:S(2)}, u32[]{:S(2)}) collective-permute-start(bf16[560,128]{1,0:T(8,128)(2,1)S(1)} %get-tuple-element.54), channel_id=1, source_target_pairs={{0,2},{1,3},{2,0},{3,1},{4,6},{5,7},{6,4},{7,5},{8,10},{9,11},{10,... | collective-permute-start | bytes 430088 | tf_op jit(solution)/shard_map/ppermute | solution.py:265
  95.1 6.4 %collective-permute-start.24 = (bf16[560,128]{1,0:T(8,128)(2,1)S(1)}, bf16[560,128]{1,0:T(8,128)(2,1)S(1)}, u32[]{:S(2)}, u32[]{:S(2)}) collective-permute-start(bf16[560,128]{1,0:T(8,128)(2,1)S(1)} %get-tuple-element.55), channel_id=1, source_target_pairs={{0,1},{1,2},{2,3},{3,0},{4,5},{5,6},{6,7},{7,4},{8,9},{9,10},{10,1... | collective-permute-start | bytes 430088 | tf_op jit(solution)/shard_map/ppermute | solution.py:265
  112.6 4.3 %collective-permute-start.28 = (bf16[64,640]{1,0:T(8,128)(2,1)S(1)}, bf16[64,640]{1,0:T(8,128)(2,1)S(1)}, u32[]{:S(2)}, u32[]{:S(2)}) collective-permute-start(bf16[64,640]{1,0:T(8,128)(2,1)S(1)} %shard_map.87), channel_id=1, source_target_pairs={{0,96},{1,97},{2,98},{3,99},{32,1},{33,2},{34,3},{35,0},{64,34},{6... | collective-permute-start | bytes 245768 | tf_op jit(solution)/shard_map/ppermute | solution.py:386
  112.9 7.8 %collective-permute-start.27 = (bf16[64,640]{1,0:T(8,128)(2,1)S(1)}, bf16[64,640]{1,0:T(8,128)(2,1)S(1)}, u32[]{:S(2)}, u32[]{:S(2)}) collective-permute-start(bf16[64,640]{1,0:T(8,128)(2,1)S(1)} %shard_map.87), channel_id=1, source_target_pairs={{0,64},{1,65},{2,66},{3,67},{32,97},{33,98},{34,99},{35,96},{64,2}... | collective-permute-start | bytes 245768 | tf_op jit(solution)/shard_map/ppermute | solution.py:386
  115.2 9.2 %collective-permute-start.26 = (bf16[64,640]{1,0:T(8,128)(2,1)S(1)}, bf16[64,640]{1,0:T(8,128)(2,1)S(1)}, u32[]{:S(2)}, u32[]{:S(2)}) collective-permute-start(bf16[64,640]{1,0:T(8,128)(2,1)S(1)} %shard_map.87), channel_id=1, source_target_pairs={{0,32},{1,33},{2,34},{3,35},{32,65},{33,66},{34,67},{35,64},{64,98... | collective-permute-start | bytes 245768 | tf_op jit(solution)/shard_map/ppermute | solution.py:386
  116.2 10.4 %collective-permute-start.25 = (bf16[64,640]{1,0:T(8,128)(2,1)S(1)}, bf16[64,640]{1,0:T(8,128)(2,1)S(1)}, u32[]{:S(2)}, u32[]{:S(2)}) collective-permute-start(bf16[64,640]{1,0:T(8,128)(2,1)S(1)} %shard_map.87), channel_id=1, source_target_pairs={{0,0},{1,1},{2,2},{3,3},{32,33},{33,34},{34,35},{35,32},{64,66},{6... | collective-permute-start | bytes 245768 | tf_op jit(solution)/shard_map/ppermute | solution.py:386
  116.9 9.7 %collective-permute-start.32 = (bf16[64,640]{1,0:T(8,128)(2,1)S(1)}, bf16[64,640]{1,0:T(8,128)(2,1)S(1)}, u32[]{:S(2)}, u32[]{:S(2)}) collective-permute-start(bf16[64,640]{1,0:T(8,128)(2,1)S(1)} %collective-permute-done.28.r3), channel_id=1, source_target_pairs={{0,16},{16,0},{1,17},{17,1},{2,18},{18,2},{3,19},{19,3},{4,20},{20... | collective-permute-start | bytes 245768 | tf_op jit(solution)/shard_map/ppermute | solution.py:265
  120.7 5.9 %collective-permute-start.31 = (bf16[64,640]{1,0:T(8,128)(2,1)S(1)}, bf16[64,640]{1,0:T(8,128)(2,1)S(1)}, u32[]{:S(2)}, u32[]{:S(2)}) collective-permute-start(bf16[64,640]{1,0:T(8,128)(2,1)S(1)} %collective-permute-done.27.r2), channel_id=1, source_target_pairs={{0,16},{16,0},{1,17},{17,1},{2,18},{18,2},{3,19},{19,3},{4,20},{20... | collective-permute-start | bytes 245768 | tf_op jit(solution)/shard_map/ppermute | solution.py:265
  124.4 3.1 %collective-permute-start.30 = (bf16[64,640]{1,0:T(8,128)(2,1)S(1)}, bf16[64,640]{1,0:T(8,128)(2,1)S(1)}, u32[]{:S(2)}, u32[]{:S(2)}) collective-permute-start(bf16[64,640]{1,0:T(8,128)(2,1)S(1)} %collective-permute-done.26.r1), channel_id=1, source_target_pairs={{0,16},{16,0},{1,17},{17,1},{2,18},{18,2},{3,19},{19,3},{4,20},{20... | collective-permute-start | bytes 245768 | tf_op jit(solution)/shard_map/ppermute | solution.py:265
  126.6 1.3 collective-permute-start.29
